TPU v7x, 128 devices: a whole 4x4x4 slice. The times are simulated.
128 devices in a mesh: inline: 8 (over z_hi, x), xline: 16 (over y, z_lo, core).
Axes of the slice: x: 4, y: 4, z: 4 (z_hi: 2, z_lo: 2; z = z_hi * 2 + z_lo), core: 2. Of those that a mesh axis runs over, the one named last changes fastest.
Arguments:
- base_volume: float32 [128, 256, 256], P('inline', 'xline'), may hold values from -6 to 6
- vintage_traces: float32 [131072, 256], P(('inline', 'xline')), may hold values from -6 to 6
- dest_device: int32 [131072, 1], P(('inline', 'xline')), may hold values from 0 to 127; in each aligned block of 1024 rows (0 to 1023, 1024 to 2047, ...) at most 16 rows name the same one
- dest_slot: int32 [131072], P(('inline', 'xline')), may hold values from 0 to 255
- vintage_id: int32 [131072], P(('inline', 'xline')), may hold values from 0 to 3
- vintage_gains: float32 [4], replicated, may hold values from 0.5 to 2
- dictionary: bfloat16 [512, 512], replicated, may hold values from -0.09375 to 0.09375
Outputs:
- codes: float32 [32, 64, 64, 512], P('inline', 'xline')
- residual: float32 [128, 256, 256], P('inline', 'xline')
Inputs may be any that keep to these rules, and one draw needn't show every extreme that they name: `dest_device`: among the traces of one device, no tile is named more than 16 times, a bound that some block reaches.
All inputs are finite; a program needn't handle non-finite values.
Results may differ from a plain program's by a relative error of at most 0.0022.
Values may be sent and summed in bfloat16 or wider, within the bound.
No kernel may reach another device: no remote copies, remote signals or barrier semaphores. Data moves between devices by JAX's collectives and lax.ppermute only.
A program may use at most 64 MiB of HBM per device.

v0:
```python
import jax
import jax.numpy as jnp
from jax import lax
from jax.sharding import PartitionSpec as P

step_size = 0.25
threshold = 0.02


def passed_along(block, axis, distance):
    devices = range(lax.axis_size(axis))
    route = [(i - distance, i) for i in devices if i - distance in devices]
    return lax.ppermute(block, axis, route)


def shrink_codes(values):
    return values - jnp.clip(values, -threshold, threshold)


def extend_field(field_half):
    beyond_cols = passed_along(field_half[:, :4], "xline", -1)
    widened = jnp.concatenate([field_half, beyond_cols], axis=1)
    beyond_rows = passed_along(widened[:4], "inline", -1)
    return jnp.concatenate([widened, beyond_rows], axis=0)


def correlate(field_half, dict_blocks):
    tile_side, time_len = (field_half.shape[0], field_half.shape[2])
    patch_i, patch_k = (tile_side // 4, time_len // 4)
    extended = jnp.pad(extend_field(field_half), ((0, 0), (0, 0), (0, 4)))
    extended = extended.reshape(patch_i + 1, 4, patch_i + 1, 4, patch_k + 1, 4)
    running = None
    for shift_a in (0, 1):
        for shift_b in (0, 1):
            for shift_c in (0, 1):
                block_piece = extended[
                    shift_a : shift_a + patch_i,
                    :,
                    shift_b : shift_b + patch_i,
                    :,
                    shift_c : shift_c + patch_k,
                    :,
                ]
                partial_sum = jnp.einsum(
                    "iajbkc,abcn->ijkn",
                    block_piece,
                    dict_blocks[shift_a, :, shift_b, :, shift_c, :, :],
                    preferred_element_type=jnp.float32,
                )
                running = partial_sum if running is None else running + partial_sum
    return running


def reconstruct(codes_half, dictionary, time_len):
    patch_i, patch_j, patch_k, atom_count = codes_half.shape
    contrib = jnp.einsum(
        "ijkn,en->ijke", codes_half, dictionary, preferred_element_type=jnp.float32
    )
    contrib = contrib.reshape(patch_i, patch_j, patch_k, 2, 4, 2, 4, 2, 4)
    running = None
    for shift_a in (0, 1):
        for shift_b in (0, 1):
            for shift_c in (0, 1):
                block_piece = contrib[:, :, :, shift_a, :, shift_b, :, shift_c, :].transpose(
                    0, 3, 1, 4, 2, 5
                )
                moved = jnp.pad(
                    block_piece,
                    (
                        (shift_a, 1 - shift_a),
                        (0, 0),
                        (shift_b, 1 - shift_b),
                        (0, 0),
                        (shift_c, 1 - shift_c),
                        (0, 0),
                    ),
                )
                running = moved if running is None else running + moved
    extended = running.reshape((patch_i + 1) * 4, (patch_j + 1) * 4, (patch_k + 1) * 4)[
        :, :, :time_len
    ]
    tile_side = patch_i * 4
    from_rows = passed_along(extended[tile_side:].astype(jnp.bfloat16), "inline", 1).astype(
        jnp.float32
    )
    upper_part = extended[:tile_side].at[:4].add(from_rows)
    from_cols = passed_along(upper_part[:, tile_side:].astype(jnp.bfloat16), "xline", 1).astype(
        jnp.float32
    )
    return upper_part[:, :tile_side].at[:, :4].add(from_cols)


def body(
    base_volume, vintage_traces, dest_device, dest_slot, vintage_id, vintage_gains, dictionary
):
    tile_side, time_len = (base_volume.shape[0], base_volume.shape[2])
    inline_count = lax.axis_size("inline")
    xline_count = lax.axis_size("xline")
    device_count = inline_count * xline_count
    trace_count = vintage_traces.shape[0]
    capacity = 2 * trace_count // device_count
    survey_table = (
        vintage_id[:, None] == jnp.arange(vintage_gains.shape[0], dtype=jnp.int32)[None, :]
    )
    trace_gain = jnp.sum(jnp.where(survey_table, vintage_gains[None, :], 0.0), axis=1)
    weighted = vintage_traces * trace_gain[:, None]
    target = dest_device[:, 0]
    onehot = (target[:, None] == jnp.arange(device_count, dtype=jnp.int32)[None, :]).astype(
        jnp.int32
    )
    rank_in = jnp.sum(jnp.cumsum(onehot, axis=0) * onehot, axis=1) - 1
    place_at = target * capacity + rank_in
    send_traces = (
        jnp.zeros((device_count * capacity, time_len), jnp.float32).at[place_at].set(weighted)
    )
    send_slots = jnp.full((device_count * capacity,), -1, jnp.int32).at[place_at].set(dest_slot)
    got_traces, got_slots = (
        lax.all_to_all(send_traces, ("inline", "xline"), split_axis=0, concat_axis=0, tiled=True),
        lax.all_to_all(send_slots, ("inline", "xline"), split_axis=0, concat_axis=0, tiled=True),
    )
    bin_count = tile_side * tile_side
    safe_slots = jnp.where(got_slots < 0, bin_count, got_slots)
    stack = (
        jnp.zeros((bin_count, time_len), jnp.float32).at[safe_slots].add(got_traces, mode="drop")
    )
    fold = (
        jnp.zeros((bin_count,), jnp.float32)
        .at[safe_slots]
        .add(jnp.ones(safe_slots.shape, jnp.float32), mode="drop")
    )
    merged = (base_volume.reshape(bin_count, time_len) + stack) / (1.0 + fold)[:, None]
    merged = merged.reshape(tile_side, tile_side, time_len)
    dict_blocks = dictionary.reshape(2, 4, 2, 4, 2, 4, dictionary.shape[1])
    first = shrink_codes(step_size * correlate(merged.astype(jnp.bfloat16), dict_blocks))
    recon = reconstruct(first.astype(jnp.bfloat16), dictionary, time_len)
    residual = merged - recon
    codes = shrink_codes(first + step_size * correlate(residual.astype(jnp.bfloat16), dict_blocks))
    return (codes, residual)


def solution(mesh):
    in_specs = (
        P("inline", "xline", None),
        P(("inline", "xline"), None),
        P(("inline", "xline"), None),
        P(("inline", "xline")),
        P(("inline", "xline")),
        P(),
        P(),
    )
    out_specs = (P("inline", "xline", None, None), P("inline", "xline", None))
    return jax.shard_map(body, mesh=mesh, in_specs=in_specs, out_specs=out_specs, check_vma=False)
```

profile of v0, /device:TPU:14, one launch (start us, length us, event | category | flops | bytes accessed | tf_op | source)
XLA Modules:
  0.0 194.7 jit_solution(9178286266420384607)
XLA Ops:
  0.7 0.9 copy.89
  2.4 4.5 %scatter_custom_fusion = s32[2048]{0:T(1024)S(1)} fusion(s32[1024]{0:T(1024)S(1)} %bitcast.318, s32[1024]{0:T(1024)} %param.14, s32[]{:T(128)} %constant.76.clone.1), kind=kCustom, calls=%fused_computation.113 | custom fusion | bytes 8704 | tf_op jit(solution)/shard_map/scatter | solution.py:116
  6.8 0.7 all_to_all.16
  7.5 10.4 %all-to-all-start = ((s32[128,16,1]{1,2,0:T(1,128)}), s32[128,16,1]{1,2,0:T(1,128)S(1)}, u32[]{:S(2)}, u32[]{:S(2)}) async-start(s32[128,16,1]{1,2,0:T(1,128)} %bitcast.8), calls=%async_computation | async-start | bytes 131072 | tf_op jit(solution)/shard_map/all_to_all | solution.py:119
  18.0 6.7 %scatter_custom_fusion.1 = f32[2048,256]{1,0:T(8,128)} fusion(s32[1024]{0:T(1024)S(1)} %bitcast.319, f32[1024,256]{1,0:T(8,128)S(1)} %copy-done.4, f32[]{:T(128)} %constant.81.clone.1, f32[1024]{0:T(1024)S(1)} %select_reduce_fusion), kind=kCustom, calls=%fused_computation.57 | custom fusion | flops 262144 | bytes 3149828 | tf_op jit(solution)/shard_map/scatter | solution.py:114
  25.2 9.4 %all-to-all-start.1 = ((f32[128,16,256]{2,1,0:T(8,128)}), f32[128,16,256]{2,1,0:T(8,128)S(1)}, u32[]{:S(2)}, u32[]{:S(2)}) async-start(f32[128,16,256]{2,1,0:T(8,128)} %bitcast.310), calls=%async_computation.1 | async-start | bytes 4194304 | tf_op jit(solution)/shard_map/all_to_all | solution.py:118
  35.1 0.8 reduce.7
  36.0 14.7 %scatter_custom_fusion.3 = f32[256]{0:T(256)S(1)} fusion(s32[2048]{0:T(1024)S(1)} %bitcast.315, f32[2048]{0:T(1024)S(1)} %broadcast.152, f32[]{:T(128)} %constant.82.clone.1), kind=kCustom, calls=%fused_computation.116 | custom fusion | flops 2048 | bytes 1028 | tf_op jit(solution)/shard_map/scatter-add | solution.py:129
  50.7 11.9 %all-to-all-done.1 = f32[128,16,256]{2,1,0:T(8,128)S(1)} async-done(((f32[128,16,256]{2,1,0:T(8,128)}), f32[128,16,256]{2,1,0:T(8,128)S(1)}, u32[]{:S(2)}, u32[]{:S(2)}) %all-to-all-start.1) | async-done | bytes 2097184 | tf_op jit(solution)/shard_map/all_to_all | solution.py:118
  62.6 11.7 %scatter_fusion = f32[256,256]{1,0:T(8,128)S(1)} fusion(f32[256,256]{1,0:T(8,128)S(1)} %bitcast.307, s32[2048]{0:T(1024)S(1)} %bitcast.316, f32[2048,256]{1,0:T(8,128)S(1)} %bitcast.309), kind=kCustom, calls=%fused_computation.2 | custom fusion | flops 524288 | bytes 6299648 | tf_op jit(solution)/shard_map/scatter-add | solution.py:124
  74.4 2.5 %collective-permute-start = (bf16[16,4,256]{2,1,0:T(4,128)(2,1)S(1)}, bf16[16,4,256]{2,1,0:T(4,128)(2,1)S(1)}, u32[]{:S(2)}, u32[]{:S(2)}) collective-permute-start(bf16[16,4,256]{2,1,0:T(4,128)(2,1)S(1)} %slice.235), channel_id=1, source_target_pairs={{1,0},{2,1},{3,2},{4,3},{5,4},{6,5},{7,6},{8,7},{9,8},{10,9},{11,1... | collective-permute-start | bytes 98312 | tf_op jit(solution)/shard_map/ppermute | solution.py:13
  76.9 1.6 collective-permute-done
  78.5 2.9 %collective-permute-start.1 = (bf16[4,20,256]{2,1,0:T(8,128)(2,1)S(1)}, bf16[4,20,256]{2,1,0:T(8,128)(2,1)S(1)}, u32[]{:S(2)}, u32[]{:S(2)}) collective-permute-start(bf16[4,20,256]{2,1,0:T(8,128)(2,1)S(1)} %pad_maximum_fusion.1), channel_id=1, source_target_pairs={{16,0},{32,16},{48,32},{64,48},{80,64},{96,80},{112,96},{17,1},{33... | collective-permute-start | bytes 122888 | tf_op jit(solution)/shard_map/ppermute | solution.py:13
  81.6 6.8 %collective-permute-done.1 = bf16[4,20,256]{2,1,0:T(8,128)(2,1)S(1)} collective-permute-done((bf16[4,20,256]{2,1,0:T(8,128)(2,1)S(1)}, bf16[4,20,256]{2,1,0:T(8,128)(2,1)S(1)}, u32[]{:S(2)}, u32[]{:S(2)}) %collective-permute-start.1) | collective-permute-done | bytes 40992 | tf_op jit(solution)/shard_map/ppermute | solution.py:13
  88.4 6.3 %reshape.150 = bf16[5,4,5,4,65,4]{5,4,3,2,1,0:T(8,128)(2,1)} reshape(bf16[20,20,260]{2,1,0:T(8,128)(2,1)S(1)} %fusion.56) | data formatting | bytes 416000 | tf_op jit(solution)/shard_map/reshape | solution.py:31
  94.8 3.5 %fusion.18 = f32[4,4,64,512,1,1]{3,2,5,1,4,0:T(8,128)S(1)} fusion(bf16[5,4,5,4,65,4]{5,4,3,2,1,0:T(8,128)(2,1)} %reshape.150, bf16[2,4,2,4,2,4,512]{6,5,4,3,2,1,0:T(4,128)(2,1)S(1)} %reshape.151), kind=kOutput, calls=%fused_computation.22 | convolution fusion | flops 67108864 | bytes 6356992 | tf_op jit(solution)/shard_map/iajbkc,abcn->ijkn/dot_general | solution.py:44
  98.3 0.8 copy-done.2
  99.1 1.6 fusion.20
  100.7 1.2 fusion.22
  101.9 1.6 fusion.24
  103.5 1.2 fusion.26
  104.7 1.6 fusion.28
  106.4 1.2 fusion.30
  107.5 14.9 %clamp_subtract_fusion.1 = f32[4,4,64,512]{3,2,1,0:T(8,128)S(1)} fusion(f32[4,4,64,512,1,1]{3,2,5,1,4,0:T(8,128)S(1)} %fusion.18, f32[4,4,64,512,1,1]{3,2,5,1,4,0:T(8,128)S(1)} %fusion.20, f32[4,4,64,512,1,1]{3,2,5,1,4,0:T(8,128)S(1)} %fusion.22, f32[4,4,64,512,1,1]{3,2,5,1,4,0:T(8,128)S(1)} %fusion.24, f32[4,4,64,512,1,1]{3,2,5,1,4,0:T(8,128)S(1)} %fusion.26, ...), kind=kOutput, calls=%fused_computation.37 | convolution fusion | flops 72351744 | bytes 21037056 | tf_op jit(solution)/shard_map/iajbkc,abcn->ijkn/dot_general | solution.py:44
  122.4 1.3 fusion.39
  123.7 1.2 slice_bitcast_fusion.7
  124.9 1.2 pad_add_fusion
  126.1 8.7 %copy.116 = f32[5,4,5,4,65,4]{5,4,3,2,1,0:T(8,128)} copy(f32[5,4,5,4,65,4]{4,5,3,1,2,0:T(4,128)S(1)} %pad_add_fusion) | data formatting | bytes 832000 | tf_op jit(solution)/shard_map/add | solution.py:78
  134.7 8.6 %reshape.153 = f32[20,20,260]{2,1,0:T(8,128)S(1)} reshape(f32[5,4,5,4,65,4]{5,4,3,2,1,0:T(8,128)} %copy.116) | data formatting | bytes 832000 | tf_op jit(solution)/shard_map/reshape | solution.py:79
  143.3 1.9 collective-permute-start.2
  145.3 4.0 %collective-permute-done.2 = bf16[4,20,256]{2,1,0:T(8,128)(2,1)S(1)} collective-permute-done((bf16[4,20,256]{2,1,0:T(8,128)(2,1)S(1)}, bf16[4,20,256]{2,1,0:T(8,128)(2,1)S(1)}, u32[]{:S(2)}, u32[]{:S(2)}) %collective-permute-start.2) | collective-permute-done | bytes 40992 | tf_op jit(solution)/shard_map/ppermute | solution.py:13
  149.3 1.9 collective-permute-start.3
  151.3 4.2 %collective-permute-done.3 = bf16[16,4,256]{2,1,0:T(4,128)(2,1)S(1)} collective-permute-done((bf16[16,4,256]{2,1,0:T(4,128)(2,1)S(1)}, bf16[16,4,256]{2,1,0:T(4,128)(2,1)S(1)}, u32[]{:S(2)}, u32[]{:S(2)}) %collective-permute-start.3) | collective-permute-done | bytes 32800 | tf_op jit(solution)/shard_map/ppermute | solution.py:13
  155.5 0.7 fusion.66
  156.3 1.9 collective-permute-start.4
  158.2 1.6 collective-permute-done.4
  159.8 1.9 collective-permute-start.5
  161.7 7.7 %collective-permute-done.5 = bf16[4,20,256]{2,1,0:T(8,128)(2,1)S(1)} collective-permute-done((bf16[4,20,256]{2,1,0:T(8,128)(2,1)S(1)}, bf16[4,20,256]{2,1,0:T(8,128)(2,1)S(1)}, u32[]{:S(2)}, u32[]{:S(2)}) %collective-permute-start.5) | collective-permute-done | bytes 40992 | tf_op jit(solution)/shard_map/ppermute | solution.py:13
  169.4 6.1 %reshape.154 = bf16[5,4,5,4,65,4]{5,4,3,2,1,0:T(8,128)(2,1)} reshape(bf16[20,20,260]{2,1,0:T(8,128)(2,1)S(1)} %fusion.58) | data formatting | bytes 416000 | tf_op jit(solution)/shard_map/reshape | solution.py:31
  175.5 3.5 %fusion.2 = f32[4,4,64,512,1,1]{3,2,5,1,4,0:T(8,128)S(1)} fusion(bf16[5,4,5,4,65,4]{5,4,3,2,1,0:T(8,128)(2,1)} %reshape.154, bf16[2,4,2,4,2,4,512]{6,5,4,3,2,1,0:T(4,128)(2,1)S(1)} %copy-done.6), kind=kOutput, calls=%fused_computation.6 | convolution fusion | flops 67108864 | bytes 6356992 | tf_op jit(solution)/shard_map/iajbkc,abcn->ijkn/dot_general | solution.py:44
  179.0 0.8 copy-done.1
  179.9 1.6 fusion.4
  181.5 1.2 fusion.6
  182.7 1.6 fusion.8
  184.3 1.2 fusion.10
  185.5 1.6 fusion.12
  187.1 2.5 %fusion.14 = f32[4,4,64,512,1,1]{3,2,5,1,4,0:T(8,128)} fusion(bf16[5,4,5,4,65,4]{5,4,3,2,1,0:T(8,128)(2,1)S(1)} %copy-done.1, bf16[2,4,2,4,2,4,512]{6,5,4,3,2,1,0:T(4,128)(2,1)S(1)} %copy-done.6), kind=kOutput, calls=%fused_computation.18 | convolution fusion | flops 67108864 | bytes 6356992 | tf_op jit(solution)/shard_map/iajbkc,abcn->ijkn/dot_general | solution.py:44
  189.6 4.8 %clamp_subtract_fusion = f32[4,4,64,512]{3,2,1,0:T(8,128)} fusion(f32[4,4,64,512]{3,2,1,0:T(8,128)S(1)} %clamp_subtract_fusion.1, f32[4,4,64,512,1,1]{3,2,5,1,4,0:T(8,128)S(1)} %fusion.2, f32[4,4,64,512,1,1]{3,2,5,1,4,0:T(8,128)S(1)} %fusion.4, f32[4,4,64,512,1,1]{3,2,5,1,4,0:T(8,128)S(1)} %fusion.6, f32[4,4,64,512,1,1]{3,2,5,1,4,0:T(8,128)S(1)} %fusion.8, ...), kind=kOutput, calls=%fused_computation.36 | convolution fusion | flops 72876032 | bytes 23134208 | tf_op jit(solution)/shard_map/iajbkc,abcn->ijkn/dot_general | solution.py:44
  (48 shorter events, 2.4 us)
Async XLA Ops:
  0.6 17.4 %copy-start.4 = (f32[1024,256]{1,0:T(8,128)S(1)}, f32[1024,256]{1,0:T(8,128)}, u32[]{:S(2)}) copy-start(f32[1024,256]{1,0:T(8,128)} %param.12) | copy-start | bytes 3145732
  0.6 1.3 copy-start.7
  0.7 17.3 %copy-start.8 = (s32[1024]{0:T(1024)S(1)}, s32[1024]{0:T(1024)}, u32[]{:S(2)}) copy-start(s32[1024]{0:T(1024)} %param.15) | copy-start | bytes 12292
  0.7 17.3 %copy-start.9 = (f32[4]{0:T(128)S(1)}, f32[4]{0:T(128)}, u32[]{:S(2)}) copy-start(f32[4]{0:T(128)} %param.16) | copy-start | bytes 52
  7.5 17.6 %all-to-all-start = ((s32[128,16,1]{1,2,0:T(1,128)}), s32[128,16,1]{1,2,0:T(1,128)S(1)}, u32[]{:S(2)}, u32[]{:S(2)}) async-start(s32[128,16,1]{1,2,0:T(1,128)} %bitcast.8), calls=%async_computation | async-start | bytes 131072 | tf_op jit(solution)/shard_map/all_to_all | solution.py:119
  25.1 37.4 %copy-start = (f32[16,16,256]{2,1,0:T(8,128)S(1)}, f32[16,16,256]{2,1,0:T(8,128)}, u32[]{:S(2)}) copy-start(f32[16,16,256]{2,1,0:T(8,128)} %param.11) | copy-start | bytes 786436
  25.2 37.4 %all-to-all-start.1 = ((f32[128,16,256]{2,1,0:T(8,128)}), f32[128,16,256]{2,1,0:T(8,128)S(1)}, u32[]{:S(2)}, u32[]{:S(2)}) async-start(f32[128,16,256]{2,1,0:T(8,128)} %bitcast.310), calls=%async_computation.1 | async-start | bytes 4194304 | tf_op jit(solution)/shard_map/all_to_all | solution.py:118
  62.6 18.9 %copy-start.3 = (bf16[512,512]{1,0:T(8,128)(2,1)S(1)}, bf16[512,512]{1,0:T(8,128)(2,1)}, u32[]{:S(2)}) copy-start(bf16[512,512]{1,0:T(8,128)(2,1)} %param.17) | copy-start | bytes 1572868
  74.4 4.1 %collective-permute-start = (bf16[16,4,256]{2,1,0:T(4,128)(2,1)S(1)}, bf16[16,4,256]{2,1,0:T(4,128)(2,1)S(1)}, u32[]{:S(2)}, u32[]{:S(2)}) collective-permute-start(bf16[16,4,256]{2,1,0:T(4,128)(2,1)S(1)} %slice.235), channel_id=1, source_target_pairs={{1,0},{2,1},{3,2},{4,3},{5,4},{6,5},{7,6},{8,7},{9,8},{10,9},{11,1... | collective-permute-start | bytes 98312 | tf_op jit(solution)/shard_map/ppermute | solution.py:13
  78.5 9.9 %collective-permute-start.1 = (bf16[4,20,256]{2,1,0:T(8,128)(2,1)S(1)}, bf16[4,20,256]{2,1,0:T(8,128)(2,1)S(1)}, u32[]{:S(2)}, u32[]{:S(2)}) collective-permute-start(bf16[4,20,256]{2,1,0:T(8,128)(2,1)S(1)} %pad_maximum_fusion.1), channel_id=1, source_target_pairs={{16,0},{32,16},{48,32},{64,48},{80,64},{96,80},{112,96},{17,1},{33... | collective-permute-start | bytes 122888 | tf_op jit(solution)/shard_map/ppermute | solution.py:13
  81.6 24.7 %copy-start.5 = (bf16[2,4,2,4,2,4,512]{6,5,4,3,2,1,0:T(4,128)(2,1)}, bf16[2,4,2,4,2,4,512]{6,5,4,3,2,1,0:T(4,128)(2,1)S(1)}, u32[]{:S(2)}) copy-start(bf16[2,4,2,4,2,4,512]{6,5,4,3,2,1,0:T(4,128)(2,1)S(1)} %reshape.151) | copy-start | bytes 1572868
  94.8 4.4 %copy-start.2 = (bf16[5,4,5,4,65,4]{5,4,3,2,1,0:T(8,128)(2,1)S(1)}, bf16[5,4,5,4,65,4]{5,4,3,2,1,0:T(8,128)(2,1)}, u32[]{:S(2)}) copy-start(bf16[5,4,5,4,65,4]{5,4,3,2,1,0:T(8,128)(2,1)} %reshape.150) | copy-start | bytes 624004
  143.3 6.0 %collective-permute-start.2 = (bf16[4,20,256]{2,1,0:T(8,128)(2,1)S(1)}, bf16[4,20,256]{2,1,0:T(8,128)(2,1)S(1)}, u32[]{:S(2)}, u32[]{:S(2)}) collective-permute-start(bf16[4,20,256]{2,1,0:T(8,128)(2,1)S(1)} %slice.352), channel_id=1, source_target_pairs={{0,16},{16,32},{32,48},{48,64},{64,80},{80,96},{96,112},{1,17},{17... | collective-permute-start | bytes 122888 | tf_op jit(solution)/shard_map/ppermute | solution.py:13
  149.3 6.1 %collective-permute-start.3 = (bf16[16,4,256]{2,1,0:T(4,128)(2,1)S(1)}, bf16[16,4,256]{2,1,0:T(4,128)(2,1)S(1)}, u32[]{:S(2)}, u32[]{:S(2)}) collective-permute-start(bf16[16,4,256]{2,1,0:T(4,128)(2,1)S(1)} %slice.353), channel_id=1, source_target_pairs={{0,1},{1,2},{2,3},{3,4},{4,5},{5,6},{6,7},{7,8},{8,9},{9,10},{10,1... | collective-permute-start | bytes 98312 | tf_op jit(solution)/shard_map/ppermute | solution.py:13
  156.3 3.5 %collective-permute-start.4 = (bf16[16,4,256]{2,1,0:T(4,128)(2,1)S(1)}, bf16[16,4,256]{2,1,0:T(4,128)(2,1)S(1)}, u32[]{:S(2)}, u32[]{:S(2)}) collective-permute-start(bf16[16,4,256]{2,1,0:T(4,128)(2,1)S(1)} %slice.266), channel_id=1, source_target_pairs={{1,0},{2,1},{3,2},{4,3},{5,4},{6,5},{7,6},{8,7},{9,8},{10,9},{11,1... | collective-permute-start | bytes 98312 | tf_op jit(solution)/shard_map/ppermute | solution.py:13
  159.8 9.6 %collective-permute-start.5 = (bf16[4,20,256]{2,1,0:T(8,128)(2,1)S(1)}, bf16[4,20,256]{2,1,0:T(8,128)(2,1)S(1)}, u32[]{:S(2)}, u32[]{:S(2)}) collective-permute-start(bf16[4,20,256]{2,1,0:T(8,128)(2,1)S(1)} %pad_maximum_fusion), channel_id=1, source_target_pairs={{16,0},{32,16},{48,32},{64,48},{80,64},{96,80},{112,96},{17,1},{33... | collective-permute-start | bytes 122888 | tf_op jit(solution)/shard_map/ppermute | solution.py:13
  169.4 6.1 %copy-start.6 = (bf16[2,4,2,4,2,4,512]{6,5,4,3,2,1,0:T(4,128)(2,1)S(1)}, bf16[2,4,2,4,2,4,512]{6,5,4,3,2,1,0:T(4,128)(2,1)}, u32[]{:S(2)}) copy-start(bf16[2,4,2,4,2,4,512]{6,5,4,3,2,1,0:T(4,128)(2,1)} %copy-done.5) | copy-start | bytes 1572868
  175.5 4.4 %copy-start.1 = (bf16[5,4,5,4,65,4]{5,4,3,2,1,0:T(8,128)(2,1)S(1)}, bf16[5,4,5,4,65,4]{5,4,3,2,1,0:T(8,128)(2,1)}, u32[]{:S(2)}) copy-start(bf16[5,4,5,4,65,4]{5,4,3,2,1,0:T(8,128)(2,1)} %reshape.154) | copy-start | bytes 624004
where the time goes:
time: 197 us; the launch traced here: 195 us
  matrix products  46.1 us (23%)
  local copies, waits for them, and re-layouts  39.5 us (20%)
  waiting for transfers between devices  38.1 us (19%)
  other arithmetic  36.8 us (19%)
  starting transfers between devices  32.9 us (17%)
    dot_general x16, matrix products, correlate(): jnp.einsum('iajbkc,abcn->ijkn', block_piece, dict_blocks[shift_a, :, shif...  44.9 us
    ppermute x6, waiting for transfers between devices, passed_along(): return lax.ppermute(block, axis, route)  25.8 us
    scatter-add x1, other arithmetic, body(): fold = jnp.zeros((bin_count,), jnp.float32).at[safe_slots].add(jnp.ones(s...  14.7 us
    ppermute x6, starting transfers between devices, passed_along(): return lax.ppermute(block, axis, route)  13.1 us
    reshape x2, local copies, waits for them, and re-layouts, correlate(): extended = extended.reshape(patch_i + 1, 4, patch_i + 1, 4, patch_k + 1, 4)  12.4 us
    all_to_all x1, waiting for transfers between devices, body(): lax.all_to_all(send_traces, ('inline', 'xline'), split_axis=0, concat_axi...  11.9 us
    scatter-add x1, other arithmetic, body(): jnp.zeros((bin_count, time_len), jnp.float32).at[safe_slots]  11.7 us
    all_to_all x1, starting transfers between devices, body(): lax.all_to_all(send_slots, ('inline', 'xline'), split_axis=0, concat_axis...  10.4 us
  transfers between devices with their start and end apart: 8, of which 8 were waited for; matrix products, arithmetic and copies ran while one was open for 12% of the time, Pallas kernels for 0%

commit v1 on v0

v1 whole, which is shorter than its diff:
```python
import math

import jax
import jax.numpy as jnp
from jax import lax
from jax.experimental import pallas as pl
from jax.experimental.pallas import tpu as pltpu
from jax.sharding import PartitionSpec as P

step_size = 0.25
threshold = 0.02
octaves = 40.0
code_top = 32767.0
log_top = math.log2(12.0)
vmem_bytes = 48 * 1024 * 1024


def shrink_codes(values):
    return values - jnp.clip(values, -threshold, threshold)


def call_kernel(kernel, out_shape, scratch, smem_inputs, inputs):
    vmem = pl.BlockSpec(memory_space=pltpu.VMEM)
    smem = pl.BlockSpec(memory_space=pltpu.SMEM)
    return pl.pallas_call(
        kernel,
        out_shape=out_shape,
        in_specs=[smem] * len(smem_inputs) + [vmem] * len(inputs),
        out_specs=jax.tree.map(lambda _: vmem, out_shape),
        scratch_shapes=scratch,
        compiler_params=pltpu.CompilerParams(vmem_limit_bytes=vmem_bytes),
    )(*smem_inputs, *inputs)


def encode(values):
    size = jnp.log2(jnp.maximum(jnp.abs(values), 1e-30))
    code = (size + (octaves - log_top)) * (code_top / octaves)
    code = jnp.clip(jnp.round(code), 0.0, code_top).astype(jnp.int32)
    return jnp.where(values < 0, -code, code)


def decode(code):
    code = code.astype(jnp.float32)
    size = jnp.exp2(jnp.abs(code) * (octaves / code_top) + (log_top - octaves))
    return size * jnp.clip(code, -1.0, 1.0)


def pack_kernel(gains, traces, dest, slot, vid, out):
    trace_count = traces.shape[0]
    device_count = out.shape[0]
    chunks = trace_count // 128
    source = lax.rem(lax.axis_index("xline"), 8)
    survey = vid[...]
    gain = jnp.zeros(survey.shape, jnp.float32)
    for number in range(gains.shape[0]):
        gain = jnp.where(survey == number, gains[number], gain)
    gain = jnp.transpose(jnp.broadcast_to(gain, (128, trace_count)))
    high, low = [], []
    for half in range(2):
        code = encode(traces[:, half * 128 : half * 128 + 128] * gain)
        high.append((code >> 8).astype(jnp.float32).astype(jnp.bfloat16))
        low.append((code & 255).astype(jnp.float32).astype(jnp.bfloat16))
    halves = jnp.concatenate(high + low, axis=1)

    row = lax.broadcasted_iota(jnp.int32, (128, 128), 0)
    lane = lax.broadcasted_iota(jnp.int32, (128, 128), 1)
    before = jnp.where(row < lane, 1.0, 0.0).astype(jnp.bfloat16)
    carry = jnp.zeros((device_count, 1), jnp.float32)
    places, owners, listed = [], [], []
    for chunk in range(chunks):
        target = dest[:, chunk * 128 : chunk * 128 + 128]
        hit = jnp.where(row == target, 1.0, 0.0)
        hit_half = hit.astype(jnp.bfloat16)
        earlier = jnp.dot(hit_half, before, preferred_element_type=jnp.float32)
        rank = jnp.sum(hit * (earlier + carry), axis=0, keepdims=True)
        carry = carry + jnp.sum(hit, axis=1, keepdims=True)
        rank = rank.astype(jnp.int32)
        places.append(target * 16 + rank)
        owners.append(hit_half)
        wanted = (slot[:, chunk * 128 : chunk * 128 + 128] + 1).astype(jnp.float32)
        listed.append(jnp.where(row == rank + 16 * source, wanted, 0.0).astype(jnp.bfloat16))
    place = jnp.concatenate(places, axis=1)
    owner = jnp.concatenate(owners, axis=1)
    listing = jnp.concatenate(listed, axis=1)
    slots = lax.dot_general(
        owner, listing, (((1,), (1,)), ((), ())), preferred_element_type=jnp.float32
    )
    slots = slots.astype(jnp.int32)
    out[:, 32:40, :] = jnp.broadcast_to(slots[:, None, :], (device_count, 8, 128)).astype(jnp.int16)
    rows = 256
    index = lax.broadcasted_iota(jnp.int32, (rows, trace_count), 0)
    for block in range(device_count * 16 // rows):
        pick = jnp.where(index == place - block * rows, 1.0, 0.0).astype(jnp.bfloat16)
        moved = jnp.dot(pick, halves, preferred_element_type=jnp.float32)
        code = (moved[:, :256] * 256.0 + moved[:, 256:]).astype(jnp.int32).astype(jnp.int16)
        spot = pl.ds(block * (rows // 16), rows // 16)
        out[spot, 0:16, :] = code[:, :128].reshape(rows // 16, 16, 128)
        out[spot, 16:32, :] = code[:, 128:].reshape(rows // 16, 16, 128)


def merge_kernel(got, base, whole, half, upper, lower, pick, parts, turned):
    groups = got.shape[0] // 8
    bin_row = lax.broadcasted_iota(jnp.int32, (256, 128), 0)
    bin_slot = (
        (bin_row // 64) * 64 + ((bin_row // 4) % 4) * 16 + ((bin_row // 16) % 4) * 4 + bin_row % 4
    )
    wanted = bin_slot + 1
    fold = jnp.zeros((256, 128), jnp.float32)
    for group in range(groups):
        spot = pl.ds(group * 8, 8)
        listed = jnp.sum(got[spot, 32:40, :].astype(jnp.int32), axis=0)
        listed = jnp.broadcast_to(listed[None], (32, 8, 128)).reshape(256, 128)
        hit = jnp.where(listed == wanted, 1.0, 0.0)
        fold = fold + hit
        pick[:, group * 128 : group * 128 + 128] = hit.astype(jnp.bfloat16)
        for side in range(2):
            code = got[spot, side * 16 : side * 16 + 16, :].reshape(128, 128).astype(jnp.int32)
            value = decode(code)
            high = value.astype(jnp.bfloat16)
            low = (value - high.astype(jnp.float32)).astype(jnp.bfloat16)
            parts[group * 128 : group * 128 + 128, side * 128 : side * 128 + 128] = high
            parts[group * 128 : group * 128 + 128, 256 + side * 128 : 384 + side * 128] = low
    stack = jnp.dot(pick[...], parts[...], preferred_element_type=jnp.float32)
    fold = jnp.sum(fold, axis=1, keepdims=True)
    merged = (base[...] + (stack[:, :256] + stack[:, 256:])) / (1.0 + fold)
    turned[0] = jnp.transpose(merged[:128])
    turned[1] = jnp.transpose(merged[128:])
    lane = lax.broadcasted_iota(jnp.int32, (64, 128), 1) // 16
    for tile in range(2):
        slabs = [turned[tile, pl.ds(phase, 64, stride=4), :] for phase in range(4)]
        for part in range(2):
            for pair in range(2):
                made = None
                for odd in range(2):
                    for phase in range(4):
                        shift = (48 * odd + 16 * phase - 64 * part - 32 * pair) % 128
                        piece = slabs[phase] if shift == 0 else pltpu.roll(slabs[phase], shift, 1)
                        made = (
                            piece if made is None else jnp.where(lane == 4 * odd + phase, piece, made)
                        )
                block_row = 2 * tile + part
                whole[block_row, pair] = made
                made = made.astype(jnp.bfloat16)
                half[pair, block_row] = made
                if block_row < 2:
                    upper[pair, block_row] = made
                if block_row == 3:
                    lower[pair, 0] = made


def time_rolled(values, distance):
    row = lax.broadcasted_iota(jnp.int32, values.shape, 0)
    if distance < 0:
        return jnp.where(row == values.shape[0] - 1, 0.0, pltpu.roll(values, values.shape[0] - 1, 0))
    return jnp.where(row == 0, 0.0, pltpu.roll(values, 1, 0))


def widened(both):
    left = lax.broadcasted_iota(jnp.int32, both.shape, 1) < 64
    later = time_rolled(both, -1)
    even = jnp.where(left, both, pltpu.roll(later, 64, 1))
    odd = jnp.where(left, pltpu.roll(both, 64, 1), later)
    return even.astype(jnp.bfloat16), odd.astype(jnp.bfloat16)


def sparse_kernel(
    whole, own, before, after, words, words_back, codes, residual, field, first, recon, tail, turned, binned
):
    inline_at, xline_at = lax.axis_index("inline"), lax.axis_index("xline")
    inline_last = inline_at == lax.axis_size("inline") - 1
    xline_last = xline_at == lax.axis_size("xline") - 1
    not_top = jnp.where(inline_at == 0, 0.0, 1.0)
    not_left = jnp.where(xline_at == 0, 0.0, 1.0)
    not_bottom = jnp.where(inline_last, 0.0, 1.0)
    not_right = jnp.where(xline_last, 0.0, 1.0)

    sources = [before.at[0], own.at[0], own.at[1], after.at[0]]
    for block_row in range(7):
        for pair in range(4):
            even, odd = widened(sources[pair][block_row].astype(jnp.float32))
            if pair > 0:
                field[block_row, 2 * pair - 1] = even
            if pair < 4:
                field[block_row, 2 * pair] = odd

    def correlated(source, patch_row, count):
        lhs = [
            source[patch_row + shift_a, shift_b : shift_b + count].reshape(count * 64, 128)
            for shift_a in (0, 1)
            for shift_b in (0, 1)
        ]
        return jnp.dot(
            jnp.concatenate(lhs, axis=1), words[...], preferred_element_type=jnp.float32
        )

    for patch_row in range(6):
        found = shrink_codes(step_size * correlated(field, patch_row, 6))
        if 1 <= patch_row <= 4:
            first[patch_row - 1] = found[64:320]
        if patch_row == 0:
            found = found * not_top
        found = jnp.concatenate([found[:64] * not_left, found[64:]], axis=0).astype(jnp.bfloat16)
        given = jnp.dot(found, words_back[...], preferred_element_type=jnp.float32)
        given = given.reshape(6, 64, 512)
        if patch_row > 0:
            upper = given[0:5, :, 128:256] + given[1:6, :, 0:128]
            if patch_row == 1:
                recon[0] = tail[...] + upper
            elif patch_row < 6:
                recon[patch_row - 1] = tail[...] + upper
        if patch_row < 5:
            tail[...] = given[0:5, :, 384:512] + given[1:6, :, 256:384]

    left = lax.broadcasted_iota(jnp.int32, (64, 128), 1) < 64
    for block_row in range(5):
        for pair in range(3):
            even = recon[block_row, 2 * pair]
            odd = recon[block_row, 2 * pair + 1] if pair < 2 else even
            near = jnp.where(left, even, pltpu.roll(odd, 64, 1))
            far = jnp.where(left, pltpu.roll(even, 64, 1), odd)
            rebuilt = near + time_rolled(far, 1)
            if block_row < 4 and pair < 2:
                rest = whole[block_row, pair] - rebuilt
                whole_rest = rest
                binned[block_row, pair] = whole_rest
            elif pair < 2:
                rest = (own[pair, 5].astype(jnp.float32) - rebuilt) * not_bottom
            else:
                rest = (after[0, block_row + 1].astype(jnp.float32) - rebuilt) * not_right
                if block_row == 4:
                    rest = rest * not_bottom
            even, odd = widened(rest)
            field[block_row, 2 * pair] = even
            if pair < 2:
                field[block_row, 2 * pair + 1] = odd

    for patch_row in range(4):
        found = first[patch_row] + step_size * correlated(field, patch_row, 4)
        codes[patch_row] = shrink_codes(found).reshape(4, 64, 512)

    lane = lax.broadcasted_iota(jnp.int32, (64, 128), 1) // 16
    for tile in range(2):
        for phase in range(4):
            made = None
            for part in range(2):
                for pair in range(2):
                    for odd in range(2):
                        shift = (64 * part + 32 * pair - 48 * odd - 16 * phase) % 128
                        piece = binned[2 * tile + part, pair]
                        piece = piece if shift == 0 else pltpu.roll(piece, shift, 1)
                        made = (
                            piece
                            if made is None
                            else jnp.where(lane == 4 * part + 2 * pair + odd, piece, made)
                        )
            turned[tile, pl.ds(phase, 64, stride=4), :] = made
    for tile in range(2):
        flat = jnp.transpose(turned[tile])
        for part in range(2):
            for block_col in range(4):
                for row in range(4):
                    at = part * 64 + block_col * 16 + row * 4
                    to = (2 * tile + part) * 64 + row * 16 + block_col * 4
                    residual[to : to + 4, :] = flat[at : at + 4, :]


def body(
    base_volume, vintage_traces, dest_device, dest_slot, vintage_id, vintage_gains, dictionary
):
    trace_count, time_len = vintage_traces.shape
    device_count = lax.axis_size("inline") * lax.axis_size("xline")
    sent = call_kernel(
        pack_kernel,
        jax.ShapeDtypeStruct((device_count, 40, 128), jnp.int16),
        [],
        [vintage_gains],
        [
            vintage_traces,
            dest_device.reshape(1, trace_count),
            dest_slot.reshape(1, trace_count),
            vintage_id.reshape(1, trace_count),
        ],
    )
    got = lax.all_to_all(sent, ("inline", "xline"), split_axis=0, concat_axis=0, tiled=True)
    words = dictionary.reshape(2, 4, 2, 4, 2, 4, 512).transpose(0, 2, 4, 5, 1, 3, 6).reshape(512, 512)
    words_back = words.T
    base = (
        base_volume.reshape(4, 4, 4, 4, time_len).transpose(0, 2, 1, 3, 4).reshape(256, time_len)
    )
    pair_shape = lambda *lead: jax.ShapeDtypeStruct(lead + (64, 128), jnp.bfloat16)
    whole, half, upper, lower = call_kernel(
        merge_kernel,
        (
            jax.ShapeDtypeStruct((4, 2, 64, 128), jnp.float32),
            pair_shape(2, 4),
            pair_shape(2, 2),
            pair_shape(2, 1),
        ),
        [
            pltpu.VMEM((256, device_count * 16), jnp.bfloat16),
            pltpu.VMEM((device_count * 16, 512), jnp.bfloat16),
            pltpu.VMEM((2, 256, 128), jnp.float32),
        ],
        [],
        [got, base],
    )

    def along(block, axis, distance):
        devices = range(lax.axis_size(axis))
        route = [(i - distance, i) for i in devices if i - distance in devices]
        return lax.ppermute(block, axis, route)

    from_below = along(upper, "inline", -1)
    from_above = along(lower, "inline", 1)
    own = jnp.concatenate([from_above, half, from_below], axis=1)
    after = along(own[0:1], "xline", -1)
    before = along(own[1:2], "xline", 1)
    codes, residual = call_kernel(
        sparse_kernel,
        (
            jax.ShapeDtypeStruct((4, 4, 64, 512), jnp.float32),
            jax.ShapeDtypeStruct((256, time_len), jnp.float32),
        ),
        [
            pltpu.VMEM((7, 7, 64, 128), jnp.bfloat16),
            pltpu.VMEM((4, 256, 512), jnp.float32),
            pltpu.VMEM((5, 5, 64, 128), jnp.float32),
            pltpu.VMEM((5, 64, 128), jnp.float32),
            pltpu.VMEM((2, 256, 128), jnp.float32),
            pltpu.VMEM((4, 2, 64, 128), jnp.float32),
        ],
        [],
        [whole, own, before, after, words, words_back],
    )
    return codes, residual.reshape(16, 16, time_len)


def solution(mesh):
    in_specs = (
        P("inline", "xline", None),
        P(("inline", "xline"), None),
        P(("inline", "xline"), None),
        P(("inline", "xline")),
        P(("inline", "xline")),
        P(),
        P(),
    )
    out_specs = (P("inline", "xline", None, None), P("inline", "xline", None))
    return jax.shard_map(body, mesh=mesh, in_specs=in_specs, out_specs=out_specs, check_vma=False)
```

time: 197 us -> 70.7 us (0.36)
  matrix products: 46.1 us -> 0 us
  other arithmetic: 36.8 us -> 0 us
  local copies, waits for them, and re-layouts: 39.5 us -> 4.92 us
  starting transfers between devices: 32.9 us -> 20.8 us
  Pallas kernels: 0 us -> 12 us
  waiting for transfers between devices: 38.1 us -> 31.8 us
    dot_general x17 -> x0, matrix products: 46.1 us -> none  [the longest x16 44.9 us: correlate(): jnp.einsum('iajbkc,abcn->ijkn', block_piece, dict_blocks[shift_a, :, shif...]
    scatter-add x4 -> x0, other arithmetic: 26.4 us -> none  [the longest x1 14.7 us: body(): fold = jnp.zeros((bin_count,), jnp.float32).at[safe_slots].add(jnp.ones(s...]
    reshape x4 -> x7, local copies, waits for them, and re-layouts: 21.1 us -> 0.92 us  [the longest x4 0.73 us: body(): dictionary.reshape(2, 4, 2, 4, 2, 4, 512).transpose(0, 2, 4, 5, 1, 3, 6)]
    ppermute x6 -> x4, waiting for transfers between devices: 25.8 us -> 12.3 us  [along(): return lax.ppermute(block, axis, route)]
    pallas_call x0 -> x3, Pallas kernels: none -> 12 us  [call_kernel(): pl.pallas_call(kernel, out_shape=out_shape, in_specs=[smem] * len(smem_in...]
    all_to_all x2 -> x1, starting transfers between devices: 19.7 us -> 10.4 us  [body(): lax.all_to_all(sent, ('inline', 'xline'), split_axis=0, concat_axis=0, ti...]
    add x1 -> x0, local copies, waits for them, and re-layouts: 8.66 us -> none  [reconstruct(): running = moved if running is None else running + moved]
    all_to_all x2 -> x1, waiting for transfers between devices: 12.3 us -> 19.5 us  [body(): lax.all_to_all(sent, ('inline', 'xline'), split_axis=0, concat_axis=0, ti...]
  transfers between devices with their start and end apart: 8 -> 5, of which waited for: 8 -> 3; matrix products, arithmetic and copies ran while one was open for 12% -> 1% of each run, Pallas kernels for 0% -> 0%
where the time goes in v1:
time: 70.7 us; the launch traced here: 70.3 us
  waiting for transfers between devices  31.8 us (45%)
  starting transfers between devices  20.8 us (29%)
  Pallas kernels  12 us (17%)
  local copies, waits for them, and re-layouts  4.92 us (7%)
  between operations  0.8 us (1%)
    all_to_all x1, waiting for transfers between devices, body(): lax.all_to_all(sent, ('inline', 'xline'), split_axis=0, concat_axis=0, ti...  19.5 us
    ppermute x4, waiting for transfers between devices, along(): return lax.ppermute(block, axis, route)  12.3 us
    pallas_call x3, Pallas kernels, call_kernel(): pl.pallas_call(kernel, out_shape=out_shape, in_specs=[smem] * len(smem_in...  12 us
    ppermute x4, starting transfers between devices, along(): return lax.ppermute(block, axis, route)  10.4 us
    all_to_all x1, starting transfers between devices, body(): lax.all_to_all(sent, ('inline', 'xline'), split_axis=0, concat_axis=0, ti...  10.4 us
    unnamed x16, local copies, waits for them, and re-layouts  3.97 us
  transfers between devices with their start and end apart: 5, of which 3 were waited for; matrix products, arithmetic and copies ran while one was open for 1% of the time, Pallas kernels for 0%

profile of v1, /device:TPU:14, one launch (start us, length us, event | category | flops | bytes accessed | tf_op | source)
XLA Modules:
  0.0 70.3 jit_solution(16850091585834522160)
XLA Ops:
  0.6 0.0 copy-start
  0.6 1.2 %copy-done = f32[1024,256]{1,0:T(8,128)S(1)} copy-done((f32[1024,256]{1,0:T(8,128)S(1)}, f32[1024,256]{1,0:T(8,128)}, u32[]{:S(2)}) %copy-start) | copy-done | bytes 1048600
  1.9 0.0 copy-start.1
  1.9 0.7 copy-done.1
  2.5 0.0 copy-start.2
  2.5 0.7 copy-done.2
  3.2 0.0 copy-start.3
  3.2 0.7 copy-done.3
  3.9 0.0 copy-start.4
  3.9 0.7 copy-done.4
  4.6 4.9 %shard_map.86 = s16[128,40,128]{2,1,0:T(8,128)(2,1)} custom-call(f32[4]{0:T(128)S(1)} %copy-done.4, f32[1024,256]{1,0:T(8,128)S(1)} %copy-done, s32[1,1024]{1,0:T(1,128)S(1)} %bitcast.12, s32[1,1024]{1,0:T(1,128)S(1)} %bitcast.13, s32[1,1024]{1,0:T(1,128)S(1)} %bitcast.14), custom_call_target="tpu_custom_call" | custom-call | tf_op jit(solution)/shard_map/pallas_call | solution.py:25
  9.4 0.0 copy-start.6
  9.4 10.4 %all-to-all-start = ((s16[128,40,128]{2,1,0:T(8,128)(2,1)}), s16[128,40,128]{2,1,0:T(8,128)(2,1)S(1)}, u32[]{:S(2)}, u32[]{:S(2)}) async-start(s16[128,40,128]{2,1,0:T(8,128)(2,1)} %shard_map.86), calls=%async_computation | async-start | bytes 2621440 | tf_op jit(solution)/shard_map/all_to_all | solution.py:284
  19.8 0.0 copy-done.6
  19.8 0.1 reshape.31
  19.9 0.1 reshape.32.base
  20.0 0.0 copy-start.5
  20.0 19.5 %all-to-all-done.got = s16[128,40,128]{2,1,0:T(8,128)(2,1)S(1)} async-done(((s16[128,40,128]{2,1,0:T(8,128)(2,1)}), s16[128,40,128]{2,1,0:T(8,128)(2,1)S(1)}, u32[]{:S(2)}, u32[]{:S(2)}) %all-to-all-start) | async-done | bytes 1310752 | tf_op jit(solution)/shard_map/all_to_all | solution.py:284
  39.5 2.4 %shard_map.87 = (f32[4,2,64,128]{3,2,1,0:T(8,128)S(1)}, bf16[2,4,64,128]{3,2,1,0:T(8,128)(2,1)S(1)}, bf16[2,2,64,128]{3,2,1,0:T(8,128)(2,1)S(1)}, bf16[2,1,64,128]{3,2,1,0:T(8,128)(2,1)S(1)}) custom-call(s16[128,40,128]{2,1,0:T(8,128)(2,1)S(1)} %all-to-all-done.got, f32[256,256]{1,0:T(8,128)S(1)} %reshape.32.base), custom_call_target="tpu_custom_call" | custom-call | tf_op jit(solution)/shard_map/pallas_call | solution.py:25
  42.0 4.2 %collective-permute-start = (bf16[2,1,64,128]{3,2,1,0:T(8,128)(2,1)S(1)}, bf16[2,1,64,128]{3,2,1,0:T(8,128)(2,1)S(1)}, u32[]{:S(2)}, u32[]{:S(2)}) collective-permute-start(bf16[2,1,64,128]{3,2,1,0:T(8,128)(2,1)S(1)} %get-tuple-element.9), channel_id=1, source_target_pairs={{0,16},{16,32},{32,48},{48,64},{64,80},{80,96},{96,112},{1,17},{17... | collective-permute-start | bytes 98312 | tf_op jit(solution)/shard_map/ppermute | solution.py:311
  46.2 1.9 %collective-permute-start.1 = (bf16[2,2,64,128]{3,2,1,0:T(8,128)(2,1)S(1)}, bf16[2,2,64,128]{3,2,1,0:T(8,128)(2,1)S(1)}, u32[]{:S(2)}, u32[]{:S(2)}) collective-permute-start(bf16[2,2,64,128]{3,2,1,0:T(8,128)(2,1)S(1)} %get-tuple-element.11), channel_id=1, source_target_pairs={{16,0},{32,16},{48,32},{64,48},{80,64},{96,80},{112,96},{17,1},{33... | collective-permute-start | bytes 196616 | tf_op jit(solution)/shard_map/ppermute | solution.py:311
  48.1 0.0 collective-permute-done
  48.2 8.5 %collective-permute-done.1 = bf16[2,2,64,128]{3,2,1,0:T(8,128)(2,1)S(1)} collective-permute-done((bf16[2,2,64,128]{3,2,1,0:T(8,128)(2,1)S(1)}, bf16[2,2,64,128]{3,2,1,0:T(8,128)(2,1)S(1)}, u32[]{:S(2)}, u32[]{:S(2)}) %collective-permute-start.1) | collective-permute-done | bytes 65568 | tf_op jit(solution)/shard_map/ppermute | solution.py:311
  56.7 1.9 %collective-permute-start.3 = (bf16[1,7,64,128]{3,2,1,0:T(8,128)(2,1)S(1)}, bf16[1,7,64,128]{3,2,1,0:T(8,128)(2,1)S(1)}, u32[]{:S(2)}, u32[]{:S(2)}) collective-permute-start(bf16[1,7,64,128]{3,2,1,0:T(8,128)(2,1)S(1)} %get-tuple-element.14), channel_id=1, source_target_pairs={{1,0},{2,1},{3,2},{4,3},{5,4},{6,5},{7,6},{8,7},{9,8},{10,9},{11,1... | collective-permute-start | bytes 344072 | tf_op jit(solution)/shard_map/ppermute | solution.py:311
  58.6 2.4 %collective-permute-start.2 = (bf16[1,7,64,128]{3,2,1,0:T(8,128)(2,1)S(1)}, bf16[1,7,64,128]{3,2,1,0:T(8,128)(2,1)S(1)}, u32[]{:S(2)}, u32[]{:S(2)}) collective-permute-start(bf16[1,7,64,128]{3,2,1,0:T(8,128)(2,1)S(1)} %get-tuple-element.15), channel_id=1, source_target_pairs={{0,1},{1,2},{2,3},{3,4},{4,5},{5,6},{6,7},{7,8},{8,9},{9,10},{10,1... | collective-permute-start | bytes 344072 | tf_op jit(solution)/shard_map/ppermute | solution.py:311
  61.0 0.0 copy-done.5
  61.0 0.1 reshape.33
  61.2 0.3 copy.17
  61.5 0.1 reshape.34.words
  61.6 0.2 copy.14
  61.8 0.0 collective-permute-done.3.after
  61.8 3.8 %collective-permute-done.2.before = bf16[1,7,64,128]{3,2,1,0:T(8,128)(2,1)S(1)} collective-permute-done((bf16[1,7,64,128]{3,2,1,0:T(8,128)(2,1)S(1)}, bf16[1,7,64,128]{3,2,1,0:T(8,128)(2,1)S(1)}, u32[]{:S(2)}, u32[]{:S(2)}) %collective-permute-start.2) | collective-permute-done | bytes 114720 | tf_op jit(solution)/shard_map/ppermute | solution.py:311
  65.6 4.7 %shard_map.88 = (f32[4,4,64,512]{3,2,1,0:T(8,128)}, f32[256,256]{1,0:T(8,128)}) custom-call(f32[4,2,64,128]{3,2,1,0:T(8,128)S(1)} %get-tuple-element.8.whole, bf16[2,7,64,128]{3,2,1,0:T(8,128)(2,1)S(1)} %constant_dynamic-update-slice_fusion.own, bf16[1,7,64,128]{3,2,1,0:T(8,128)(2,1)S(1)} %collective-permute-done.2.before, ...), custom_call_target="tpu_custom_call" | custom-call | tf_op jit(solution)/shard_map/pallas_call | solution.py:25
  (5 shorter events, 0.1 us)
Async XLA Ops:
  0.6 1.2 %copy-start = (f32[1024,256]{1,0:T(8,128)S(1)}, f32[1024,256]{1,0:T(8,128)}, u32[]{:S(2)}) copy-start(f32[1024,256]{1,0:T(8,128)} %traces.1) | copy-start | bytes 3145732
  1.9 0.7 copy-start.1
  2.5 0.7 copy-start.2
  3.2 0.7 copy-start.3
  3.9 0.7 copy-start.4
  9.4 10.4 %copy-start.6 = (f32[16,16,256]{2,1,0:T(8,128)S(1)}, f32[16,16,256]{2,1,0:T(8,128)}, u32[]{:S(2)}) copy-start(f32[16,16,256]{2,1,0:T(8,128)} %param.7) | copy-start | bytes 786436
  9.4 30.1 %all-to-all-start = ((s16[128,40,128]{2,1,0:T(8,128)(2,1)}), s16[128,40,128]{2,1,0:T(8,128)(2,1)S(1)}, u32[]{:S(2)}, u32[]{:S(2)}) async-start(s16[128,40,128]{2,1,0:T(8,128)(2,1)} %shard_map.86), calls=%async_computation | async-start | bytes 2621440 | tf_op jit(solution)/shard_map/all_to_all | solution.py:284
  20.0 41.0 %copy-start.5 = (bf16[512,512]{1,0:T(8,128)(2,1)S(1)}, bf16[512,512]{1,0:T(8,128)(2,1)}, u32[]{:S(2)}) copy-start(bf16[512,512]{1,0:T(8,128)(2,1)} %param.13) | copy-start | bytes 1572868
  42.0 6.1 %collective-permute-start = (bf16[2,1,64,128]{3,2,1,0:T(8,128)(2,1)S(1)}, bf16[2,1,64,128]{3,2,1,0:T(8,128)(2,1)S(1)}, u32[]{:S(2)}, u32[]{:S(2)}) collective-permute-start(bf16[2,1,64,128]{3,2,1,0:T(8,128)(2,1)S(1)} %get-tuple-element.9), channel_id=1, source_target_pairs={{0,16},{16,32},{32,48},{48,64},{64,80},{80,96},{96,112},{1,17},{17... | collective-permute-start | bytes 98312 | tf_op jit(solution)/shard_map/ppermute | solution.py:311
  46.2 10.5 %collective-permute-start.1 = (bf16[2,2,64,128]{3,2,1,0:T(8,128)(2,1)S(1)}, bf16[2,2,64,128]{3,2,1,0:T(8,128)(2,1)S(1)}, u32[]{:S(2)}, u32[]{:S(2)}) collective-permute-start(bf16[2,2,64,128]{3,2,1,0:T(8,128)(2,1)S(1)} %get-tuple-element.11), channel_id=1, source_target_pairs={{16,0},{32,16},{48,32},{64,48},{80,64},{96,80},{112,96},{17,1},{33... | collective-permute-start | bytes 196616 | tf_op jit(solution)/shard_map/ppermute | solution.py:311
  56.7 5.1 %collective-permute-start.3 = (bf16[1,7,64,128]{3,2,1,0:T(8,128)(2,1)S(1)}, bf16[1,7,64,128]{3,2,1,0:T(8,128)(2,1)S(1)}, u32[]{:S(2)}, u32[]{:S(2)}) collective-permute-start(bf16[1,7,64,128]{3,2,1,0:T(8,128)(2,1)S(1)} %get-tuple-element.14), channel_id=1, source_target_pairs={{1,0},{2,1},{3,2},{4,3},{5,4},{6,5},{7,6},{8,7},{9,8},{10,9},{11,1... | collective-permute-start | bytes 344072 | tf_op jit(solution)/shard_map/ppermute | solution.py:311
  58.6 7.0 %collective-permute-start.2 = (bf16[1,7,64,128]{3,2,1,0:T(8,128)(2,1)S(1)}, bf16[1,7,64,128]{3,2,1,0:T(8,128)(2,1)S(1)}, u32[]{:S(2)}, u32[]{:S(2)}) collective-permute-start(bf16[1,7,64,128]{3,2,1,0:T(8,128)(2,1)S(1)} %get-tuple-element.15), channel_id=1, source_target_pairs={{0,1},{1,2},{2,3},{3,4},{4,5},{5,6},{6,7},{7,8},{8,9},{9,10},{10,1... | collective-permute-start | bytes 344072 | tf_op jit(solution)/shard_map/ppermute | solution.py:311

commit v2 on v1

--- a/solution.py
+++ b/solution.py
@@ -19,17 +19,15 @@
     return values - jnp.clip(values, -threshold, threshold)
 
 
-def call_kernel(kernel, out_shape, scratch, smem_inputs, inputs):
-    vmem = pl.BlockSpec(memory_space=pltpu.VMEM)
-    smem = pl.BlockSpec(memory_space=pltpu.SMEM)
+def call_kernel(kernel, out_shape, out_spaces, scratch, in_space, inputs):
     return pl.pallas_call(
         kernel,
         out_shape=out_shape,
-        in_specs=[smem] * len(smem_inputs) + [vmem] * len(inputs),
-        out_specs=jax.tree.map(lambda _: vmem, out_shape),
+        in_specs=[pl.BlockSpec(memory_space=in_space)] * len(inputs),
+        out_specs=jax.tree.map(lambda space: pl.BlockSpec(memory_space=space), out_spaces),
         scratch_shapes=scratch,
         compiler_params=pltpu.CompilerParams(vmem_limit_bytes=vmem_bytes),
-    )(*smem_inputs, *inputs)
+    )(*inputs)
 
 
 def encode(values):
@@ -45,23 +43,21 @@
     return size * jnp.clip(code, -1.0, 1.0)
 
 
-def pack_kernel(gains, traces, dest, slot, vid, out):
+def pack_kernel(gains_in, traces_in, dest_in, slot_in, vid_in, out, gains, traces, dest, slot, vid, built, arrive, leave):
+    loads = [
+        pltpu.make_async_copy(source, target, arrive.at[number])
+        for number, (source, target) in enumerate(
+            ((dest_in, dest), (slot_in, slot), (gains_in, gains), (vid_in, vid), (traces_in, traces))
+        )
+    ]
+    for load in loads:
+        load.start()
     trace_count = traces.shape[0]
-    device_count = out.shape[0]
+    device_count = out.shape[0] // 17
     chunks = trace_count // 128
-    source = lax.rem(lax.axis_index("xline"), 8)
-    survey = vid[...]
-    gain = jnp.zeros(survey.shape, jnp.float32)
-    for number in range(gains.shape[0]):
-        gain = jnp.where(survey == number, gains[number], gain)
-    gain = jnp.transpose(jnp.broadcast_to(gain, (128, trace_count)))
-    high, low = [], []
-    for half in range(2):
-        code = encode(traces[:, half * 128 : half * 128 + 128] * gain)
-        high.append((code >> 8).astype(jnp.float32).astype(jnp.bfloat16))
-        low.append((code & 255).astype(jnp.float32).astype(jnp.bfloat16))
-    halves = jnp.concatenate(high + low, axis=1)
-
+    me = lax.axis_index("inline") * lax.axis_size("xline") + lax.axis_index("xline")
+    loads[0].wait()
+    loads[1].wait()
     row = lax.broadcasted_iota(jnp.int32, (128, 128), 0)
     lane = lax.broadcasted_iota(jnp.int32, (128, 128), 1)
     before = jnp.where(row < lane, 1.0, 0.0).astype(jnp.bfloat16)
@@ -75,51 +71,81 @@
         rank = jnp.sum(hit * (earlier + carry), axis=0, keepdims=True)
         carry = carry + jnp.sum(hit, axis=1, keepdims=True)
         rank = rank.astype(jnp.int32)
-        places.append(target * 16 + rank)
+        places.append(target * 17 + rank)
         owners.append(hit_half)
         wanted = (slot[:, chunk * 128 : chunk * 128 + 128] + 1).astype(jnp.float32)
-        listed.append(jnp.where(row == rank + 16 * source, wanted, 0.0).astype(jnp.bfloat16))
+        spot = lax.rem(17 * me + rank, 128)
+        listed.append(jnp.where(row == spot, wanted, 0.0).astype(jnp.bfloat16))
     place = jnp.concatenate(places, axis=1)
     owner = jnp.concatenate(owners, axis=1)
     listing = jnp.concatenate(listed, axis=1)
     slots = lax.dot_general(
         owner, listing, (((1,), (1,)), ((), ())), preferred_element_type=jnp.float32
-    )
-    slots = slots.astype(jnp.int32)
-    out[:, 32:40, :] = jnp.broadcast_to(slots[:, None, :], (device_count, 8, 128)).astype(jnp.int16)
-    rows = 256
+    ).astype(jnp.int32)
+
+    loads[2].wait()
+    loads[3].wait()
+    survey = vid[...]
+    gain = jnp.zeros(survey.shape, jnp.float32)
+    for number in range(gains.shape[0]):
+        gain = jnp.where(survey == number, gains[number], gain)
+    gain = jnp.transpose(jnp.broadcast_to(gain, (128, trace_count)))
+    loads[4].wait()
+    high, low = [], []
+    for half in range(2):
+        code = encode(traces[:, half * 128 : half * 128 + 128] * gain)
+        high.append((code >> 8).astype(jnp.float32).astype(jnp.bfloat16))
+        low.append((code & 255).astype(jnp.float32).astype(jnp.bfloat16))
+    halves = jnp.concatenate(high + low, axis=1)
+
+    owners_each = 16
+    rows = owners_each * 17
     index = lax.broadcasted_iota(jnp.int32, (rows, trace_count), 0)
-    for block in range(device_count * 16 // rows):
+    stores = []
+    for block in range(device_count // owners_each):
         pick = jnp.where(index == place - block * rows, 1.0, 0.0).astype(jnp.bfloat16)
         moved = jnp.dot(pick, halves, preferred_element_type=jnp.float32)
-        code = (moved[:, :256] * 256.0 + moved[:, 256:]).astype(jnp.int32).astype(jnp.int16)
-        spot = pl.ds(block * (rows // 16), rows // 16)
-        out[spot, 0:16, :] = code[:, :128].reshape(rows // 16, 16, 128)
-        out[spot, 16:32, :] = code[:, 128:].reshape(rows // 16, 16, 128)
+        code = (moved[:, :256] * 256.0 + moved[:, 256:]).astype(jnp.int32)
+        built[block * rows : block * rows + rows, :] = (code[:, :128] << 16) | (
+            code[:, 128:] & 65535
+        )
+        built[pl.ds(block * rows + 16, owners_each, stride=17), :] = slots[
+            block * owners_each : block * owners_each + owners_each
+        ]
+        spot = pl.ds(block * rows, rows)
+        stores.append(pltpu.make_async_copy(built.at[spot], out.at[spot], leave.at[block]))
+        stores[-1].start()
+    for store in stores:
+        store.wait()
 
 
 def merge_kernel(got, base, whole, half, upper, lower, pick, parts, turned):
-    groups = got.shape[0] // 8
+    tiles = got.shape[0] // 128
     bin_row = lax.broadcasted_iota(jnp.int32, (256, 128), 0)
     bin_slot = (
         (bin_row // 64) * 64 + ((bin_row // 4) % 4) * 16 + ((bin_row // 16) % 4) * 4 + bin_row % 4
     )
     wanted = bin_slot + 1
+    listed = got[pl.ds(16, 128, stride=17), :]
+    begin = 17 * lax.broadcasted_iota(jnp.int32, (128, 128), 0)
+    lane = lax.broadcasted_iota(jnp.int32, (128, 128), 1)
+    tile_of = begin // 128 + jnp.where(lane < begin % 128, 1, 0)
     fold = jnp.zeros((256, 128), jnp.float32)
-    for group in range(groups):
-        spot = pl.ds(group * 8, 8)
-        listed = jnp.sum(got[spot, 32:40, :].astype(jnp.int32), axis=0)
-        listed = jnp.broadcast_to(listed[None], (32, 8, 128)).reshape(256, 128)
-        hit = jnp.where(listed == wanted, 1.0, 0.0)
+    for tile in range(tiles):
+        low_group, high_group = (128 * tile) // 136, min((128 * tile + 127) // 136, 15)
+        spot = slice(8 * low_group, 8 * high_group + 8)
+        slots = jnp.sum(jnp.where(tile_of[spot] == tile, listed[spot], 0), axis=0, keepdims=True)
+        hit = jnp.where(wanted == slots, 1.0, 0.0)
         fold = fold + hit
-        pick[:, group * 128 : group * 128 + 128] = hit.astype(jnp.bfloat16)
-        for side in range(2):
-            code = got[spot, side * 16 : side * 16 + 16, :].reshape(128, 128).astype(jnp.int32)
+        spot = slice(128 * tile, 128 * tile + 128)
+        pick[:, spot] = hit.astype(jnp.bfloat16)
+        word = got[spot, :]
+        for side, code in enumerate((word >> 16, (word << 16) >> 16)):
             value = decode(code)
             high = value.astype(jnp.bfloat16)
             low = (value - high.astype(jnp.float32)).astype(jnp.bfloat16)
-            parts[group * 128 : group * 128 + 128, side * 128 : side * 128 + 128] = high
-            parts[group * 128 : group * 128 + 128, 256 + side * 128 : 384 + side * 128] = low
+            parts[spot, side * 128 : side * 128 + 128] = high
+            parts[spot, 256 + side * 128 : 384 + side * 128] = low
     stack = jnp.dot(pick[...], parts[...], preferred_element_type=jnp.float32)
     fold = jnp.sum(fold, axis=1, keepdims=True)
     merged = (base[...] + (stack[:, :256] + stack[:, 256:])) / (1.0 + fold)
@@ -164,7 +190,7 @@
 
 
 def sparse_kernel(
-    whole, own, before, after, words, words_back, codes, residual, field, first, recon, tail, turned, binned
+    whole, own, before, after, words, words_back, codes, residual, field, first, recon, tail, turned, binned, leave
 ):
     inline_at, xline_at = lax.axis_index("inline"), lax.axis_index("xline")
     inline_last = inline_at == lax.axis_size("inline") - 1
@@ -234,9 +260,14 @@
             if pair < 2:
                 field[block_row, 2 * pair + 1] = odd
 
+    stores = []
     for patch_row in range(4):
         found = first[patch_row] + step_size * correlated(field, patch_row, 4)
-        codes[patch_row] = shrink_codes(found).reshape(4, 64, 512)
+        first[patch_row] = shrink_codes(found)
+        stores.append(
+            pltpu.make_async_copy(first.at[patch_row], codes.at[patch_row], leave.at[patch_row])
+        )
+        stores[-1].start()
 
     lane = lax.broadcasted_iota(jnp.int32, (64, 128), 1) // 16
     for tile in range(2):
@@ -262,6 +293,8 @@
                     at = part * 64 + block_col * 16 + row * 4
                     to = (2 * tile + part) * 64 + row * 16 + block_col * 4
                     residual[to : to + 4, :] = flat[at : at + 4, :]
+    for store in stores:
+        store.wait()
 
 
 def body(
@@ -269,19 +302,33 @@
 ):
     trace_count, time_len = vintage_traces.shape
     device_count = lax.axis_size("inline") * lax.axis_size("xline")
+    send_rows = device_count * 17
     sent = call_kernel(
         pack_kernel,
-        jax.ShapeDtypeStruct((device_count, 40, 128), jnp.int16),
-        [],
-        [vintage_gains],
+        jax.ShapeDtypeStruct((send_rows, 128), jnp.int32),
+        pltpu.HBM,
         [
+            pltpu.SMEM(vintage_gains.shape, jnp.float32),
+            pltpu.VMEM(vintage_traces.shape, jnp.float32),
+            pltpu.VMEM((1, trace_count), jnp.int32),
+            pltpu.VMEM((1, trace_count), jnp.int32),
+            pltpu.VMEM((1, trace_count), jnp.int32),
+            pltpu.VMEM((send_rows, 128), jnp.int32),
+            pltpu.SemaphoreType.DMA((5,)),
+            pltpu.SemaphoreType.DMA((device_count // 16,)),
+        ],
+        pltpu.HBM,
+        [
+            vintage_gains,
             vintage_traces,
             dest_device.reshape(1, trace_count),
             dest_slot.reshape(1, trace_count),
             vintage_id.reshape(1, trace_count),
         ],
     )
-    got = lax.all_to_all(sent, ("inline", "xline"), split_axis=0, concat_axis=0, tiled=True)
+    got = lax.all_to_all(
+        sent.reshape(send_rows, 1, 128), ("inline", "xline"), split_axis=0, concat_axis=0, tiled=True
+    ).reshape(send_rows, 128)
     words = dictionary.reshape(2, 4, 2, 4, 2, 4, 512).transpose(0, 2, 4, 5, 1, 3, 6).reshape(512, 512)
     words_back = words.T
     base = (
@@ -296,12 +343,13 @@
             pair_shape(2, 2),
             pair_shape(2, 1),
         ),
+        (pltpu.VMEM,) * 4,
         [
-            pltpu.VMEM((256, device_count * 16), jnp.bfloat16),
-            pltpu.VMEM((device_count * 16, 512), jnp.bfloat16),
+            pltpu.VMEM((256, send_rows), jnp.bfloat16),
+            pltpu.VMEM((send_rows, 512), jnp.bfloat16),
             pltpu.VMEM((2, 256, 128), jnp.float32),
         ],
-        [],
+        pltpu.VMEM,
         [got, base],
     )
 
@@ -318,9 +366,10 @@
     codes, residual = call_kernel(
         sparse_kernel,
         (
-            jax.ShapeDtypeStruct((4, 4, 64, 512), jnp.float32),
+            jax.ShapeDtypeStruct((4, 256, 512), jnp.float32),
             jax.ShapeDtypeStruct((256, time_len), jnp.float32),
         ),
+        (pltpu.HBM, pltpu.VMEM),
         [
             pltpu.VMEM((7, 7, 64, 128), jnp.bfloat16),
             pltpu.VMEM((4, 256, 512), jnp.float32),
@@ -328,11 +377,12 @@
             pltpu.VMEM((5, 64, 128), jnp.float32),
             pltpu.VMEM((2, 256, 128), jnp.float32),
             pltpu.VMEM((4, 2, 64, 128), jnp.float32),
+            pltpu.SemaphoreType.DMA((4,)),
         ],
-        [],
+        pltpu.VMEM,
         [whole, own, before, after, words, words_back],
     )
-    return codes, residual.reshape(16, 16, time_len)
+    return codes.reshape(4, 4, 64, 512), residual.reshape(16, 16, time_len)
 
 
 def solution(mesh):

time: 70.7 us -> 68.7 us (0.972)
  waiting for transfers between devices: 31.8 us -> 29.7 us
    all_to_all x1, waiting for transfers between devices: 19.5 us -> 17.4 us  [body(): lax.all_to_all(sent.reshape(send_rows, 1, 128), ('inline', 'xline'), spli...]
where the time goes in v2:
time: 68.7 us; the launch traced here: 68.3 us
  waiting for transfers between devices  29.7 us (43%)
  starting transfers between devices  20.7 us (30%)
  Pallas kernels  12.2 us (18%)
  local copies, waits for them, and re-layouts  4.92 us (7%)
  between operations  0.81 us (1%)
    all_to_all x1, waiting for transfers between devices, body(): lax.all_to_all(sent.reshape(send_rows, 1, 128), ('inline', 'xline'), spli...  17.4 us
    ppermute x4, waiting for transfers between devices, along(): return lax.ppermute(block, axis, route)  12.3 us
    pallas_call x3, Pallas kernels, call_kernel(): pl.pallas_call(kernel, out_shape=out_shape, in_specs=[pl.BlockSpec(memory...  12.2 us
    ppermute x4, starting transfers between devices, along(): return lax.ppermute(block, axis, route)  10.4 us
    all_to_all x1, starting transfers between devices, body(): lax.all_to_all(sent.reshape(send_rows, 1, 128), ('inline', 'xline'), spli...  10.4 us
    unnamed x16, local copies, waits for them, and re-layouts  3.97 us
  transfers between devices with their start and end apart: 5, of which 3 were waited for; matrix products, arithmetic and copies ran while one was open for 1% of the time, Pallas kernels for 0%

profile of v2, /device:TPU:14, one launch (start us, length us, event | category | flops | bytes accessed | tf_op | source)
XLA Modules:
  0.0 68.3 jit_solution(18269895490264517228)
XLA Ops:
  0.6 0.0 copy-start
  0.6 1.2 %copy-done = f32[1024,256]{1,0:T(8,128)S(1)} copy-done((f32[1024,256]{1,0:T(8,128)S(1)}, f32[1024,256]{1,0:T(8,128)}, u32[]{:S(2)}) %copy-start) | copy-done | bytes 1048600
  1.9 0.0 copy-start.1
  1.9 0.7 %copy-done.1 = s32[1024,1]{0,1:T(1,128)S(1)} copy-done((s32[1024,1]{0,1:T(1,128)S(1)}, s32[1024,1]{0,1:T(1,128)}, u32[]{:S(2)}) %copy-start.1) | copy-done | bytes 4120
  2.5 0.0 copy-start.2
  2.5 0.7 %copy-done.2 = s32[1024]{0:T(1024)S(1)} copy-done((s32[1024]{0:T(1024)S(1)}, s32[1024]{0:T(1024)}, u32[]{:S(2)}) %copy-start.2) | copy-done | bytes 4120
  3.2 0.0 copy-start.3
  3.2 0.7 %copy-done.3 = s32[1024]{0:T(1024)S(1)} copy-done((s32[1024]{0:T(1024)S(1)}, s32[1024]{0:T(1024)}, u32[]{:S(2)}) %copy-start.3) | copy-done | bytes 4120
  3.9 0.0 copy-start.4
  3.9 0.7 copy-done.4
  4.6 4.6 %shard_map.86 = s32[2176,128]{1,0:T(8,128)} custom-call(f32[4]{0:T(128)S(1)} %copy-done.4, f32[1024,256]{1,0:T(8,128)S(1)} %copy-done, s32[1,1024]{1,0:T(1,128)S(1)} %bitcast.18, s32[1,1024]{1,0:T(1,128)S(1)} %bitcast.19, s32[1,1024]{1,0:T(1,128)S(1)} %bitcast.20), custom_call_target="tpu_custom_call" | custom-call | tf_op jit(solution)/shard_map/pallas_call | solution.py:23
  9.2 0.0 copy-start.6
  9.2 10.4 %all-to-all-start = ((s32[2176,1,128]{2,1,0:T(1,128)}), s32[2176,1,128]{2,1,0:T(1,128)S(1)}, u32[]{:S(2)}, u32[]{:S(2)}) async-start(s32[2176,1,128]{2,1,0:T(1,128)} %bitcast.4), calls=%async_computation | async-start | bytes 2228224 | tf_op jit(solution)/shard_map/all_to_all | solution.py:329
  19.6 0.0 copy-done.6
  19.6 0.1 reshape.42
  19.7 0.1 reshape.43.base
  19.8 17.4 %all-to-all-done = s32[2176,1,128]{2,1,0:T(1,128)S(1)} async-done(((s32[2176,1,128]{2,1,0:T(1,128)}), s32[2176,1,128]{2,1,0:T(1,128)S(1)}, u32[]{:S(2)}, u32[]{:S(2)}) %all-to-all-start) | async-done | bytes 1114144 | tf_op jit(solution)/shard_map/all_to_all | solution.py:329
  37.1 0.0 copy-start.5
  37.2 2.6 %shard_map.87 = (f32[4,2,64,128]{3,2,1,0:T(8,128)S(1)}, bf16[2,4,64,128]{3,2,1,0:T(8,128)(2,1)S(1)}, bf16[2,2,64,128]{3,2,1,0:T(8,128)(2,1)S(1)}, bf16[2,1,64,128]{3,2,1,0:T(8,128)(2,1)S(1)}) custom-call(s32[2176,128]{1,0:T(8,128)S(1)} %bitcast.16, f32[256,256]{1,0:T(8,128)S(1)} %reshape.43.base), custom_call_target="tpu_custom_call" | custom-call | tf_op jit(solution)/shard_map/pallas_call | solution.py:23
  39.8 4.1 %collective-permute-start = (bf16[2,1,64,128]{3,2,1,0:T(8,128)(2,1)S(1)}, bf16[2,1,64,128]{3,2,1,0:T(8,128)(2,1)S(1)}, u32[]{:S(2)}, u32[]{:S(2)}) collective-permute-start(bf16[2,1,64,128]{3,2,1,0:T(8,128)(2,1)S(1)} %get-tuple-element.9), channel_id=1, source_target_pairs={{0,16},{16,32},{32,48},{48,64},{64,80},{80,96},{96,112},{1,17},{17... | collective-permute-start | bytes 98312 | tf_op jit(solution)/shard_map/ppermute | solution.py:359
  43.9 1.9 %collective-permute-start.1 = (bf16[2,2,64,128]{3,2,1,0:T(8,128)(2,1)S(1)}, bf16[2,2,64,128]{3,2,1,0:T(8,128)(2,1)S(1)}, u32[]{:S(2)}, u32[]{:S(2)}) collective-permute-start(bf16[2,2,64,128]{3,2,1,0:T(8,128)(2,1)S(1)} %get-tuple-element.11), channel_id=1, source_target_pairs={{16,0},{32,16},{48,32},{64,48},{80,64},{96,80},{112,96},{17,1},{33... | collective-permute-start | bytes 196616 | tf_op jit(solution)/shard_map/ppermute | solution.py:359
  45.8 0.0 collective-permute-done
  45.9 8.5 %collective-permute-done.1 = bf16[2,2,64,128]{3,2,1,0:T(8,128)(2,1)S(1)} collective-permute-done((bf16[2,2,64,128]{3,2,1,0:T(8,128)(2,1)S(1)}, bf16[2,2,64,128]{3,2,1,0:T(8,128)(2,1)S(1)}, u32[]{:S(2)}, u32[]{:S(2)}) %collective-permute-start.1) | collective-permute-done | bytes 65568 | tf_op jit(solution)/shard_map/ppermute | solution.py:359
  54.4 1.9 %collective-permute-start.3 = (bf16[1,7,64,128]{3,2,1,0:T(8,128)(2,1)S(1)}, bf16[1,7,64,128]{3,2,1,0:T(8,128)(2,1)S(1)}, u32[]{:S(2)}, u32[]{:S(2)}) collective-permute-start(bf16[1,7,64,128]{3,2,1,0:T(8,128)(2,1)S(1)} %get-tuple-element.14), channel_id=1, source_target_pairs={{1,0},{2,1},{3,2},{4,3},{5,4},{6,5},{7,6},{8,7},{9,8},{10,9},{11,1... | collective-permute-start | bytes 344072 | tf_op jit(solution)/shard_map/ppermute | solution.py:359
  56.3 2.4 %collective-permute-start.2 = (bf16[1,7,64,128]{3,2,1,0:T(8,128)(2,1)S(1)}, bf16[1,7,64,128]{3,2,1,0:T(8,128)(2,1)S(1)}, u32[]{:S(2)}, u32[]{:S(2)}) collective-permute-start(bf16[1,7,64,128]{3,2,1,0:T(8,128)(2,1)S(1)} %get-tuple-element.15), channel_id=1, source_target_pairs={{0,1},{1,2},{2,3},{3,4},{4,5},{5,6},{6,7},{7,8},{8,9},{9,10},{10,1... | collective-permute-start | bytes 344072 | tf_op jit(solution)/shard_map/ppermute | solution.py:359
  58.7 0.0 copy-done.5
  58.7 0.1 reshape.44
  58.9 0.3 copy.21
  59.2 0.1 reshape.45.words
  59.3 0.2 copy.18
  59.5 0.0 collective-permute-done.3.after
  59.5 3.8 %collective-permute-done.2.before = bf16[1,7,64,128]{3,2,1,0:T(8,128)(2,1)S(1)} collective-permute-done((bf16[1,7,64,128]{3,2,1,0:T(8,128)(2,1)S(1)}, bf16[1,7,64,128]{3,2,1,0:T(8,128)(2,1)S(1)}, u32[]{:S(2)}, u32[]{:S(2)}) %collective-permute-start.2) | collective-permute-done | bytes 114720 | tf_op jit(solution)/shard_map/ppermute | solution.py:359
  63.3 5.0 %shard_map.88 = (f32[4,256,512]{2,1,0:T(8,128)}, f32[256,256]{1,0:T(8,128)}) custom-call(f32[4,2,64,128]{3,2,1,0:T(8,128)S(1)} %get-tuple-element.8.whole, bf16[2,7,64,128]{3,2,1,0:T(8,128)(2,1)S(1)} %constant_dynamic-update-slice_fusion.own, bf16[1,7,64,128]{3,2,1,0:T(8,128)(2,1)S(1)} %collective-permute-done.2.before, ...), custom_call_target="tpu_custom_call" | custom-call | tf_op jit(solution)/shard_map/pallas_call | solution.py:23
  (5 shorter events, 0.1 us)
Async XLA Ops:
  0.6 1.2 %copy-start = (f32[1024,256]{1,0:T(8,128)S(1)}, f32[1024,256]{1,0:T(8,128)}, u32[]{:S(2)}) copy-start(f32[1024,256]{1,0:T(8,128)} %traces_in.1) | copy-start | bytes 3145732
  1.9 0.7 %copy-start.1 = (s32[1024,1]{0,1:T(1,128)S(1)}, s32[1024,1]{0,1:T(1,128)}, u32[]{:S(2)}) copy-start(s32[1024,1]{0,1:T(1,128)} %param.9) | copy-start | bytes 12292
  2.5 0.7 %copy-start.2 = (s32[1024]{0:T(1024)S(1)}, s32[1024]{0:T(1024)}, u32[]{:S(2)}) copy-start(s32[1024]{0:T(1024)} %param.10) | copy-start | bytes 12292
  3.2 0.7 %copy-start.3 = (s32[1024]{0:T(1024)S(1)}, s32[1024]{0:T(1024)}, u32[]{:S(2)}) copy-start(s32[1024]{0:T(1024)} %param.11) | copy-start | bytes 12292
  3.9 0.7 copy-start.4
  9.2 10.4 %copy-start.6 = (f32[16,16,256]{2,1,0:T(8,128)S(1)}, f32[16,16,256]{2,1,0:T(8,128)}, u32[]{:S(2)}) copy-start(f32[16,16,256]{2,1,0:T(8,128)} %param.7) | copy-start | bytes 786436
  9.2 27.9 %all-to-all-start = ((s32[2176,1,128]{2,1,0:T(1,128)}), s32[2176,1,128]{2,1,0:T(1,128)S(1)}, u32[]{:S(2)}, u32[]{:S(2)}) async-start(s32[2176,1,128]{2,1,0:T(1,128)} %bitcast.4), calls=%async_computation | async-start | bytes 2228224 | tf_op jit(solution)/shard_map/all_to_all | solution.py:329
  37.1 21.6 %copy-start.5 = (bf16[512,512]{1,0:T(8,128)(2,1)S(1)}, bf16[512,512]{1,0:T(8,128)(2,1)}, u32[]{:S(2)}) copy-start(bf16[512,512]{1,0:T(8,128)(2,1)} %param.13) | copy-start | bytes 1572868
  39.8 6.1 %collective-permute-start = (bf16[2,1,64,128]{3,2,1,0:T(8,128)(2,1)S(1)}, bf16[2,1,64,128]{3,2,1,0:T(8,128)(2,1)S(1)}, u32[]{:S(2)}, u32[]{:S(2)}) collective-permute-start(bf16[2,1,64,128]{3,2,1,0:T(8,128)(2,1)S(1)} %get-tuple-element.9), channel_id=1, source_target_pairs={{0,16},{16,32},{32,48},{48,64},{64,80},{80,96},{96,112},{1,17},{17... | collective-permute-start | bytes 98312 | tf_op jit(solution)/shard_map/ppermute | solution.py:359
  43.9 10.5 %collective-permute-start.1 = (bf16[2,2,64,128]{3,2,1,0:T(8,128)(2,1)S(1)}, bf16[2,2,64,128]{3,2,1,0:T(8,128)(2,1)S(1)}, u32[]{:S(2)}, u32[]{:S(2)}) collective-permute-start(bf16[2,2,64,128]{3,2,1,0:T(8,128)(2,1)S(1)} %get-tuple-element.11), channel_id=1, source_target_pairs={{16,0},{32,16},{48,32},{64,48},{80,64},{96,80},{112,96},{17,1},{33... | collective-permute-start | bytes 196616 | tf_op jit(solution)/shard_map/ppermute | solution.py:359
  54.4 5.1 %collective-permute-start.3 = (bf16[1,7,64,128]{3,2,1,0:T(8,128)(2,1)S(1)}, bf16[1,7,64,128]{3,2,1,0:T(8,128)(2,1)S(1)}, u32[]{:S(2)}, u32[]{:S(2)}) collective-permute-start(bf16[1,7,64,128]{3,2,1,0:T(8,128)(2,1)S(1)} %get-tuple-element.14), channel_id=1, source_target_pairs={{1,0},{2,1},{3,2},{4,3},{5,4},{6,5},{7,6},{8,7},{9,8},{10,9},{11,1... | collective-permute-start | bytes 344072 | tf_op jit(solution)/shard_map/ppermute | solution.py:359
  56.3 7.0 %collective-permute-start.2 = (bf16[1,7,64,128]{3,2,1,0:T(8,128)(2,1)S(1)}, bf16[1,7,64,128]{3,2,1,0:T(8,128)(2,1)S(1)}, u32[]{:S(2)}, u32[]{:S(2)}) collective-permute-start(bf16[1,7,64,128]{3,2,1,0:T(8,128)(2,1)S(1)} %get-tuple-element.15), channel_id=1, source_target_pairs={{0,1},{1,2},{2,3},{3,4},{4,5},{5,6},{6,7},{7,8},{8,9},{9,10},{10,1... | collective-permute-start | bytes 344072 | tf_op jit(solution)/shard_map/ppermute | solution.py:359

commit v3 on v2

--- a/solution.py
+++ b/solution.py
@@ -13,20 +13,21 @@
 code_top = 32767.0
 log_top = math.log2(12.0)
 vmem_bytes = 48 * 1024 * 1024
+all_vmem_bytes = 64 * 1024 * 1024
 
 
 def shrink_codes(values):
     return values - jnp.clip(values, -threshold, threshold)
 
 
-def call_kernel(kernel, out_shape, out_spaces, scratch, in_space, inputs):
+def call_kernel(kernel, out_shape, out_spaces, scratch, in_space, inputs, vmem_limit=vmem_bytes):
     return pl.pallas_call(
         kernel,
         out_shape=out_shape,
         in_specs=[pl.BlockSpec(memory_space=in_space)] * len(inputs),
         out_specs=jax.tree.map(lambda space: pl.BlockSpec(memory_space=space), out_spaces),
         scratch_shapes=scratch,
-        compiler_params=pltpu.CompilerParams(vmem_limit_bytes=vmem_bytes),
+        compiler_params=pltpu.CompilerParams(vmem_limit_bytes=vmem_limit),
     )(*inputs)
 
 
@@ -119,7 +120,7 @@
         store.wait()
 
 
-def merge_kernel(got, base, whole, half, upper, lower, pick, parts, turned):
+def merge_kernel(got, base, whole, half, to_even, to_odd, pick, parts, turned):
     tiles = got.shape[0] // 128
     bin_row = lax.broadcasted_iota(jnp.int32, (256, 128), 0)
     bin_slot = (
@@ -168,10 +169,22 @@
                 whole[block_row, pair] = made
                 made = made.astype(jnp.bfloat16)
                 half[pair, block_row] = made
-                if block_row < 2:
-                    upper[pair, block_row] = made
-                if block_row == 3:
-                    lower[pair, 0] = made
+    odd_device = lax.rem(lax.axis_index("inline"), 2)
+    to_even[...] = half[:, pl.ds(2 - 2 * odd_device, 2)]
+    to_odd[...] = half[:, pl.ds(2 * odd_device, 2)]
+
+
+def assemble_kernel(half, from_even, from_odd, to_even, to_odd):
+    inline_at = lax.axis_index("inline")
+    odd_row = lax.rem(inline_at, 2) == 1
+    odd_col = lax.rem(lax.axis_index("xline"), 2)
+    for target, pair in ((to_even, 1 - odd_col), (to_odd, odd_col)):
+        above = jnp.where(odd_row, from_even[pair, 1], from_odd[pair, 1])
+        target[0] = jnp.where(inline_at == 0, jnp.zeros_like(above), above)
+        target[1:5] = half[pair]
+        below = jnp.where(odd_row, from_odd[pair], from_even[pair])
+        last = inline_at == lax.axis_size("inline") - 1
+        target[5:7] = jnp.where(last, jnp.zeros_like(below), below)
 
 
 def time_rolled(values, distance):
@@ -190,7 +203,7 @@
 
 
 def sparse_kernel(
-    whole, own, before, after, words, words_back, codes, residual, field, first, recon, tail, turned, binned, leave
+    whole, own_even, own_odd, from_even, from_odd, words, words_back, codes, residual, field, first, recon, tail, turned, binned, leave
 ):
     inline_at, xline_at = lax.axis_index("inline"), lax.axis_index("xline")
     inline_last = inline_at == lax.axis_size("inline") - 1
@@ -200,10 +213,18 @@
     not_bottom = jnp.where(inline_last, 0.0, 1.0)
     not_right = jnp.where(xline_last, 0.0, 1.0)
 
-    sources = [before.at[0], own.at[0], own.at[1], after.at[0]]
+    odd_device = lax.rem(xline_at, 2) == 1
+    sources = ((from_odd, from_even), (own_odd, own_even), (own_even, own_odd), (from_even, from_odd))
+    edges = (not_left, None, None, not_right)
+
+    def loaded(pair, block_row):
+        if_even, if_odd = sources[pair]
+        both = jnp.where(odd_device, if_odd[block_row], if_even[block_row]).astype(jnp.float32)
+        return both if edges[pair] is None else both * edges[pair]
+
     for block_row in range(7):
         for pair in range(4):
-            even, odd = widened(sources[pair][block_row].astype(jnp.float32))
+            even, odd = widened(loaded(pair, block_row))
             if pair > 0:
                 field[block_row, 2 * pair - 1] = even
             if pair < 4:
@@ -250,9 +271,9 @@
                 whole_rest = rest
                 binned[block_row, pair] = whole_rest
             elif pair < 2:
-                rest = (own[pair, 5].astype(jnp.float32) - rebuilt) * not_bottom
+                rest = (loaded(pair + 1, 5) - rebuilt) * not_bottom
             else:
-                rest = (after[0, block_row + 1].astype(jnp.float32) - rebuilt) * not_right
+                rest = (loaded(3, block_row + 1) - rebuilt) * not_right
                 if block_row == 4:
                     rest = rest * not_bottom
             even, odd = widened(rest)
@@ -325,6 +346,7 @@
             dest_slot.reshape(1, trace_count),
             vintage_id.reshape(1, trace_count),
         ],
+        all_vmem_bytes,
     )
     got = lax.all_to_all(
         sent.reshape(send_rows, 1, 128), ("inline", "xline"), split_axis=0, concat_axis=0, tiled=True
@@ -335,13 +357,13 @@
         base_volume.reshape(4, 4, 4, 4, time_len).transpose(0, 2, 1, 3, 4).reshape(256, time_len)
     )
     pair_shape = lambda *lead: jax.ShapeDtypeStruct(lead + (64, 128), jnp.bfloat16)
-    whole, half, upper, lower = call_kernel(
+    whole, half, to_even, to_odd = call_kernel(
         merge_kernel,
         (
             jax.ShapeDtypeStruct((4, 2, 64, 128), jnp.float32),
             pair_shape(2, 4),
             pair_shape(2, 2),
-            pair_shape(2, 1),
+            pair_shape(2, 2),
         ),
         (pltpu.VMEM,) * 4,
         [
@@ -353,16 +375,21 @@
         [got, base],
     )
 
-    def along(block, axis, distance):
-        devices = range(lax.axis_size(axis))
-        route = [(i - distance, i) for i in devices if i - distance in devices]
-        return lax.ppermute(block, axis, route)
-
-    from_below = along(upper, "inline", -1)
-    from_above = along(lower, "inline", 1)
-    own = jnp.concatenate([from_above, half, from_below], axis=1)
-    after = along(own[0:1], "xline", -1)
-    before = along(own[1:2], "xline", 1)
+    def swapped(block, axis, odd_pairs):
+        count = lax.axis_size(axis)
+        partner = [(i + 1 if i % 2 == odd_pairs else i - 1) % count for i in range(count)]
+        return lax.ppermute(block, axis, list(enumerate(partner)))
+
+    from_even, from_odd = swapped(to_even, "inline", 0), swapped(to_odd, "inline", 1)
+    own_even, own_odd = call_kernel(
+        assemble_kernel,
+        (pair_shape(7), pair_shape(7)),
+        (pltpu.VMEM,) * 2,
+        [],
+        pltpu.VMEM,
+        [half, from_even, from_odd],
+    )
+    from_even, from_odd = swapped(own_even, "xline", 0), swapped(own_odd, "xline", 1)
     codes, residual = call_kernel(
         sparse_kernel,
         (
@@ -380,7 +407,7 @@
             pltpu.SemaphoreType.DMA((4,)),
         ],
         pltpu.VMEM,
-        [whole, own, before, after, words, words_back],
+        [whole, own_even, own_odd, from_even, from_odd, words, words_back],
     )
     return codes.reshape(4, 4, 64, 512), residual.reshape(16, 16, time_len)
 

time: 68.7 us -> 59.1 us (0.86)
  the two profiles are of different devices: /device:TPU:14 before, /device:TPU:0 now
where the time goes in v3:
time: 59.1 us; the launch traced here: 58.9 us
  waiting for transfers between devices  29.5 us (50%)
  starting transfers between devices  14.8 us (25%)
  Pallas kernels  12.9 us (22%)
  local copies, waits for them, and re-layouts  0.93 us (2%)
  between operations  0.75 us (1%)
    all_to_all x1, waiting for transfers between devices, body(): lax.all_to_all(sent.reshape(send_rows, 1, 128), ('inline', 'xline'), spli...  19.4 us
    pallas_call x4, Pallas kernels, call_kernel(): pl.pallas_call(kernel, out_shape=out_shape, in_specs=[pl.BlockSpec(memory...  12.9 us
    all_to_all x1, starting transfers between devices, body(): lax.all_to_all(sent.reshape(send_rows, 1, 128), ('inline', 'xline'), spli...  11.1 us
    ppermute x4, waiting for transfers between devices, swapped(): return lax.ppermute(block, axis, list(enumerate(partner)))  10.1 us
    ppermute x4, starting transfers between devices, swapped(): return lax.ppermute(block, axis, list(enumerate(partner)))  3.7 us
  transfers between devices with their start and end apart: 5, of which 4 were waited for; matrix products, arithmetic and copies ran while one was open for 2% of the time, Pallas kernels for 0%

profile of v3, /device:TPU:0, one launch (start us, length us, event | category | flops | bytes accessed | tf_op | source)
XLA Modules:
  0.0 58.9 jit_solution(5039987350076985192)
XLA Ops:
  0.6 5.2 %shard_map.86 = s32[2176,128]{1,0:T(8,128)} custom-call(f32[4]{0:T(128)} %gains_in.1, f32[1024,256]{1,0:T(8,128)} %traces_in.1, s32[1,1024]{1,0:T(1,128)} %bitcast.21, s32[1,1024]{1,0:T(1,128)} %bitcast.22, s32[1,1024]{1,0:T(1,128)} %bitcast.23), custom_call_target="tpu_custom_call" | custom-call | tf_op jit(solution)/shard_map/pallas_call | solution.py:24
  5.9 0.0 copy-start.1
  5.9 11.1 %all-to-all-start = ((s32[2176,1,128]{2,1,0:T(1,128)}), s32[2176,1,128]{2,1,0:T(1,128)S(1)}, u32[]{:S(2)}, u32[]{:S(2)}) async-start(s32[2176,1,128]{2,1,0:T(1,128)} %bitcast.18), calls=%async_computation | async-start | bytes 2228224 | tf_op jit(solution)/shard_map/all_to_all | solution.py:351
  17.0 0.0 copy-done.1
  17.0 0.1 reshape.42
  17.1 0.0 copy-start
  17.2 0.1 reshape.43.base
  17.3 19.4 %all-to-all-done = s32[2176,1,128]{2,1,0:T(1,128)S(1)} async-done(((s32[2176,1,128]{2,1,0:T(1,128)}), s32[2176,1,128]{2,1,0:T(1,128)S(1)}, u32[]{:S(2)}, u32[]{:S(2)}) %all-to-all-start) | async-done | bytes 1114144 | tf_op jit(solution)/shard_map/all_to_all | solution.py:351
  36.7 2.6 %shard_map.87 = (f32[4,2,64,128]{3,2,1,0:T(8,128)S(1)}, bf16[2,4,64,128]{3,2,1,0:T(8,128)(2,1)S(1)}, bf16[2,2,64,128]{3,2,1,0:T(8,128)(2,1)S(1)}, bf16[2,2,64,128]{3,2,1,0:T(8,128)(2,1)S(1)}) custom-call(s32[2176,128]{1,0:T(8,128)S(1)} %bitcast.16, f32[256,256]{1,0:T(8,128)S(1)} %reshape.43.base), custom_call_target="tpu_custom_call" | custom-call | tf_op jit(solution)/shard_map/pallas_call | solution.py:24
  39.3 0.1 collective-permute-start
  39.4 2.0 %collective-permute-start.1 = (bf16[2,2,64,128]{3,2,1,0:T(8,128)(2,1)S(1)}, bf16[2,2,64,128]{3,2,1,0:T(8,128)(2,1)S(1)}, u32[]{:S(2)}, u32[]{:S(2)}) collective-permute-start(bf16[2,2,64,128]{3,2,1,0:T(8,128)(2,1)S(1)} %get-tuple-element.13), channel_id=1, source_target_pairs={{0,112},{16,32},{32,16},{48,64},{64,48},{80,96},{96,80},{112,0},{1... | collective-permute-start | bytes 196616 | tf_op jit(solution)/shard_map/ppermute | solution.py:381
  41.4 2.3 %collective-permute-done.from_even = bf16[2,2,64,128]{3,2,1,0:T(8,128)(2,1)S(1)} collective-permute-done((bf16[2,2,64,128]{3,2,1,0:T(8,128)(2,1)S(1)}, bf16[2,2,64,128]{3,2,1,0:T(8,128)(2,1)S(1)}, u32[]{:S(2)}, u32[]{:S(2)}) %collective-permute-start) | collective-permute-done | bytes 65568 | tf_op jit(solution)/shard_map/ppermute | solution.py:381
  43.6 3.7 %collective-permute-done.1.from_odd = bf16[2,2,64,128]{3,2,1,0:T(8,128)(2,1)S(1)} collective-permute-done((bf16[2,2,64,128]{3,2,1,0:T(8,128)(2,1)S(1)}, bf16[2,2,64,128]{3,2,1,0:T(8,128)(2,1)S(1)}, u32[]{:S(2)}, u32[]{:S(2)}) %collective-permute-start.1) | collective-permute-done | bytes 65568 | tf_op jit(solution)/shard_map/ppermute | solution.py:381
  47.4 0.1 collective-permute-start.2
  47.5 1.5 %collective-permute-start.3 = (bf16[7,64,128]{2,1,0:T(8,128)(2,1)S(1)}, bf16[7,64,128]{2,1,0:T(8,128)(2,1)S(1)}, u32[]{:S(2)}, u32[]{:S(2)}) collective-permute-start(bf16[7,64,128]{2,1,0:T(8,128)(2,1)S(1)} %get-tuple-element.15.own_odd), channel_id=1, source_target_pairs={{0,15},{1,2},{2,1},{3,4},{4,3},{5,6},{6,5},{7,8},{8,7},{9,10},{10,... | collective-permute-start | bytes 344072 | tf_op jit(solution)/shard_map/ppermute | solution.py:381
  49.0 0.0 copy-done
  49.0 0.1 reshape.44
  49.1 0.3 copy.21
  49.4 0.1 reshape.45.words
  49.6 0.2 copy.18
  49.8 0.0 collective-permute-done.2.from_even
  49.8 4.1 %collective-permute-done.3.from_odd = bf16[7,64,128]{2,1,0:T(8,128)(2,1)S(1)} collective-permute-done((bf16[7,64,128]{2,1,0:T(8,128)(2,1)S(1)}, bf16[7,64,128]{2,1,0:T(8,128)(2,1)S(1)}, u32[]{:S(2)}, u32[]{:S(2)}) %collective-permute-start.3) | collective-permute-done | bytes 114720 | tf_op jit(solution)/shard_map/ppermute | solution.py:381
  53.9 5.0 %shard_map.89 = (f32[4,256,512]{2,1,0:T(8,128)}, f32[256,256]{1,0:T(8,128)}) custom-call(f32[4,2,64,128]{3,2,1,0:T(8,128)S(1)} %get-tuple-element.10.whole, bf16[7,64,128]{2,1,0:T(8,128)(2,1)S(1)} %get-tuple-element.14.own_even, bf16[7,64,128]{2,1,0:T(8,128)(2,1)S(1)} %get-tuple-element.15.own_odd, bf16[7,64,128]{2,1,0:T(8,128)(2,1)S(1)} %collective-permute-done.2.from_even, ...), custom_call_target="tpu_custom_call" | custom-call | tf_op jit(solution)/shard_map/pallas_call | solution.py:24
  (2 shorter events, 0.1 us)
Async XLA Ops:
  5.9 11.2 %copy-start.1 = (f32[16,16,256]{2,1,0:T(8,128)S(1)}, f32[16,16,256]{2,1,0:T(8,128)}, u32[]{:S(2)}) copy-start(f32[16,16,256]{2,1,0:T(8,128)} %param.7) | copy-start | bytes 786436
  5.9 30.8 %all-to-all-start = ((s32[2176,1,128]{2,1,0:T(1,128)}), s32[2176,1,128]{2,1,0:T(1,128)S(1)}, u32[]{:S(2)}, u32[]{:S(2)}) async-start(s32[2176,1,128]{2,1,0:T(1,128)} %bitcast.18), calls=%async_computation | async-start | bytes 2228224 | tf_op jit(solution)/shard_map/all_to_all | solution.py:351
  17.1 31.9 %copy-start = (bf16[512,512]{1,0:T(8,128)(2,1)S(1)}, bf16[512,512]{1,0:T(8,128)(2,1)}, u32[]{:S(2)}) copy-start(bf16[512,512]{1,0:T(8,128)(2,1)} %param.13) | copy-start | bytes 1572868
  39.3 4.3 %collective-permute-start = (bf16[2,2,64,128]{3,2,1,0:T(8,128)(2,1)S(1)}, bf16[2,2,64,128]{3,2,1,0:T(8,128)(2,1)S(1)}, u32[]{:S(2)}, u32[]{:S(2)}) collective-permute-start(bf16[2,2,64,128]{3,2,1,0:T(8,128)(2,1)S(1)} %get-tuple-element.12), channel_id=1, source_target_pairs={{0,16},{16,0},{32,48},{48,32},{64,80},{80,64},{96,112},{112,96},{1... | collective-permute-start | bytes 196616 | tf_op jit(solution)/shard_map/ppermute | solution.py:381
  39.4 8.0 %collective-permute-start.1 = (bf16[2,2,64,128]{3,2,1,0:T(8,128)(2,1)S(1)}, bf16[2,2,64,128]{3,2,1,0:T(8,128)(2,1)S(1)}, u32[]{:S(2)}, u32[]{:S(2)}) collective-permute-start(bf16[2,2,64,128]{3,2,1,0:T(8,128)(2,1)S(1)} %get-tuple-element.13), channel_id=1, source_target_pairs={{0,112},{16,32},{32,16},{48,64},{64,48},{80,96},{96,80},{112,0},{1... | collective-permute-start | bytes 196616 | tf_op jit(solution)/shard_map/ppermute | solution.py:381
  47.4 2.4 %collective-permute-start.2 = (bf16[7,64,128]{2,1,0:T(8,128)(2,1)S(1)}, bf16[7,64,128]{2,1,0:T(8,128)(2,1)S(1)}, u32[]{:S(2)}, u32[]{:S(2)}) collective-permute-start(bf16[7,64,128]{2,1,0:T(8,128)(2,1)S(1)} %get-tuple-element.14.own_even), channel_id=1, source_target_pairs={{0,1},{1,0},{2,3},{3,2},{4,5},{5,4},{6,7},{7,6},{8,9},{9,8},{10,11... | collective-permute-start | bytes 344072 | tf_op jit(solution)/shard_map/ppermute | solution.py:381
  47.5 6.4 %collective-permute-start.3 = (bf16[7,64,128]{2,1,0:T(8,128)(2,1)S(1)}, bf16[7,64,128]{2,1,0:T(8,128)(2,1)S(1)}, u32[]{:S(2)}, u32[]{:S(2)}) collective-permute-start(bf16[7,64,128]{2,1,0:T(8,128)(2,1)S(1)} %get-tuple-element.15.own_odd), channel_id=1, source_target_pairs={{0,15},{1,2},{2,1},{3,4},{4,3},{5,6},{6,5},{7,8},{8,7},{9,10},{10,... | collective-permute-start | bytes 344072 | tf_op jit(solution)/shard_map/ppermute | solution.py:381

commit v4 on v3

--- a/solution.py
+++ b/solution.py
@@ -20,13 +20,14 @@
     return values - jnp.clip(values, -threshold, threshold)
 
 
-def call_kernel(kernel, out_shape, out_spaces, scratch, in_space, inputs, vmem_limit=vmem_bytes):
+def call_kernel(kernel, out_shape, out_spaces, scratch, in_space, inputs, vmem_limit=vmem_bytes, cost=None):
     return pl.pallas_call(
         kernel,
         out_shape=out_shape,
         in_specs=[pl.BlockSpec(memory_space=in_space)] * len(inputs),
         out_specs=jax.tree.map(lambda space: pl.BlockSpec(memory_space=space), out_spaces),
         scratch_shapes=scratch,
+        cost_estimate=cost,
         compiler_params=pltpu.CompilerParams(vmem_limit_bytes=vmem_limit),
     )(*inputs)
 
@@ -202,9 +203,99 @@
     return even.astype(jnp.bfloat16), odd.astype(jnp.bfloat16)
 
 
+def correlated(near, far, words, first_row, count):
+    lhs = [
+        source[first_row + shift : first_row + shift + count].reshape(count * 64, 128)
+        for shift in (0, 1)
+        for source in (near, far)
+    ]
+    return jnp.dot(jnp.concatenate(lhs, axis=1), words[...], preferred_element_type=jnp.float32)
+
+
+def given_back(found, words_back, sides):
+    given = {}
+    for side in sides:
+        for shift in (0, 1):
+            at = 256 * shift + 128 * side
+            given[shift, side] = at
+    columns = {}
+    if len(sides) == 2:
+        full = jnp.dot(found, words_back[...], preferred_element_type=jnp.float32)
+        for key, at in given.items():
+            columns[key] = full[:, at : at + 128].reshape(6, 64, 128)
+    else:
+        picked = jnp.concatenate([words_back[:, at : at + 128] for at in given.values()], axis=1)
+        full = jnp.dot(found, picked, preferred_element_type=jnp.float32)
+        for number, key in enumerate(given):
+            columns[key] = full[:, 128 * number : 128 * number + 128].reshape(6, 64, 128)
+    return [columns[0, side][1:6] + columns[1, side][0:5] for side in sides]
+
+
+def rebuilt_half(given, odd):
+    moved = pltpu.roll(given, 64, 1)
+    return moved + time_rolled(given, 1) if odd else given + time_rolled(moved, 1)
+
+
+def widened_half(block, odd):
+    left = lax.broadcasted_iota(jnp.int32, block.shape, 1) < 64
+    later = time_rolled(block, -1)
+    if odd:
+        return jnp.where(left, pltpu.roll(block, 64, 1), later).astype(jnp.bfloat16)
+    return jnp.where(left, block, pltpu.roll(later, 64, 1)).astype(jnp.bfloat16)
+
+
+def first_codes(near, far, words, not_top):
+    found = shrink_codes(step_size * correlated(near, far, words, 0, 6))
+    return found[64:320], jnp.concatenate([found[:64] * not_top, found[64:]], axis=0)
+
+
+def last_codes(before, near, far, words):
+    found = before + step_size * correlated(near, far, words, 0, 4)
+    return shrink_codes(found).reshape(4, 64, 512)
+
+
+def inner_kernel(whole, own_even, own_odd, words, words_back, field, first, recon, rests, later, made_codes):
+    inline_at = lax.axis_index("inline")
+    not_top = jnp.where(inline_at == 0, 0.0, 1.0)
+    not_bottom = jnp.where(inline_at == lax.axis_size("inline") - 1, 0.0, 1.0)
+    odd_device = lax.rem(lax.axis_index("xline"), 2) == 1
+
+    def loaded(pair, block_row):
+        if_even, if_odd = ((own_odd, own_even), (own_even, own_odd))[pair]
+        return jnp.where(odd_device, if_odd[block_row], if_even[block_row]).astype(jnp.float32)
+
+    for pair in range(2):
+        for block_row in range(7):
+            even, odd = widened(loaded(pair, block_row))
+            field[2 * pair, block_row] = even
+            field[2 * pair + 1, block_row] = odd
+    kept, found = zip(
+        *(first_codes(field.at[at], field.at[at + 1], words, not_top) for at in range(3))
+    )
+    given = [given_back(part.astype(jnp.bfloat16), words_back, (0, 1)) for part in found]
+    recon[0] = given[0][0]
+    recon[1] = given[2][1]
+    for column in (1, 2):
+        pair, odd = column // 2, column % 2
+        for block_row in range(5):
+            rebuilt = rebuilt_half(given[column][0][block_row] + given[column - 1][1][block_row], odd)
+            if block_row < 4:
+                rest = whole[block_row, pair] - rebuilt
+                rests[column - 1, block_row] = rest
+            else:
+                rest = (loaded(pair, 5) - rebuilt) * not_bottom
+            later[column - 1, block_row] = widened_half(rest, odd)
+    first[0] = kept[0]
+    first[1] = kept[2]
+    made_codes[...] = last_codes(kept[1], later.at[0], later.at[1], words)
+
+
 def sparse_kernel(
-    whole, own_even, own_odd, from_even, from_odd, words, words_back, codes, residual, field, first, recon, tail, turned, binned, leave
+    whole, own_even, own_odd, from_even, from_odd, inner, first_inner, recon_inner, rests, later_inner,
+    codes_inner, words, words_back, codes, residual, outer, later, turned, binned, made_codes, flat_rest, leave
 ):
+    stores = [pltpu.make_async_copy(codes_inner, codes.at[:, 1], leave.at[0])]
+    stores[0].start()
     inline_at, xline_at = lax.axis_index("inline"), lax.axis_index("xline")
     inline_last = inline_at == lax.axis_size("inline") - 1
     xline_last = xline_at == lax.axis_size("xline") - 1
@@ -222,74 +313,55 @@
         both = jnp.where(odd_device, if_odd[block_row], if_even[block_row]).astype(jnp.float32)
         return both if edges[pair] is None else both * edges[pair]
 
+    def leaving(column, made):
+        made_codes[len(stores) - 1] = made
+        for part in range(2 if column == 3 else 1):
+            rows = pl.ds(2 * part, 2) if column == 3 else pl.ds(0, 4)
+            stores.append(
+                pltpu.make_async_copy(
+                    made_codes.at[len(stores) - 1 - part, rows],
+                    codes.at[rows, column],
+                    leave.at[len(stores)],
+                )
+            )
+            stores[-1].start()
+
+    def rest_of(column, given, spot):
+        pair, odd = column // 2, column % 2
+        for block_row in range(5):
+            rebuilt = rebuilt_half(given[block_row], odd)
+            if column == 4:
+                rest = (loaded(3, block_row + 1) - rebuilt) * not_right
+            elif block_row < 4:
+                rest = whole[block_row, pair] - rebuilt
+                binned[pair, block_row] = rest
+            else:
+                rest = loaded(pair + 1, 5) - rebuilt
+            if block_row == 4:
+                rest = rest * not_bottom
+            later[spot, block_row] = widened_half(rest, odd)
+
     for block_row in range(7):
-        for pair in range(4):
-            even, odd = widened(loaded(pair, block_row))
-            if pair > 0:
-                field[block_row, 2 * pair - 1] = even
-            if pair < 4:
-                field[block_row, 2 * pair] = odd
-
-    def correlated(source, patch_row, count):
-        lhs = [
-            source[patch_row + shift_a, shift_b : shift_b + count].reshape(count * 64, 128)
-            for shift_a in (0, 1)
-            for shift_b in (0, 1)
-        ]
-        return jnp.dot(
-            jnp.concatenate(lhs, axis=1), words[...], preferred_element_type=jnp.float32
-        )
-
-    for patch_row in range(6):
-        found = shrink_codes(step_size * correlated(field, patch_row, 6))
-        if 1 <= patch_row <= 4:
-            first[patch_row - 1] = found[64:320]
-        if patch_row == 0:
-            found = found * not_top
-        found = jnp.concatenate([found[:64] * not_left, found[64:]], axis=0).astype(jnp.bfloat16)
-        given = jnp.dot(found, words_back[...], preferred_element_type=jnp.float32)
-        given = given.reshape(6, 64, 512)
-        if patch_row > 0:
-            upper = given[0:5, :, 128:256] + given[1:6, :, 0:128]
-            if patch_row == 1:
-                recon[0] = tail[...] + upper
-            elif patch_row < 6:
-                recon[patch_row - 1] = tail[...] + upper
-        if patch_row < 5:
-            tail[...] = given[0:5, :, 384:512] + given[1:6, :, 256:384]
-
+        outer[0, block_row] = widened(loaded(0, block_row))[1]
+        even, odd = widened(loaded(3, block_row))
+        outer[1, block_row] = even
+        outer[2, block_row] = odd
+    unused, left_found = first_codes(outer.at[0], inner.at[0], words, not_top)
+    kept, middle = first_codes(inner.at[3], outer.at[1], words, not_top)
+    unused, right_found = first_codes(outer.at[1], outer.at[2], words, not_top)
+    (left_far,) = given_back((left_found * not_left).astype(jnp.bfloat16), words_back, (1,))
+    near, far = given_back(middle.astype(jnp.bfloat16), words_back, (0, 1))
+    (right_near,) = given_back(right_found.astype(jnp.bfloat16), words_back, (0,))
+    rest_of(0, recon_inner[0] + left_far, 0)
+    rest_of(3, recon_inner[1] + near, 1)
+    rest_of(4, far + right_near, 2)
+    leaving(0, last_codes(first_inner[0], later.at[0], later_inner.at[0], words))
+    leaving(2, last_codes(first_inner[1], later_inner.at[1], later.at[1], words))
+    leaving(3, last_codes(kept, later.at[1], later.at[2], words))
     left = lax.broadcasted_iota(jnp.int32, (64, 128), 1) < 64
-    for block_row in range(5):
-        for pair in range(3):
-            even = recon[block_row, 2 * pair]
-            odd = recon[block_row, 2 * pair + 1] if pair < 2 else even
-            near = jnp.where(left, even, pltpu.roll(odd, 64, 1))
-            far = jnp.where(left, pltpu.roll(even, 64, 1), odd)
-            rebuilt = near + time_rolled(far, 1)
-            if block_row < 4 and pair < 2:
-                rest = whole[block_row, pair] - rebuilt
-                whole_rest = rest
-                binned[block_row, pair] = whole_rest
-            elif pair < 2:
-                rest = (loaded(pair + 1, 5) - rebuilt) * not_bottom
-            else:
-                rest = (loaded(3, block_row + 1) - rebuilt) * not_right
-                if block_row == 4:
-                    rest = rest * not_bottom
-            even, odd = widened(rest)
-            field[block_row, 2 * pair] = even
-            if pair < 2:
-                field[block_row, 2 * pair + 1] = odd
-
-    stores = []
-    for patch_row in range(4):
-        found = first[patch_row] + step_size * correlated(field, patch_row, 4)
-        first[patch_row] = shrink_codes(found)
-        stores.append(
-            pltpu.make_async_copy(first.at[patch_row], codes.at[patch_row], leave.at[patch_row])
-        )
-        stores[-1].start()
-
+    for block_row in range(4):
+        binned[0, block_row] = jnp.where(left, binned[0, block_row], rests[0, block_row])
+        binned[1, block_row] = jnp.where(left, rests[1, block_row], binned[1, block_row])
     lane = lax.broadcasted_iota(jnp.int32, (64, 128), 1) // 16
     for tile in range(2):
         for phase in range(4):
@@ -298,7 +370,7 @@
                 for pair in range(2):
                     for odd in range(2):
                         shift = (64 * part + 32 * pair - 48 * odd - 16 * phase) % 128
-                        piece = binned[2 * tile + part, pair]
+                        piece = binned[pair, 2 * tile + part]
                         piece = piece if shift == 0 else pltpu.roll(piece, shift, 1)
                         made = (
                             piece
@@ -313,7 +385,9 @@
                 for row in range(4):
                     at = part * 64 + block_col * 16 + row * 4
                     to = (2 * tile + part) * 64 + row * 16 + block_col * 4
-                    residual[to : to + 4, :] = flat[at : at + 4, :]
+                    flat_rest[to : to + 4, :] = flat[at : at + 4, :]
+    stores.append(pltpu.make_async_copy(flat_rest, residual, leave.at[5]))
+    stores[-1].start()
     for store in stores:
         store.wait()
 
@@ -390,26 +464,43 @@
         [half, from_even, from_odd],
     )
     from_even, from_odd = swapped(own_even, "xline", 0), swapped(own_odd, "xline", 1)
+    full_shape = lambda *shape: jax.ShapeDtypeStruct(shape, jnp.float32)
+    inner, first, recon, rests, later, codes_inner = call_kernel(
+        inner_kernel,
+        (
+            pair_shape(4, 7),
+            full_shape(2, 256, 512),
+            full_shape(2, 5, 64, 128),
+            full_shape(2, 4, 64, 128),
+            pair_shape(2, 5),
+            full_shape(4, 64, 512),
+        ),
+        (pltpu.VMEM,) * 6,
+        [],
+        pltpu.VMEM,
+        [whole, own_even, own_odd, words, words_back],
+        cost=pl.CostEstimate(flops=1_400_000_000, bytes_accessed=4_000_000, transcendentals=0),
+    )
     codes, residual = call_kernel(
         sparse_kernel,
-        (
-            jax.ShapeDtypeStruct((4, 256, 512), jnp.float32),
-            jax.ShapeDtypeStruct((256, time_len), jnp.float32),
-        ),
-        (pltpu.HBM, pltpu.VMEM),
+        (full_shape(4, 4, 64, 512), full_shape(256, time_len)),
+        (pltpu.HBM, pltpu.HBM),
         [
-            pltpu.VMEM((7, 7, 64, 128), jnp.bfloat16),
-            pltpu.VMEM((4, 256, 512), jnp.float32),
-            pltpu.VMEM((5, 5, 64, 128), jnp.float32),
-            pltpu.VMEM((5, 64, 128), jnp.float32),
+            pltpu.VMEM((3, 7, 64, 128), jnp.bfloat16),
+            pltpu.VMEM((3, 5, 64, 128), jnp.bfloat16),
             pltpu.VMEM((2, 256, 128), jnp.float32),
-            pltpu.VMEM((4, 2, 64, 128), jnp.float32),
-            pltpu.SemaphoreType.DMA((4,)),
+            pltpu.VMEM((2, 4, 64, 128), jnp.float32),
+            pltpu.VMEM((3, 4, 64, 512), jnp.float32),
+            pltpu.VMEM((256, time_len), jnp.float32),
+            pltpu.SemaphoreType.DMA((6,)),
         ],
         pltpu.VMEM,
-        [whole, own_even, own_odd, from_even, from_odd, words, words_back],
-    )
-    return codes.reshape(4, 4, 64, 512), residual.reshape(16, 16, time_len)
+        [
+            whole, own_even, own_odd, from_even, from_odd, inner, first, recon, rests, later,
+            codes_inner, words, words_back,
+        ],
+    )
+    return codes, residual.reshape(16, 16, time_len)
 
 
 def solution(mesh):

time: 59.1 us -> 57.1 us (0.966)
  waiting for transfers between devices: 29.5 us -> 27.4 us
    ppermute x4, waiting for transfers between devices: 10.1 us -> 7.95 us  [swapped(): return lax.ppermute(block, axis, list(enumerate(partner)))]
    pallas_call x4 -> x5, Pallas kernels: 12.9 us -> 13 us  [call_kernel(): pl.pallas_call(kernel, out_shape=out_shape, in_specs=[pl.BlockSpec(memory...]
  transfers between devices with their start and end apart: 5 -> 5, of which waited for: 4 -> 4; matrix products, arithmetic and copies ran while one was open for 2% -> 2% of each run, Pallas kernels for 0% -> 4%
where the time goes in v4:
time: 57.1 us; the launch traced here: 56.9 us
  waiting for transfers between devices  27.4 us (48%)
  starting transfers between devices  14.8 us (26%)
  Pallas kernels  13 us (23%)
  local copies, waits for them, and re-layouts  0.93 us (2%)
  between operations  0.76 us (1%)
    all_to_all x1, waiting for transfers between devices, body(): lax.all_to_all(sent.reshape(send_rows, 1, 128), ('inline', 'xline'), spli...  19.4 us
    pallas_call x5, Pallas kernels, call_kernel(): pl.pallas_call(kernel, out_shape=out_shape, in_specs=[pl.BlockSpec(memory...  13 us
    all_to_all x1, starting transfers between devices, body(): lax.all_to_all(sent.reshape(send_rows, 1, 128), ('inline', 'xline'), spli...  11.1 us
    ppermute x4, waiting for transfers between devices, swapped(): return lax.ppermute(block, axis, list(enumerate(partner)))  7.95 us
    ppermute x4, starting transfers between devices, swapped(): return lax.ppermute(block, axis, list(enumerate(partner)))  3.7 us
  transfers between devices with their start and end apart: 5, of which 4 were waited for; matrix products, arithmetic and copies ran while one was open for 2% of the time, Pallas kernels for 4%

profile of v4, /device:TPU:0, one launch (start us, length us, event | category | flops | bytes accessed | tf_op | source)
XLA Modules:
  0.0 56.9 jit_solution(8548124182938563854)
XLA Ops:
  0.6 5.2 %shard_map.86 = s32[2176,128]{1,0:T(8,128)} custom-call(f32[4]{0:T(128)} %gains_in.1, f32[1024,256]{1,0:T(8,128)} %traces_in.1, s32[1,1024]{1,0:T(1,128)} %bitcast.21, s32[1,1024]{1,0:T(1,128)} %bitcast.22, s32[1,1024]{1,0:T(1,128)} %bitcast.23), custom_call_target="tpu_custom_call" | custom-call | tf_op jit(solution)/shard_map/pallas_call | solution.py:24
  5.9 0.0 copy-start.1
  5.9 11.1 %all-to-all-start = ((s32[2176,1,128]{2,1,0:T(1,128)}), s32[2176,1,128]{2,1,0:T(1,128)S(1)}, u32[]{:S(2)}, u32[]{:S(2)}) async-start(s32[2176,1,128]{2,1,0:T(1,128)} %bitcast.18), calls=%async_computation | async-start | bytes 2228224 | tf_op jit(solution)/shard_map/all_to_all | solution.py:425
  17.0 0.0 copy-done.1
  17.0 0.1 reshape.39
  17.1 0.0 copy-start
  17.2 0.1 reshape.40.base
  17.3 19.4 %all-to-all-done = s32[2176,1,128]{2,1,0:T(1,128)S(1)} async-done(((s32[2176,1,128]{2,1,0:T(1,128)}), s32[2176,1,128]{2,1,0:T(1,128)S(1)}, u32[]{:S(2)}, u32[]{:S(2)}) %all-to-all-start) | async-done | bytes 1114144 | tf_op jit(solution)/shard_map/all_to_all | solution.py:425
  36.7 2.6 %shard_map.87 = (f32[4,2,64,128]{3,2,1,0:T(8,128)S(1)}, bf16[2,4,64,128]{3,2,1,0:T(8,128)(2,1)S(1)}, bf16[2,2,64,128]{3,2,1,0:T(8,128)(2,1)S(1)}, bf16[2,2,64,128]{3,2,1,0:T(8,128)(2,1)S(1)}) custom-call(s32[2176,128]{1,0:T(8,128)S(1)} %bitcast.15, f32[256,256]{1,0:T(8,128)S(1)} %reshape.40.base), custom_call_target="tpu_custom_call" | custom-call | tf_op jit(solution)/shard_map/pallas_call | solution.py:24
  39.3 0.1 collective-permute-start
  39.4 2.0 %collective-permute-start.1 = (bf16[2,2,64,128]{3,2,1,0:T(8,128)(2,1)S(1)}, bf16[2,2,64,128]{3,2,1,0:T(8,128)(2,1)S(1)}, u32[]{:S(2)}, u32[]{:S(2)}) collective-permute-start(bf16[2,2,64,128]{3,2,1,0:T(8,128)(2,1)S(1)} %get-tuple-element.19), channel_id=1, source_target_pairs={{0,112},{16,32},{32,16},{48,64},{64,48},{80,96},{96,80},{112,0},{1... | collective-permute-start | bytes 196616 | tf_op jit(solution)/shard_map/ppermute | solution.py:455
  41.4 0.0 copy-done
  41.4 0.1 reshape.41
  41.5 0.3 copy.22
  41.8 0.1 reshape.42.words
  41.9 0.2 copy.19
  42.1 1.5 %collective-permute-done.from_even = bf16[2,2,64,128]{3,2,1,0:T(8,128)(2,1)S(1)} collective-permute-done((bf16[2,2,64,128]{3,2,1,0:T(8,128)(2,1)S(1)}, bf16[2,2,64,128]{3,2,1,0:T(8,128)(2,1)S(1)}, u32[]{:S(2)}, u32[]{:S(2)}) %collective-permute-start) | collective-permute-done | bytes 65568 | tf_op jit(solution)/shard_map/ppermute | solution.py:455
  43.6 3.7 %collective-permute-done.1.from_odd = bf16[2,2,64,128]{3,2,1,0:T(8,128)(2,1)S(1)} collective-permute-done((bf16[2,2,64,128]{3,2,1,0:T(8,128)(2,1)S(1)}, bf16[2,2,64,128]{3,2,1,0:T(8,128)(2,1)S(1)}, u32[]{:S(2)}, u32[]{:S(2)}) %collective-permute-start.1) | collective-permute-done | bytes 65568 | tf_op jit(solution)/shard_map/ppermute | solution.py:455
  47.4 0.1 collective-permute-start.2
  47.5 1.5 %collective-permute-start.3 = (bf16[7,64,128]{2,1,0:T(8,128)(2,1)S(1)}, bf16[7,64,128]{2,1,0:T(8,128)(2,1)S(1)}, u32[]{:S(2)}, u32[]{:S(2)}) collective-permute-start(bf16[7,64,128]{2,1,0:T(8,128)(2,1)S(1)} %get-tuple-element.21.own_odd), channel_id=1, source_target_pairs={{0,15},{1,2},{2,1},{3,4},{4,3},{5,6},{6,5},{7,8},{8,7},{9,10},{10,... | collective-permute-start | bytes 344072 | tf_op jit(solution)/shard_map/ppermute | solution.py:455
  49.0 2.1 %shard_map.89 = (bf16[4,7,64,128]{3,2,1,0:T(8,128)(2,1)S(1)}, f32[2,256,512]{2,1,0:T(8,128)S(1)}, f32[2,5,64,128]{3,2,1,0:T(8,128)S(1)}, f32[2,4,64,128]{3,2,1,0...) custom-call(f32[4,2,64,128]{3,2,1,0:T(8,128)S(1)} %get-tuple-element.16.whole, ...), custom_call_target="tpu_custom_call" | custom-call | flops 1400000000 | bytes 4000000 | tf_op jit(solution)/shard_map/pallas_call | solution.py:24
  51.1 0.0 collective-permute-done.2.from_even
  51.1 2.7 %collective-permute-done.3.from_odd = bf16[7,64,128]{2,1,0:T(8,128)(2,1)S(1)} collective-permute-done((bf16[7,64,128]{2,1,0:T(8,128)(2,1)S(1)}, bf16[7,64,128]{2,1,0:T(8,128)(2,1)S(1)}, u32[]{:S(2)}, u32[]{:S(2)}) %collective-permute-start.3) | collective-permute-done | bytes 114720 | tf_op jit(solution)/shard_map/ppermute | solution.py:455
  53.9 3.0 %shard_map.90 = (f32[4,4,64,512]{3,2,1,0:T(8,128)}, f32[256,256]{1,0:T(8,128)}) custom-call(f32[4,2,64,128]{3,2,1,0:T(8,128)S(1)} %get-tuple-element.16.whole, bf16[7,64,128]{2,1,0:T(8,128)(2,1)S(1)} %get-tuple-element.20.own_even, bf16[7,64,128]{2,1,0:T(8,128)(2,1)S(1)} %get-tuple-element.21.own_odd, ...), custom_call_target="tpu_custom_call" | custom-call | tf_op jit(solution)/shard_map/pallas_call | solution.py:24
  (2 shorter events, 0.1 us)
Async XLA Ops:
  5.9 11.2 %copy-start.1 = (f32[16,16,256]{2,1,0:T(8,128)S(1)}, f32[16,16,256]{2,1,0:T(8,128)}, u32[]{:S(2)}) copy-start(f32[16,16,256]{2,1,0:T(8,128)} %param.7) | copy-start | bytes 786436
  5.9 30.8 %all-to-all-start = ((s32[2176,1,128]{2,1,0:T(1,128)}), s32[2176,1,128]{2,1,0:T(1,128)S(1)}, u32[]{:S(2)}, u32[]{:S(2)}) async-start(s32[2176,1,128]{2,1,0:T(1,128)} %bitcast.18), calls=%async_computation | async-start | bytes 2228224 | tf_op jit(solution)/shard_map/all_to_all | solution.py:425
  17.1 24.3 %copy-start = (bf16[512,512]{1,0:T(8,128)(2,1)S(1)}, bf16[512,512]{1,0:T(8,128)(2,1)}, u32[]{:S(2)}) copy-start(bf16[512,512]{1,0:T(8,128)(2,1)} %param.13) | copy-start | bytes 1572868
  39.3 4.3 %collective-permute-start = (bf16[2,2,64,128]{3,2,1,0:T(8,128)(2,1)S(1)}, bf16[2,2,64,128]{3,2,1,0:T(8,128)(2,1)S(1)}, u32[]{:S(2)}, u32[]{:S(2)}) collective-permute-start(bf16[2,2,64,128]{3,2,1,0:T(8,128)(2,1)S(1)} %get-tuple-element.18), channel_id=1, source_target_pairs={{0,16},{16,0},{32,48},{48,32},{64,80},{80,64},{96,112},{112,96},{1... | collective-permute-start | bytes 196616 | tf_op jit(solution)/shard_map/ppermute | solution.py:455
  39.4 8.0 %collective-permute-start.1 = (bf16[2,2,64,128]{3,2,1,0:T(8,128)(2,1)S(1)}, bf16[2,2,64,128]{3,2,1,0:T(8,128)(2,1)S(1)}, u32[]{:S(2)}, u32[]{:S(2)}) collective-permute-start(bf16[2,2,64,128]{3,2,1,0:T(8,128)(2,1)S(1)} %get-tuple-element.19), channel_id=1, source_target_pairs={{0,112},{16,32},{32,16},{48,64},{64,48},{80,96},{96,80},{112,0},{1... | collective-permute-start | bytes 196616 | tf_op jit(solution)/shard_map/ppermute | solution.py:455
  47.4 3.8 %collective-permute-start.2 = (bf16[7,64,128]{2,1,0:T(8,128)(2,1)S(1)}, bf16[7,64,128]{2,1,0:T(8,128)(2,1)S(1)}, u32[]{:S(2)}, u32[]{:S(2)}) collective-permute-start(bf16[7,64,128]{2,1,0:T(8,128)(2,1)S(1)} %get-tuple-element.20.own_even), channel_id=1, source_target_pairs={{0,1},{1,0},{2,3},{3,2},{4,5},{5,4},{6,7},{7,6},{8,9},{9,8},{10,11... | collective-permute-start | bytes 344072 | tf_op jit(solution)/shard_map/ppermute | solution.py:455
  47.5 6.4 %collective-permute-start.3 = (bf16[7,64,128]{2,1,0:T(8,128)(2,1)S(1)}, bf16[7,64,128]{2,1,0:T(8,128)(2,1)S(1)}, u32[]{:S(2)}, u32[]{:S(2)}) collective-permute-start(bf16[7,64,128]{2,1,0:T(8,128)(2,1)S(1)} %get-tuple-element.21.own_odd), channel_id=1, source_target_pairs={{0,15},{1,2},{2,1},{3,4},{4,3},{5,6},{6,5},{7,8},{8,7},{9,10},{10,... | collective-permute-start | bytes 344072 | tf_op jit(solution)/shard_map/ppermute | solution.py:455

commit v5 on v4

--- a/solution.py
+++ b/solution.py
@@ -121,55 +121,67 @@
         store.wait()
 
 
-def merge_kernel(got, base, whole, half, to_even, to_odd, pick, parts, turned):
+def exchanged(four):
+    lane = lax.broadcasted_iota(jnp.int32, four[0].shape, 1)
+
+    def crossed(lower, upper, distance):
+        keep = (lane // distance) % 2 == 0
+        return (
+            jnp.where(keep, lower, pltpu.roll(upper, distance, 1)),
+            jnp.where(keep, pltpu.roll(lower, 128 - distance, 1), upper),
+        )
+
+    (zero, two), (one, three) = crossed(four[0], four[2], 32), crossed(four[1], four[3], 32)
+    (zero, one), (two, three) = crossed(zero, one, 16), crossed(two, three, 16)
+    return zero, one, two, three
+
+
+def merge_kernel(got, base, whole, half, to_even, to_odd, turned):
     tiles = got.shape[0] // 128
     bin_row = lax.broadcasted_iota(jnp.int32, (256, 128), 0)
-    bin_slot = (
-        (bin_row // 64) * 64 + ((bin_row // 4) % 4) * 16 + ((bin_row // 16) % 4) * 4 + bin_row % 4
-    )
+    tile, part, pair, odd = bin_row // 128, (bin_row // 32) % 2, (bin_row // 16) % 2, (bin_row // 64) % 2
+    block_row, block_col = 2 * tile + part, 2 * pair + odd
+    bin_slot = block_row * 64 + ((bin_row // 4) % 4) * 16 + block_col * 4 + bin_row % 4
     wanted = bin_slot + 1
     listed = got[pl.ds(16, 128, stride=17), :]
     begin = 17 * lax.broadcasted_iota(jnp.int32, (128, 128), 0)
     lane = lax.broadcasted_iota(jnp.int32, (128, 128), 1)
     tile_of = begin // 128 + jnp.where(lane < begin % 128, 1, 0)
+    tiles_each = 4
     fold = jnp.zeros((256, 128), jnp.float32)
-    for tile in range(tiles):
-        low_group, high_group = (128 * tile) // 136, min((128 * tile + 127) // 136, 15)
-        spot = slice(8 * low_group, 8 * high_group + 8)
-        slots = jnp.sum(jnp.where(tile_of[spot] == tile, listed[spot], 0), axis=0, keepdims=True)
-        hit = jnp.where(wanted == slots, 1.0, 0.0)
-        fold = fold + hit
-        spot = slice(128 * tile, 128 * tile + 128)
-        pick[:, spot] = hit.astype(jnp.bfloat16)
-        word = got[spot, :]
-        for side, code in enumerate((word >> 16, (word << 16) >> 16)):
-            value = decode(code)
-            high = value.astype(jnp.bfloat16)
-            low = (value - high.astype(jnp.float32)).astype(jnp.bfloat16)
-            parts[spot, side * 128 : side * 128 + 128] = high
-            parts[spot, 256 + side * 128 : 384 + side * 128] = low
-    stack = jnp.dot(pick[...], parts[...], preferred_element_type=jnp.float32)
+    stack = jnp.zeros((256, 512), jnp.float32)
+    for at in range(0, tiles, tiles_each):
+        hits, rows = [], []
+        for tile in range(at, min(at + tiles_each, tiles)):
+            low_group, high_group = (128 * tile) // 136, min((128 * tile + 127) // 136, 15)
+            spot = slice(8 * low_group, 8 * high_group + 8)
+            slots = jnp.sum(jnp.where(tile_of[spot] == tile, listed[spot], 0), axis=0, keepdims=True)
+            hit = jnp.where(wanted == slots, 1.0, 0.0)
+            fold = fold + hit
+            hits.append(hit.astype(jnp.bfloat16))
+            word = got[128 * tile : 128 * tile + 128, :]
+            values = [decode(code) for code in (word >> 16, (word << 16) >> 16)]
+            high = [value.astype(jnp.bfloat16) for value in values]
+            low = [
+                (value - part.astype(jnp.float32)).astype(jnp.bfloat16)
+                for value, part in zip(values, high)
+            ]
+            rows.append(jnp.concatenate(high + low, axis=1))
+        stack = stack + jnp.dot(
+            jnp.concatenate(hits, axis=1),
+            jnp.concatenate(rows, axis=0),
+            preferred_element_type=jnp.float32,
+        )
     fold = jnp.sum(fold, axis=1, keepdims=True)
     merged = (base[...] + (stack[:, :256] + stack[:, 256:])) / (1.0 + fold)
     turned[0] = jnp.transpose(merged[:128])
     turned[1] = jnp.transpose(merged[128:])
-    lane = lax.broadcasted_iota(jnp.int32, (64, 128), 1) // 16
     for tile in range(2):
         slabs = [turned[tile, pl.ds(phase, 64, stride=4), :] for phase in range(4)]
-        for part in range(2):
-            for pair in range(2):
-                made = None
-                for odd in range(2):
-                    for phase in range(4):
-                        shift = (48 * odd + 16 * phase - 64 * part - 32 * pair) % 128
-                        piece = slabs[phase] if shift == 0 else pltpu.roll(slabs[phase], shift, 1)
-                        made = (
-                            piece if made is None else jnp.where(lane == 4 * odd + phase, piece, made)
-                        )
-                block_row = 2 * tile + part
-                whole[block_row, pair] = made
-                made = made.astype(jnp.bfloat16)
-                half[pair, block_row] = made
+        for number, made in enumerate(exchanged(slabs)):
+            part, pair = number // 2, number % 2
+            whole[2 * tile + part, pair] = made
+            half[pair, 2 * tile + part] = made.astype(jnp.bfloat16)
     odd_device = lax.rem(lax.axis_index("inline"), 2)
     to_even[...] = half[:, pl.ds(2 - 2 * odd_device, 2)]
     to_odd[...] = half[:, pl.ds(2 * odd_device, 2)]
@@ -362,30 +374,18 @@
     for block_row in range(4):
         binned[0, block_row] = jnp.where(left, binned[0, block_row], rests[0, block_row])
         binned[1, block_row] = jnp.where(left, rests[1, block_row], binned[1, block_row])
-    lane = lax.broadcasted_iota(jnp.int32, (64, 128), 1) // 16
     for tile in range(2):
-        for phase in range(4):
-            made = None
-            for part in range(2):
-                for pair in range(2):
-                    for odd in range(2):
-                        shift = (64 * part + 32 * pair - 48 * odd - 16 * phase) % 128
-                        piece = binned[pair, 2 * tile + part]
-                        piece = piece if shift == 0 else pltpu.roll(piece, shift, 1)
-                        made = (
-                            piece
-                            if made is None
-                            else jnp.where(lane == 4 * part + 2 * pair + odd, piece, made)
-                        )
+        blocks = [binned[pair, 2 * tile + part] for part in range(2) for pair in range(2)]
+        for phase, made in enumerate(exchanged(blocks)):
             turned[tile, pl.ds(phase, 64, stride=4), :] = made
     for tile in range(2):
         flat = jnp.transpose(turned[tile])
-        for part in range(2):
-            for block_col in range(4):
-                for row in range(4):
-                    at = part * 64 + block_col * 16 + row * 4
-                    to = (2 * tile + part) * 64 + row * 16 + block_col * 4
-                    flat_rest[to : to + 4, :] = flat[at : at + 4, :]
+        for number in range(8):
+            odd, part, pair = number // 4, (number // 2) % 2, number % 2
+            for row in range(4):
+                at = number * 16 + row * 4
+                to = (2 * tile + part) * 64 + row * 16 + (2 * pair + odd) * 4
+                flat_rest[to : to + 4, :] = flat[at : at + 4, :]
     stores.append(pltpu.make_async_copy(flat_rest, residual, leave.at[5]))
     stores[-1].start()
     for store in stores:
@@ -428,7 +428,9 @@
     words = dictionary.reshape(2, 4, 2, 4, 2, 4, 512).transpose(0, 2, 4, 5, 1, 3, 6).reshape(512, 512)
     words_back = words.T
     base = (
-        base_volume.reshape(4, 4, 4, 4, time_len).transpose(0, 2, 1, 3, 4).reshape(256, time_len)
+        base_volume.reshape(2, 2, 4, 2, 2, 4, time_len)
+        .transpose(0, 4, 1, 3, 2, 5, 6)
+        .reshape(256, time_len)
     )
     pair_shape = lambda *lead: jax.ShapeDtypeStruct(lead + (64, 128), jnp.bfloat16)
     whole, half, to_even, to_odd = call_kernel(
@@ -441,20 +443,29 @@
         ),
         (pltpu.VMEM,) * 4,
         [
-            pltpu.VMEM((256, send_rows), jnp.bfloat16),
-            pltpu.VMEM((send_rows, 512), jnp.bfloat16),
             pltpu.VMEM((2, 256, 128), jnp.float32),
         ],
         pltpu.VMEM,
         [got, base],
     )
 
-    def swapped(block, axis, odd_pairs):
-        count = lax.axis_size(axis)
-        partner = [(i + 1 if i % 2 == odd_pairs else i - 1) % count for i in range(count)]
-        return lax.ppermute(block, axis, list(enumerate(partner)))
-
-    from_even, from_odd = swapped(to_even, "inline", 0), swapped(to_odd, "inline", 1)
+    rows, columns = lax.axis_size("inline"), lax.axis_size("xline")
+
+    def swapped(block, along_rows, odd_pairs):
+        route = []
+        for row in range(rows):
+            for column in range(columns):
+                at, count = (row, rows) if along_rows else (column, columns)
+                to = at + 1 if at % 2 == odd_pairs else at - 1
+                if not 0 <= to < count:
+                    partner = (row, column ^ 1) if along_rows else (row ^ 1, column)
+                else:
+                    partner = (to, column) if along_rows else (row, to)
+                route.append((row * columns + column, partner[0] * columns + partner[1]))
+        return lax.ppermute(block, ("inline", "xline"), route)
+
+    from_odd = swapped(to_odd, True, 1)
+    from_even = swapped(to_even, True, 0)
     own_even, own_odd = call_kernel(
         assemble_kernel,
         (pair_shape(7), pair_shape(7)),
@@ -463,7 +474,8 @@
         pltpu.VMEM,
         [half, from_even, from_odd],
     )
-    from_even, from_odd = swapped(own_even, "xline", 0), swapped(own_odd, "xline", 1)
+    from_odd = swapped(own_odd, False, 1)
+    from_even = swapped(own_even, False, 0)
     full_shape = lambda *shape: jax.ShapeDtypeStruct(shape, jnp.float32)
     inner, first, recon, rests, later, codes_inner = call_kernel(
         inner_kernel,

time: 57.1 us -> 54.1 us (0.947)
  the two profiles are of different devices: /device:TPU:0 before, /device:TPU:14 now
where the time goes in v5:
time: 54.1 us; the launch traced here: 53.1 us
  waiting for transfers between devices  24.6 us (45%)
  starting transfers between devices  14.3 us (26%)
  Pallas kernels  12.5 us (23%)
  local copies, waits for them, and re-layouts  0.94 us (2%)
  between operations  0.75 us (1%)
    all_to_all x1, waiting for transfers between devices, body(): lax.all_to_all(sent.reshape(send_rows, 1, 128), ('inline', 'xline'), spli...  17.3 us
    pallas_call x5, Pallas kernels, call_kernel(): pl.pallas_call(kernel, out_shape=out_shape, in_specs=[pl.BlockSpec(memory...  12.5 us
    all_to_all x1, starting transfers between devices, body(): lax.all_to_all(sent.reshape(send_rows, 1, 128), ('inline', 'xline'), spli...  10.4 us
    ppermute x4, waiting for transfers between devices, swapped(): return lax.ppermute(block, ('inline', 'xline'), route)  7.22 us
    ppermute x4, starting transfers between devices, swapped(): return lax.ppermute(block, ('inline', 'xline'), route)  3.97 us
  transfers between devices with their start and end apart: 5, of which 4 were waited for; matrix products, arithmetic and copies ran while one was open for 2% of the time, Pallas kernels for 4%

profile of v5, /device:TPU:14, one launch (start us, length us, event | category | flops | bytes accessed | tf_op | source)
XLA Modules:
  0.0 53.1 jit_solution(18001981650606904041)
XLA Ops:
  0.6 5.2 %shard_map.86 = s32[2176,128]{1,0:T(8,128)} custom-call(f32[4]{0:T(128)} %gains_in.1, f32[1024,256]{1,0:T(8,128)} %traces_in.1, s32[1,1024]{1,0:T(1,128)} %bitcast.21, s32[1,1024]{1,0:T(1,128)} %bitcast.22, s32[1,1024]{1,0:T(1,128)} %bitcast.23), custom_call_target="tpu_custom_call" | custom-call | tf_op jit(solution)/shard_map/pallas_call | solution.py:24
  5.9 0.0 copy-start.1
  5.9 10.4 %all-to-all-start = ((s32[2176,1,128]{2,1,0:T(1,128)}), s32[2176,1,128]{2,1,0:T(1,128)S(1)}, u32[]{:S(2)}, u32[]{:S(2)}) async-start(s32[2176,1,128]{2,1,0:T(1,128)} %bitcast.18), calls=%async_computation | async-start | bytes 2228224 | tf_op jit(solution)/shard_map/all_to_all | solution.py:425
  16.2 0.0 copy-done.1
  16.3 0.1 reshape.39
  16.3 0.0 copy-start
  16.4 0.1 reshape.40.base
  16.5 17.3 %all-to-all-done = s32[2176,1,128]{2,1,0:T(1,128)S(1)} async-done(((s32[2176,1,128]{2,1,0:T(1,128)}), s32[2176,1,128]{2,1,0:T(1,128)S(1)}, u32[]{:S(2)}, u32[]{:S(2)}) %all-to-all-start) | async-done | bytes 1114144 | tf_op jit(solution)/shard_map/all_to_all | solution.py:425
  33.8 2.0 %shard_map.87 = (f32[4,2,64,128]{3,2,1,0:T(8,128)S(1)}, bf16[2,4,64,128]{3,2,1,0:T(8,128)(2,1)S(1)}, bf16[2,2,64,128]{3,2,1,0:T(8,128)(2,1)S(1)}, bf16[2,2,64,128]{3,2,1,0:T(8,128)(2,1)S(1)}) custom-call(s32[2176,128]{1,0:T(8,128)S(1)} %bitcast.15, f32[256,256]{1,0:T(8,128)S(1)} %reshape.40.base), custom_call_target="tpu_custom_call" | custom-call | tf_op jit(solution)/shard_map/pallas_call | solution.py:24
  35.8 0.7 %collective-permute-start = (bf16[2,2,64,128]{3,2,1,0:T(8,128)(2,1)S(1)}, bf16[2,2,64,128]{3,2,1,0:T(8,128)(2,1)S(1)}, u32[]{:S(2)}, u32[]{:S(2)}) collective-permute-start(bf16[2,2,64,128]{3,2,1,0:T(8,128)(2,1)S(1)} %get-tuple-element.18), channel_id=1, source_target_pairs={{0,16},{1,17},{2,18},{3,19},{4,20},{5,21},{6,22},{7,23},{8,24},{9,... | collective-permute-start | bytes 196616 | tf_op jit(solution)/shard_map/ppermute | solution.py:465
  36.5 1.7 %collective-permute-start.1 = (bf16[2,2,64,128]{3,2,1,0:T(8,128)(2,1)S(1)}, bf16[2,2,64,128]{3,2,1,0:T(8,128)(2,1)S(1)}, u32[]{:S(2)}, u32[]{:S(2)}) collective-permute-start(bf16[2,2,64,128]{3,2,1,0:T(8,128)(2,1)S(1)} %get-tuple-element.19), channel_id=1, source_target_pairs={{0,1},{1,0},{2,3},{3,2},{4,5},{5,4},{6,7},{7,6},{8,9},{9,8},{10,11... | collective-permute-start | bytes 196616 | tf_op jit(solution)/shard_map/ppermute | solution.py:465
  38.2 0.0 copy-done
  38.2 0.1 reshape.41
  38.4 0.3 copy.22
  38.6 0.1 reshape.42.words
  38.8 0.2 copy.19
  39.0 1.2 %collective-permute-done.from_even = bf16[2,2,64,128]{3,2,1,0:T(8,128)(2,1)S(1)} collective-permute-done((bf16[2,2,64,128]{3,2,1,0:T(8,128)(2,1)S(1)}, bf16[2,2,64,128]{3,2,1,0:T(8,128)(2,1)S(1)}, u32[]{:S(2)}, u32[]{:S(2)}) %collective-permute-start) | collective-permute-done | bytes 65568 | tf_op jit(solution)/shard_map/ppermute | solution.py:465
  40.2 4.3 %collective-permute-done.1.from_odd = bf16[2,2,64,128]{3,2,1,0:T(8,128)(2,1)S(1)} collective-permute-done((bf16[2,2,64,128]{3,2,1,0:T(8,128)(2,1)S(1)}, bf16[2,2,64,128]{3,2,1,0:T(8,128)(2,1)S(1)}, u32[]{:S(2)}, u32[]{:S(2)}) %collective-permute-start.1) | collective-permute-done | bytes 65568 | tf_op jit(solution)/shard_map/ppermute | solution.py:465
  44.6 0.1 collective-permute-start.2
  44.6 1.5 %collective-permute-start.3 = (bf16[7,64,128]{2,1,0:T(8,128)(2,1)S(1)}, bf16[7,64,128]{2,1,0:T(8,128)(2,1)S(1)}, u32[]{:S(2)}, u32[]{:S(2)}) collective-permute-start(bf16[7,64,128]{2,1,0:T(8,128)(2,1)S(1)} %get-tuple-element.21.own_odd), channel_id=1, source_target_pairs={{0,16},{1,2},{2,1},{3,4},{4,3},{5,6},{6,5},{7,8},{8,7},{9,10},{10,... | collective-permute-start | bytes 344072 | tf_op jit(solution)/shard_map/ppermute | solution.py:465
  46.1 2.1 %shard_map.89 = (bf16[4,7,64,128]{3,2,1,0:T(8,128)(2,1)S(1)}, f32[2,256,512]{2,1,0:T(8,128)S(1)}, f32[2,5,64,128]{3,2,1,0:T(8,128)S(1)}, f32[2,4,64,128]{3,2,1,0...) custom-call(f32[4,2,64,128]{3,2,1,0:T(8,128)S(1)} %get-tuple-element.16.whole, ...), custom_call_target="tpu_custom_call" | custom-call | flops 1400000000 | bytes 4000000 | tf_op jit(solution)/shard_map/pallas_call | solution.py:24
  48.2 0.0 collective-permute-done.2.from_even
  48.3 1.7 %collective-permute-done.3.from_odd = bf16[7,64,128]{2,1,0:T(8,128)(2,1)S(1)} collective-permute-done((bf16[7,64,128]{2,1,0:T(8,128)(2,1)S(1)}, bf16[7,64,128]{2,1,0:T(8,128)(2,1)S(1)}, u32[]{:S(2)}, u32[]{:S(2)}) %collective-permute-start.3) | collective-permute-done | bytes 114720 | tf_op jit(solution)/shard_map/ppermute | solution.py:465
  50.0 3.1 %shard_map.90 = (f32[4,4,64,512]{3,2,1,0:T(8,128)}, f32[256,256]{1,0:T(8,128)}) custom-call(f32[4,2,64,128]{3,2,1,0:T(8,128)S(1)} %get-tuple-element.16.whole, bf16[7,64,128]{2,1,0:T(8,128)(2,1)S(1)} %get-tuple-element.20.own_even, bf16[7,64,128]{2,1,0:T(8,128)(2,1)S(1)} %get-tuple-element.21.own_odd, ...), custom_call_target="tpu_custom_call" | custom-call | tf_op jit(solution)/shard_map/pallas_call | solution.py:24
  (2 shorter events, 0.1 us)
Async XLA Ops:
  5.9 10.4 %copy-start.1 = (f32[16,16,256]{2,1,0:T(8,128)S(1)}, f32[16,16,256]{2,1,0:T(8,128)}, u32[]{:S(2)}) copy-start(f32[16,16,256]{2,1,0:T(8,128)} %param.7) | copy-start | bytes 786436
  5.9 27.9 %all-to-all-start = ((s32[2176,1,128]{2,1,0:T(1,128)}), s32[2176,1,128]{2,1,0:T(1,128)S(1)}, u32[]{:S(2)}, u32[]{:S(2)}) async-start(s32[2176,1,128]{2,1,0:T(1,128)} %bitcast.18), calls=%async_computation | async-start | bytes 2228224 | tf_op jit(solution)/shard_map/all_to_all | solution.py:425
  16.3 21.9 %copy-start = (bf16[512,512]{1,0:T(8,128)(2,1)S(1)}, bf16[512,512]{1,0:T(8,128)(2,1)}, u32[]{:S(2)}) copy-start(bf16[512,512]{1,0:T(8,128)(2,1)} %param.13) | copy-start | bytes 1572868
  35.8 4.3 %collective-permute-start = (bf16[2,2,64,128]{3,2,1,0:T(8,128)(2,1)S(1)}, bf16[2,2,64,128]{3,2,1,0:T(8,128)(2,1)S(1)}, u32[]{:S(2)}, u32[]{:S(2)}) collective-permute-start(bf16[2,2,64,128]{3,2,1,0:T(8,128)(2,1)S(1)} %get-tuple-element.18), channel_id=1, source_target_pairs={{0,16},{1,17},{2,18},{3,19},{4,20},{5,21},{6,22},{7,23},{8,24},{9,... | collective-permute-start | bytes 196616 | tf_op jit(solution)/shard_map/ppermute | solution.py:465
  36.5 8.0 %collective-permute-start.1 = (bf16[2,2,64,128]{3,2,1,0:T(8,128)(2,1)S(1)}, bf16[2,2,64,128]{3,2,1,0:T(8,128)(2,1)S(1)}, u32[]{:S(2)}, u32[]{:S(2)}) collective-permute-start(bf16[2,2,64,128]{3,2,1,0:T(8,128)(2,1)S(1)} %get-tuple-element.19), channel_id=1, source_target_pairs={{0,1},{1,0},{2,3},{3,2},{4,5},{5,4},{6,7},{7,6},{8,9},{9,8},{10,11... | collective-permute-start | bytes 196616 | tf_op jit(solution)/shard_map/ppermute | solution.py:465
  44.6 3.7 %collective-permute-start.2 = (bf16[7,64,128]{2,1,0:T(8,128)(2,1)S(1)}, bf16[7,64,128]{2,1,0:T(8,128)(2,1)S(1)}, u32[]{:S(2)}, u32[]{:S(2)}) collective-permute-start(bf16[7,64,128]{2,1,0:T(8,128)(2,1)S(1)} %get-tuple-element.20.own_even), channel_id=1, source_target_pairs={{0,1},{1,0},{2,3},{3,2},{4,5},{5,4},{6,7},{7,6},{8,9},{9,8},{10,11... | collective-permute-start | bytes 344072 | tf_op jit(solution)/shard_map/ppermute | solution.py:465
  44.6 5.3 %collective-permute-start.3 = (bf16[7,64,128]{2,1,0:T(8,128)(2,1)S(1)}, bf16[7,64,128]{2,1,0:T(8,128)(2,1)S(1)}, u32[]{:S(2)}, u32[]{:S(2)}) collective-permute-start(bf16[7,64,128]{2,1,0:T(8,128)(2,1)S(1)} %get-tuple-element.21.own_odd), channel_id=1, source_target_pairs={{0,16},{1,2},{2,1},{3,4},{4,3},{5,6},{6,5},{7,8},{8,7},{9,10},{10,... | collective-permute-start | bytes 344072 | tf_op jit(solution)/shard_map/ppermute | solution.py:465

commit v6 on v5

--- a/solution.py
+++ b/solution.py
@@ -45,7 +45,7 @@
     return size * jnp.clip(code, -1.0, 1.0)
 
 
-def pack_kernel(gains_in, traces_in, dest_in, slot_in, vid_in, out, gains, traces, dest, slot, vid, built, arrive, leave):
+def pack_kernel(gains_in, traces_in, dest_in, slot_in, vid_in, out, gains, traces, dest, slot, vid, built, words, place, place_at, arrive, leave):
     loads = [
         pltpu.make_async_copy(source, target, arrive.at[number])
         for number, (source, target) in enumerate(
@@ -56,6 +56,7 @@
         load.start()
     trace_count = traces.shape[0]
     device_count = out.shape[0] // 17
+    built[...] = jnp.zeros_like(built)
     chunks = trace_count // 128
     me = lax.axis_index("inline") * lax.axis_size("xline") + lax.axis_index("xline")
     loads[0].wait()
@@ -78,7 +79,9 @@
         wanted = (slot[:, chunk * 128 : chunk * 128 + 128] + 1).astype(jnp.float32)
         spot = lax.rem(17 * me + rank, 128)
         listed.append(jnp.where(row == spot, wanted, 0.0).astype(jnp.bfloat16))
-    place = jnp.concatenate(places, axis=1)
+    place[...] = jnp.concatenate(places, axis=1)
+    put = pltpu.make_async_copy(place, place_at, arrive.at[5])
+    put.start()
     owner = jnp.concatenate(owners, axis=1)
     listing = jnp.concatenate(listed, axis=1)
     slots = lax.dot_general(
@@ -93,32 +96,15 @@
         gain = jnp.where(survey == number, gains[number], gain)
     gain = jnp.transpose(jnp.broadcast_to(gain, (128, trace_count)))
     loads[4].wait()
-    high, low = [], []
-    for half in range(2):
-        code = encode(traces[:, half * 128 : half * 128 + 128] * gain)
-        high.append((code >> 8).astype(jnp.float32).astype(jnp.bfloat16))
-        low.append((code & 255).astype(jnp.float32).astype(jnp.bfloat16))
-    halves = jnp.concatenate(high + low, axis=1)
-
-    owners_each = 16
-    rows = owners_each * 17
-    index = lax.broadcasted_iota(jnp.int32, (rows, trace_count), 0)
-    stores = []
-    for block in range(device_count // owners_each):
-        pick = jnp.where(index == place - block * rows, 1.0, 0.0).astype(jnp.bfloat16)
-        moved = jnp.dot(pick, halves, preferred_element_type=jnp.float32)
-        code = (moved[:, :256] * 256.0 + moved[:, 256:]).astype(jnp.int32)
-        built[block * rows : block * rows + rows, :] = (code[:, :128] << 16) | (
-            code[:, 128:] & 65535
-        )
-        built[pl.ds(block * rows + 16, owners_each, stride=17), :] = slots[
-            block * owners_each : block * owners_each + owners_each
-        ]
-        spot = pl.ds(block * rows, rows)
-        stores.append(pltpu.make_async_copy(built.at[spot], out.at[spot], leave.at[block]))
-        stores[-1].start()
-    for store in stores:
-        store.wait()
+    code = [encode(traces[:, half * 128 : half * 128 + 128] * gain) for half in range(2)]
+    words[...] = (code[0] << 16) | (code[1] & 65535)
+    built[pl.ds(16, device_count, stride=17), :] = slots
+    put.wait()
+    for trace in range(trace_count):
+        built[pl.ds(place_at[0, trace], 1), :] = words[trace : trace + 1, :]
+    send = pltpu.make_async_copy(built, out, leave)
+    send.start()
+    send.wait()
 
 
 def exchanged(four):
@@ -257,13 +243,12 @@
 
 
 def first_codes(near, far, words, not_top):
-    found = shrink_codes(step_size * correlated(near, far, words, 0, 6))
+    found = shrink_codes(correlated(near, far, words, 0, 6))
     return found[64:320], jnp.concatenate([found[:64] * not_top, found[64:]], axis=0)
 
 
 def last_codes(before, near, far, words):
-    found = before + step_size * correlated(near, far, words, 0, 4)
-    return shrink_codes(found).reshape(4, 64, 512)
+    return shrink_codes(before + correlated(near, far, words, 0, 4)).reshape(4, 64, 512)
 
 
 def inner_kernel(whole, own_even, own_odd, words, words_back, field, first, recon, rests, later, made_codes):
@@ -409,8 +394,11 @@
             pltpu.VMEM((1, trace_count), jnp.int32),
             pltpu.VMEM((1, trace_count), jnp.int32),
             pltpu.VMEM((send_rows, 128), jnp.int32),
-            pltpu.SemaphoreType.DMA((5,)),
-            pltpu.SemaphoreType.DMA((device_count // 16,)),
+            pltpu.VMEM((trace_count, 128), jnp.int32),
+            pltpu.VMEM((1, trace_count), jnp.int32),
+            pltpu.SMEM((1, trace_count), jnp.int32),
+            pltpu.SemaphoreType.DMA((6,)),
+            pltpu.SemaphoreType.DMA,
         ],
         pltpu.HBM,
         [
@@ -427,11 +415,13 @@
     ).reshape(send_rows, 128)
     words = dictionary.reshape(2, 4, 2, 4, 2, 4, 512).transpose(0, 2, 4, 5, 1, 3, 6).reshape(512, 512)
     words_back = words.T
+    words = words * jnp.bfloat16(step_size)
     base = (
         base_volume.reshape(2, 2, 4, 2, 2, 4, time_len)
         .transpose(0, 4, 1, 3, 2, 5, 6)
         .reshape(256, time_len)
     )
+    got, base, words, words_back = lax.optimization_barrier((got, base, words, words_back))
     pair_shape = lambda *lead: jax.ShapeDtypeStruct(lead + (64, 128), jnp.bfloat16)
     whole, half, to_even, to_odd = call_kernel(
         merge_kernel,

time: 54.1 us -> 52.2 us (0.965)
  Pallas kernels: 12.5 us -> 10.6 us
  waiting for transfers between devices: 24.6 us -> 23.7 us
  local copies, waits for them, and re-layouts: 0.94 us -> 1.75 us
    pallas_call x5, Pallas kernels: 12.5 us -> 10.6 us  [call_kernel(): pl.pallas_call(kernel, out_shape=out_shape, in_specs=[pl.BlockSpec(memory...]
    all_to_all x1, waiting for transfers between devices: 17.3 us -> 15.7 us  [body(): lax.all_to_all(sent.reshape(send_rows, 1, 128), ('inline', 'xline'), spli...]
    unnamed x4, local copies, waits for them, and re-layouts: 0.01 us -> 0.83 us
    ppermute x4, waiting for transfers between devices: 7.22 us -> 7.97 us  [swapped(): return lax.ppermute(block, ('inline', 'xline'), route)]
where the time goes in v6:
time: 52.2 us; the launch traced here: 51.2 us
  waiting for transfers between devices  23.7 us (45%)
  starting transfers between devices  14.3 us (27%)
  Pallas kernels  10.6 us (20%)
  local copies, waits for them, and re-layouts  1.75 us (3%)
  between operations  0.76 us (1%)
    all_to_all x1, waiting for transfers between devices, body(): lax.all_to_all(sent.reshape(send_rows, 1, 128), ('inline', 'xline'), spli...  15.7 us
    pallas_call x5, Pallas kernels, call_kernel(): pl.pallas_call(kernel, out_shape=out_shape, in_specs=[pl.BlockSpec(memory...  10.6 us
    all_to_all x1, starting transfers between devices, body(): lax.all_to_all(sent.reshape(send_rows, 1, 128), ('inline', 'xline'), spli...  10.4 us
    ppermute x4, waiting for transfers between devices, swapped(): return lax.ppermute(block, ('inline', 'xline'), route)  7.97 us
    ppermute x4, starting transfers between devices, swapped(): return lax.ppermute(block, ('inline', 'xline'), route)  3.98 us
  transfers between devices with their start and end apart: 5, of which 4 were waited for; matrix products, arithmetic and copies ran while one was open for 2% of the time, Pallas kernels for 4%

profile of v6, /device:TPU:14, one launch (start us, length us, event | category | flops | bytes accessed | tf_op | source)
XLA Modules:
  0.0 51.2 jit_solution(807301820639332645)
XLA Ops:
  0.6 3.4 %shard_map.86 = s32[2176,128]{1,0:T(8,128)} custom-call(f32[4]{0:T(128)} %gains_in.1, f32[1024,256]{1,0:T(8,128)} %traces_in.1, s32[1,1024]{1,0:T(1,128)} %bitcast.21, s32[1,1024]{1,0:T(1,128)} %bitcast.22, s32[1,1024]{1,0:T(1,128)} %bitcast.23), custom_call_target="tpu_custom_call" | custom-call | tf_op jit(solution)/shard_map/pallas_call | solution.py:24
  4.1 0.0 copy-start.1
  4.1 10.4 %all-to-all-start = ((s32[2176,1,128]{2,1,0:T(1,128)}), s32[2176,1,128]{2,1,0:T(1,128)S(1)}, u32[]{:S(2)}, u32[]{:S(2)}) async-start(s32[2176,1,128]{2,1,0:T(1,128)} %bitcast.18), calls=%async_computation | async-start | bytes 2228224 | tf_op jit(solution)/shard_map/all_to_all | solution.py:413
  14.5 0.0 copy-done.1
  14.5 0.0 copy-start
  14.5 0.1 reshape.39
  14.6 0.1 reshape.40.base
  14.7 0.8 %copy-done = bf16[512,512]{1,0:T(8,128)(2,1)S(1)} copy-done((bf16[512,512]{1,0:T(8,128)(2,1)S(1)}, bf16[512,512]{1,0:T(8,128)(2,1)}, u32[]{:S(2)}) %copy-start) | copy-done | bytes 524312
  15.5 0.1 reshape.41
  15.7 0.3 copy.22
  15.9 0.1 reshape.42
  16.1 0.2 copy.19
  16.3 15.7 %all-to-all-done = s32[2176,1,128]{2,1,0:T(1,128)S(1)} async-done(((s32[2176,1,128]{2,1,0:T(1,128)}), s32[2176,1,128]{2,1,0:T(1,128)S(1)}, u32[]{:S(2)}, u32[]{:S(2)}) %all-to-all-start) | async-done | bytes 1114144 | tf_op jit(solution)/shard_map/all_to_all | solution.py:413
  32.1 2.0 %shard_map.87 = (f32[4,2,64,128]{3,2,1,0:T(8,128)S(1)}, bf16[2,4,64,128]{3,2,1,0:T(8,128)(2,1)S(1)}, bf16[2,2,64,128]{3,2,1,0:T(8,128)(2,1)S(1)}, bf16[2,2,64,128]{3,2,1,0:T(8,128)(2,1)S(1)}) custom-call(s32[2176,128]{1,0:T(8,128)S(1)} %bitcast.15, f32[256,256]{1,0:T(8,128)S(1)} %reshape.40.base), custom_call_target="tpu_custom_call" | custom-call | tf_op jit(solution)/shard_map/pallas_call | solution.py:24
  34.1 0.7 %collective-permute-start = (bf16[2,2,64,128]{3,2,1,0:T(8,128)(2,1)S(1)}, bf16[2,2,64,128]{3,2,1,0:T(8,128)(2,1)S(1)}, u32[]{:S(2)}, u32[]{:S(2)}) collective-permute-start(bf16[2,2,64,128]{3,2,1,0:T(8,128)(2,1)S(1)} %get-tuple-element.24), channel_id=1, source_target_pairs={{0,16},{1,17},{2,18},{3,19},{4,20},{5,21},{6,22},{7,23},{8,24},{9,... | collective-permute-start | bytes 196616 | tf_op jit(solution)/shard_map/ppermute | solution.py:455
  34.8 1.7 %collective-permute-start.1 = (bf16[2,2,64,128]{3,2,1,0:T(8,128)(2,1)S(1)}, bf16[2,2,64,128]{3,2,1,0:T(8,128)(2,1)S(1)}, u32[]{:S(2)}, u32[]{:S(2)}) collective-permute-start(bf16[2,2,64,128]{3,2,1,0:T(8,128)(2,1)S(1)} %get-tuple-element.25), channel_id=1, source_target_pairs={{0,1},{1,0},{2,3},{3,2},{4,5},{5,4},{6,7},{7,6},{8,9},{9,8},{10,11... | collective-permute-start | bytes 196616 | tf_op jit(solution)/shard_map/ppermute | solution.py:455
  36.5 1.9 %collective-permute-done.from_even = bf16[2,2,64,128]{3,2,1,0:T(8,128)(2,1)S(1)} collective-permute-done((bf16[2,2,64,128]{3,2,1,0:T(8,128)(2,1)S(1)}, bf16[2,2,64,128]{3,2,1,0:T(8,128)(2,1)S(1)}, u32[]{:S(2)}, u32[]{:S(2)}) %collective-permute-start) | collective-permute-done | bytes 65568 | tf_op jit(solution)/shard_map/ppermute | solution.py:455
  38.4 4.3 %collective-permute-done.1.from_odd = bf16[2,2,64,128]{3,2,1,0:T(8,128)(2,1)S(1)} collective-permute-done((bf16[2,2,64,128]{3,2,1,0:T(8,128)(2,1)S(1)}, bf16[2,2,64,128]{3,2,1,0:T(8,128)(2,1)S(1)}, u32[]{:S(2)}, u32[]{:S(2)}) %collective-permute-start.1) | collective-permute-done | bytes 65568 | tf_op jit(solution)/shard_map/ppermute | solution.py:455
  42.8 0.1 collective-permute-start.2
  42.9 1.5 %collective-permute-start.3 = (bf16[7,64,128]{2,1,0:T(8,128)(2,1)S(1)}, bf16[7,64,128]{2,1,0:T(8,128)(2,1)S(1)}, u32[]{:S(2)}, u32[]{:S(2)}) collective-permute-start(bf16[7,64,128]{2,1,0:T(8,128)(2,1)S(1)} %get-tuple-element.27.own_odd), channel_id=1, source_target_pairs={{0,16},{1,2},{2,1},{3,4},{4,3},{5,6},{6,5},{7,8},{8,7},{9,10},{10,... | collective-permute-start | bytes 344072 | tf_op jit(solution)/shard_map/ppermute | solution.py:455
  44.4 2.1 %shard_map.89 = (bf16[4,7,64,128]{3,2,1,0:T(8,128)(2,1)S(1)}, f32[2,256,512]{2,1,0:T(8,128)S(1)}, f32[2,5,64,128]{3,2,1,0:T(8,128)S(1)}, f32[2,4,64,128]{3,2,1,0...) custom-call(f32[4,2,64,128]{3,2,1,0:T(8,128)S(1)} %get-tuple-element.22.whole, ...), custom_call_target="tpu_custom_call" | custom-call | flops 1400000000 | bytes 4000000 | tf_op jit(solution)/shard_map/pallas_call | solution.py:24
  46.5 0.0 collective-permute-done.2.from_even
  46.5 1.7 %collective-permute-done.3.from_odd = bf16[7,64,128]{2,1,0:T(8,128)(2,1)S(1)} collective-permute-done((bf16[7,64,128]{2,1,0:T(8,128)(2,1)S(1)}, bf16[7,64,128]{2,1,0:T(8,128)(2,1)S(1)}, u32[]{:S(2)}, u32[]{:S(2)}) %collective-permute-start.3) | collective-permute-done | bytes 114720 | tf_op jit(solution)/shard_map/ppermute | solution.py:455
  48.2 3.0 %shard_map.90 = (f32[4,4,64,512]{3,2,1,0:T(8,128)}, f32[256,256]{1,0:T(8,128)}) custom-call(f32[4,2,64,128]{3,2,1,0:T(8,128)S(1)} %get-tuple-element.22.whole, bf16[7,64,128]{2,1,0:T(8,128)(2,1)S(1)} %get-tuple-element.26.own_even, bf16[7,64,128]{2,1,0:T(8,128)(2,1)S(1)} %get-tuple-element.27.own_odd, ...), custom_call_target="tpu_custom_call" | custom-call | tf_op jit(solution)/shard_map/pallas_call | solution.py:24
  (3 shorter events, 0.1 us)
Async XLA Ops:
  4.1 10.4 %copy-start.1 = (f32[16,16,256]{2,1,0:T(8,128)S(1)}, f32[16,16,256]{2,1,0:T(8,128)}, u32[]{:S(2)}) copy-start(f32[16,16,256]{2,1,0:T(8,128)} %param.7) | copy-start | bytes 786436
  4.1 28.0 %all-to-all-start = ((s32[2176,1,128]{2,1,0:T(1,128)}), s32[2176,1,128]{2,1,0:T(1,128)S(1)}, u32[]{:S(2)}, u32[]{:S(2)}) async-start(s32[2176,1,128]{2,1,0:T(1,128)} %bitcast.18), calls=%async_computation | async-start | bytes 2228224 | tf_op jit(solution)/shard_map/all_to_all | solution.py:413
  14.5 1.0 %copy-start = (bf16[512,512]{1,0:T(8,128)(2,1)S(1)}, bf16[512,512]{1,0:T(8,128)(2,1)}, u32[]{:S(2)}) copy-start(bf16[512,512]{1,0:T(8,128)(2,1)} %param.13) | copy-start | bytes 1572868
  34.1 4.3 %collective-permute-start = (bf16[2,2,64,128]{3,2,1,0:T(8,128)(2,1)S(1)}, bf16[2,2,64,128]{3,2,1,0:T(8,128)(2,1)S(1)}, u32[]{:S(2)}, u32[]{:S(2)}) collective-permute-start(bf16[2,2,64,128]{3,2,1,0:T(8,128)(2,1)S(1)} %get-tuple-element.24), channel_id=1, source_target_pairs={{0,16},{1,17},{2,18},{3,19},{4,20},{5,21},{6,22},{7,23},{8,24},{9,... | collective-permute-start | bytes 196616 | tf_op jit(solution)/shard_map/ppermute | solution.py:455
  34.8 8.0 %collective-permute-start.1 = (bf16[2,2,64,128]{3,2,1,0:T(8,128)(2,1)S(1)}, bf16[2,2,64,128]{3,2,1,0:T(8,128)(2,1)S(1)}, u32[]{:S(2)}, u32[]{:S(2)}) collective-permute-start(bf16[2,2,64,128]{3,2,1,0:T(8,128)(2,1)S(1)} %get-tuple-element.25), channel_id=1, source_target_pairs={{0,1},{1,0},{2,3},{3,2},{4,5},{5,4},{6,7},{7,6},{8,9},{9,8},{10,11... | collective-permute-start | bytes 196616 | tf_op jit(solution)/shard_map/ppermute | solution.py:455
  42.8 3.7 %collective-permute-start.2 = (bf16[7,64,128]{2,1,0:T(8,128)(2,1)S(1)}, bf16[7,64,128]{2,1,0:T(8,128)(2,1)S(1)}, u32[]{:S(2)}, u32[]{:S(2)}) collective-permute-start(bf16[7,64,128]{2,1,0:T(8,128)(2,1)S(1)} %get-tuple-element.26.own_even), channel_id=1, source_target_pairs={{0,1},{1,0},{2,3},{3,2},{4,5},{5,4},{6,7},{7,6},{8,9},{9,8},{10,11... | collective-permute-start | bytes 344072 | tf_op jit(solution)/shard_map/ppermute | solution.py:455
  42.9 5.3 %collective-permute-start.3 = (bf16[7,64,128]{2,1,0:T(8,128)(2,1)S(1)}, bf16[7,64,128]{2,1,0:T(8,128)(2,1)S(1)}, u32[]{:S(2)}, u32[]{:S(2)}) collective-permute-start(bf16[7,64,128]{2,1,0:T(8,128)(2,1)S(1)} %get-tuple-element.27.own_odd), channel_id=1, source_target_pairs={{0,16},{1,2},{2,1},{3,4},{4,3},{5,6},{6,5},{7,8},{8,7},{9,10},{10,... | collective-permute-start | bytes 344072 | tf_op jit(solution)/shard_map/ppermute | solution.py:455

commit v7 on v6

--- a/solution.py
+++ b/solution.py
@@ -122,7 +122,7 @@
     return zero, one, two, three
 
 
-def merge_kernel(got, base, whole, half, to_even, to_odd, turned):
+def merge_kernel(got, base, to_odd, to_even, half, whole, turned):
     tiles = got.shape[0] // 128
     bin_row = lax.broadcasted_iota(jnp.int32, (256, 128), 0)
     tile, part, pair, odd = bin_row // 128, (bin_row // 32) % 2, (bin_row // 16) % 2, (bin_row // 64) % 2
@@ -173,7 +173,7 @@
     to_odd[...] = half[:, pl.ds(2 * odd_device, 2)]
 
 
-def assemble_kernel(half, from_even, from_odd, to_even, to_odd):
+def assemble_kernel(from_odd, from_even, half, to_odd, to_even):
     inline_at = lax.axis_index("inline")
     odd_row = lax.rem(inline_at, 2) == 1
     odd_col = lax.rem(lax.axis_index("xline"), 2)
@@ -288,7 +288,7 @@
 
 
 def sparse_kernel(
-    whole, own_even, own_odd, from_even, from_odd, inner, first_inner, recon_inner, rests, later_inner,
+    from_odd, from_even, whole, own_even, own_odd, inner, first_inner, recon_inner, rests, later_inner,
     codes_inner, words, words_back, codes, residual, outer, later, turned, binned, made_codes, flat_rest, leave
 ):
     stores = [pltpu.make_async_copy(codes_inner, codes.at[:, 1], leave.at[0])]
@@ -423,13 +423,13 @@
     )
     got, base, words, words_back = lax.optimization_barrier((got, base, words, words_back))
     pair_shape = lambda *lead: jax.ShapeDtypeStruct(lead + (64, 128), jnp.bfloat16)
-    whole, half, to_even, to_odd = call_kernel(
+    to_odd, to_even, half, whole = call_kernel(
         merge_kernel,
         (
-            jax.ShapeDtypeStruct((4, 2, 64, 128), jnp.float32),
-            pair_shape(2, 4),
             pair_shape(2, 2),
             pair_shape(2, 2),
+            pair_shape(2, 4),
+            jax.ShapeDtypeStruct((4, 2, 64, 128), jnp.float32),
         ),
         (pltpu.VMEM,) * 4,
         [
@@ -456,13 +456,13 @@
 
     from_odd = swapped(to_odd, True, 1)
     from_even = swapped(to_even, True, 0)
-    own_even, own_odd = call_kernel(
+    own_odd, own_even = call_kernel(
         assemble_kernel,
         (pair_shape(7), pair_shape(7)),
         (pltpu.VMEM,) * 2,
         [],
         pltpu.VMEM,
-        [half, from_even, from_odd],
+        [from_odd, from_even, half],
     )
     from_odd = swapped(own_odd, False, 1)
     from_even = swapped(own_even, False, 0)
@@ -498,7 +498,7 @@
         ],
         pltpu.VMEM,
         [
-            whole, own_even, own_odd, from_even, from_odd, inner, first, recon, rests, later,
+            from_odd, from_even, whole, own_even, own_odd, inner, first, recon, rests, later,
             codes_inner, words, words_back,
         ],
     )

time: 52.2 us -> 50.7 us (0.971); the launches traced: 51.2 us -> 50.4 us
  starting transfers between devices: 14.3 us -> 13.7 us
    ppermute x4, starting transfers between devices: 3.98 us -> 3.37 us  [swapped(): return lax.ppermute(block, ('inline', 'xline'), route)]
  transfers between devices with their start and end apart: 5 -> 5, of which waited for: 4 -> 3; matrix products, arithmetic and copies ran while one was open for 2% -> 2% of each run, Pallas kernels for 4% -> 4%
where the time goes in v7:
time: 50.7 us; the launch traced here: 50.4 us
  waiting for transfers between devices  23.4 us (46%)
  starting transfers between devices  13.7 us (27%)
  Pallas kernels  10.7 us (21%)
  local copies, waits for them, and re-layouts  1.75 us (3%)
  between operations  0.75 us (1%)
    all_to_all x1, waiting for transfers between devices, body(): lax.all_to_all(sent.reshape(send_rows, 1, 128), ('inline', 'xline'), spli...  15.7 us
    pallas_call x5, Pallas kernels, call_kernel(): pl.pallas_call(kernel, out_shape=out_shape, in_specs=[pl.BlockSpec(memory...  10.7 us
    all_to_all x1, starting transfers between devices, body(): lax.all_to_all(sent.reshape(send_rows, 1, 128), ('inline', 'xline'), spli...  10.4 us
    ppermute x4, waiting for transfers between devices, swapped(): return lax.ppermute(block, ('inline', 'xline'), route)  7.67 us
    ppermute x4, starting transfers between devices, swapped(): return lax.ppermute(block, ('inline', 'xline'), route)  3.37 us
  transfers between devices with their start and end apart: 5, of which 3 were waited for; matrix products, arithmetic and copies ran while one was open for 2% of the time, Pallas kernels for 4%

profile of v7, /device:TPU:14, one launch (start us, length us, event | category | flops | bytes accessed | tf_op | source)
XLA Modules:
  0.0 50.4 jit_solution(14308507821069607363)
XLA Ops:
  0.6 3.4 %shard_map.86 = s32[2176,128]{1,0:T(8,128)} custom-call(f32[4]{0:T(128)} %gains_in.1, f32[1024,256]{1,0:T(8,128)} %traces_in.1, s32[1,1024]{1,0:T(1,128)} %bitcast.21, s32[1,1024]{1,0:T(1,128)} %bitcast.22, s32[1,1024]{1,0:T(1,128)} %bitcast.23), custom_call_target="tpu_custom_call" | custom-call | tf_op jit(solution)/shard_map/pallas_call | solution.py:24
  4.1 0.0 copy-start.1
  4.1 10.4 %all-to-all-start = ((s32[2176,1,128]{2,1,0:T(1,128)}), s32[2176,1,128]{2,1,0:T(1,128)S(1)}, u32[]{:S(2)}, u32[]{:S(2)}) async-start(s32[2176,1,128]{2,1,0:T(1,128)} %bitcast.18), calls=%async_computation | async-start | bytes 2228224 | tf_op jit(solution)/shard_map/all_to_all | solution.py:413
  14.5 0.0 copy-done.1
  14.5 0.0 copy-start
  14.5 0.1 reshape.39
  14.6 0.1 reshape.40.base
  14.7 0.8 %copy-done = bf16[512,512]{1,0:T(8,128)(2,1)S(1)} copy-done((bf16[512,512]{1,0:T(8,128)(2,1)S(1)}, bf16[512,512]{1,0:T(8,128)(2,1)}, u32[]{:S(2)}) %copy-start) | copy-done | bytes 524312
  15.5 0.1 reshape.41
  15.7 0.3 copy.22
  15.9 0.1 reshape.42
  16.1 0.2 copy.19
  16.3 15.7 %all-to-all-done = s32[2176,1,128]{2,1,0:T(1,128)S(1)} async-done(((s32[2176,1,128]{2,1,0:T(1,128)}), s32[2176,1,128]{2,1,0:T(1,128)S(1)}, u32[]{:S(2)}, u32[]{:S(2)}) %all-to-all-start) | async-done | bytes 1114144 | tf_op jit(solution)/shard_map/all_to_all | solution.py:413
  32.1 2.0 %shard_map.87 = (bf16[2,2,64,128]{3,2,1,0:T(8,128)(2,1)S(1)}, bf16[2,2,64,128]{3,2,1,0:T(8,128)(2,1)S(1)}, bf16[2,4,64,128]{3,2,1,0:T(8,128)(2,1)S(1)}, f32[4,2,64,128]{3,2,1,0:T(8,128)S(1)}) custom-call(s32[2176,128]{1,0:T(8,128)S(1)} %bitcast.15, f32[256,256]{1,0:T(8,128)S(1)} %reshape.40.base), custom_call_target="tpu_custom_call" | custom-call | tf_op jit(solution)/shard_map/pallas_call | solution.py:24
  34.1 2.3 %collective-permute-start = (bf16[2,2,64,128]{3,2,1,0:T(8,128)(2,1)S(1)}, bf16[2,2,64,128]{3,2,1,0:T(8,128)(2,1)S(1)}, u32[]{:S(2)}, u32[]{:S(2)}) collective-permute-start(bf16[2,2,64,128]{3,2,1,0:T(8,128)(2,1)S(1)} %get-tuple-element.22), channel_id=1, source_target_pairs={{0,1},{1,0},{2,3},{3,2},{4,5},{5,4},{6,7},{7,6},{8,9},{9,8},{10,11... | collective-permute-start | bytes 196616 | tf_op jit(solution)/shard_map/ppermute | solution.py:455
  36.4 0.0 collective-permute-start.1
  36.4 5.7 %collective-permute-done.from_odd = bf16[2,2,64,128]{3,2,1,0:T(8,128)(2,1)S(1)} collective-permute-done((bf16[2,2,64,128]{3,2,1,0:T(8,128)(2,1)S(1)}, bf16[2,2,64,128]{3,2,1,0:T(8,128)(2,1)S(1)}, u32[]{:S(2)}, u32[]{:S(2)}) %collective-permute-start) | collective-permute-done | bytes 65568 | tf_op jit(solution)/shard_map/ppermute | solution.py:455
  42.0 0.0 collective-permute-done.1.from_even
  42.1 0.1 collective-permute-start.2
  42.2 1.0 %collective-permute-start.3 = (bf16[7,64,128]{2,1,0:T(8,128)(2,1)S(1)}, bf16[7,64,128]{2,1,0:T(8,128)(2,1)S(1)}, u32[]{:S(2)}, u32[]{:S(2)}) collective-permute-start(bf16[7,64,128]{2,1,0:T(8,128)(2,1)S(1)} %get-tuple-element.26.own_even), channel_id=1, source_target_pairs={{0,1},{1,0},{2,3},{3,2},{4,5},{5,4},{6,7},{7,6},{8,9},{9,8},{10,11... | collective-permute-start | bytes 344072 | tf_op jit(solution)/shard_map/ppermute | solution.py:455
  43.1 2.1 %shard_map.89 = (bf16[4,7,64,128]{3,2,1,0:T(8,128)(2,1)S(1)}, f32[2,256,512]{2,1,0:T(8,128)S(1)}, f32[2,5,64,128]{3,2,1,0:T(8,128)S(1)}, f32[2,4,64,128]{3,2,1,0...) custom-call(f32[4,2,64,128]{3,2,1,0:T(8,128)S(1)} %get-tuple-element.27.whole, ...), custom_call_target="tpu_custom_call" | custom-call | flops 1400000000 | bytes 4000000 | tf_op jit(solution)/shard_map/pallas_call | solution.py:24
  45.3 2.0 %collective-permute-done.2.from_odd = bf16[7,64,128]{2,1,0:T(8,128)(2,1)S(1)} collective-permute-done((bf16[7,64,128]{2,1,0:T(8,128)(2,1)S(1)}, bf16[7,64,128]{2,1,0:T(8,128)(2,1)S(1)}, u32[]{:S(2)}, u32[]{:S(2)}) %collective-permute-start.2) | collective-permute-done | bytes 114720 | tf_op jit(solution)/shard_map/ppermute | solution.py:455
  47.3 0.0 collective-permute-done.3.from_even
  47.3 3.1 %shard_map.90 = (f32[4,4,64,512]{3,2,1,0:T(8,128)}, f32[256,256]{1,0:T(8,128)}) custom-call(bf16[7,64,128]{2,1,0:T(8,128)(2,1)S(1)} %collective-permute-done.2.from_odd, bf16[7,64,128]{2,1,0:T(8,128)(2,1)S(1)} %collective-permute-done.3.from_even, f32[4,2,64,128]{3,2,1,0:T(8,128)S(1)} %get-tuple-element.27.whole, ...), custom_call_target="tpu_custom_call" | custom-call | tf_op jit(solution)/shard_map/pallas_call | solution.py:24
  (3 shorter events, 0.1 us)
Async XLA Ops:
  4.1 10.4 %copy-start.1 = (f32[16,16,256]{2,1,0:T(8,128)S(1)}, f32[16,16,256]{2,1,0:T(8,128)}, u32[]{:S(2)}) copy-start(f32[16,16,256]{2,1,0:T(8,128)} %param.7) | copy-start | bytes 786436
  4.1 28.0 %all-to-all-start = ((s32[2176,1,128]{2,1,0:T(1,128)}), s32[2176,1,128]{2,1,0:T(1,128)S(1)}, u32[]{:S(2)}, u32[]{:S(2)}) async-start(s32[2176,1,128]{2,1,0:T(1,128)} %bitcast.18), calls=%async_computation | async-start | bytes 2228224 | tf_op jit(solution)/shard_map/all_to_all | solution.py:413
  14.5 1.0 %copy-start = (bf16[512,512]{1,0:T(8,128)(2,1)S(1)}, bf16[512,512]{1,0:T(8,128)(2,1)}, u32[]{:S(2)}) copy-start(bf16[512,512]{1,0:T(8,128)(2,1)} %param.13) | copy-start | bytes 1572868
  34.1 8.0 %collective-permute-start = (bf16[2,2,64,128]{3,2,1,0:T(8,128)(2,1)S(1)}, bf16[2,2,64,128]{3,2,1,0:T(8,128)(2,1)S(1)}, u32[]{:S(2)}, u32[]{:S(2)}) collective-permute-start(bf16[2,2,64,128]{3,2,1,0:T(8,128)(2,1)S(1)} %get-tuple-element.22), channel_id=1, source_target_pairs={{0,1},{1,0},{2,3},{3,2},{4,5},{5,4},{6,7},{7,6},{8,9},{9,8},{10,11... | collective-permute-start | bytes 196616 | tf_op jit(solution)/shard_map/ppermute | solution.py:455
  36.4 5.7 %collective-permute-start.1 = (bf16[2,2,64,128]{3,2,1,0:T(8,128)(2,1)S(1)}, bf16[2,2,64,128]{3,2,1,0:T(8,128)(2,1)S(1)}, u32[]{:S(2)}, u32[]{:S(2)}) collective-permute-start(bf16[2,2,64,128]{3,2,1,0:T(8,128)(2,1)S(1)} %get-tuple-element.23), channel_id=1, source_target_pairs={{0,16},{1,17},{2,18},{3,19},{4,20},{5,21},{6,22},{7,23},{8,24},{9,... | collective-permute-start | bytes 196616 | tf_op jit(solution)/shard_map/ppermute | solution.py:455
  42.1 5.2 %collective-permute-start.2 = (bf16[7,64,128]{2,1,0:T(8,128)(2,1)S(1)}, bf16[7,64,128]{2,1,0:T(8,128)(2,1)S(1)}, u32[]{:S(2)}, u32[]{:S(2)}) collective-permute-start(bf16[7,64,128]{2,1,0:T(8,128)(2,1)S(1)} %get-tuple-element.25.own_odd), channel_id=1, source_target_pairs={{0,16},{1,2},{2,1},{3,4},{4,3},{5,6},{6,5},{7,8},{8,7},{9,10},{10,... | collective-permute-start | bytes 344072 | tf_op jit(solution)/shard_map/ppermute | solution.py:455
  42.2 5.1 %collective-permute-start.3 = (bf16[7,64,128]{2,1,0:T(8,128)(2,1)S(1)}, bf16[7,64,128]{2,1,0:T(8,128)(2,1)S(1)}, u32[]{:S(2)}, u32[]{:S(2)}) collective-permute-start(bf16[7,64,128]{2,1,0:T(8,128)(2,1)S(1)} %get-tuple-element.26.own_even), channel_id=1, source_target_pairs={{0,1},{1,0},{2,3},{3,2},{4,5},{5,4},{6,7},{7,6},{8,9},{9,8},{10,11... | collective-permute-start | bytes 344072 | tf_op jit(solution)/shard_map/ppermute | solution.py:455

commit v8 on v7

--- a/solution.py
+++ b/solution.py
@@ -122,7 +122,7 @@
     return zero, one, two, three
 
 
-def merge_kernel(got, base, to_odd, to_even, half, whole, turned):
+def merge_kernel(got, base, to_odd, to_even, side_odd, side_even, half, whole, turned):
     tiles = got.shape[0] // 128
     bin_row = lax.broadcasted_iota(jnp.int32, (256, 128), 0)
     tile, part, pair, odd = bin_row // 128, (bin_row // 32) % 2, (bin_row // 16) % 2, (bin_row // 64) % 2
@@ -171,19 +171,21 @@
     odd_device = lax.rem(lax.axis_index("inline"), 2)
     to_even[...] = half[:, pl.ds(2 - 2 * odd_device, 2)]
     to_odd[...] = half[:, pl.ds(2 * odd_device, 2)]
-
-
-def assemble_kernel(from_odd, from_even, half, to_odd, to_even):
+    odd_device = lax.rem(lax.axis_index("xline"), 2)
+    side_even[...] = half[1 - odd_device]
+    side_odd[...] = half[odd_device]
+
+
+def assemble_kernel(from_odd, from_even, to_odd, to_even):
     inline_at = lax.axis_index("inline")
     odd_row = lax.rem(inline_at, 2) == 1
     odd_col = lax.rem(lax.axis_index("xline"), 2)
+    last = inline_at == lax.axis_size("inline") - 1
     for target, pair in ((to_even, 1 - odd_col), (to_odd, odd_col)):
         above = jnp.where(odd_row, from_even[pair, 1], from_odd[pair, 1])
         target[0] = jnp.where(inline_at == 0, jnp.zeros_like(above), above)
-        target[1:5] = half[pair]
         below = jnp.where(odd_row, from_odd[pair], from_even[pair])
-        last = inline_at == lax.axis_size("inline") - 1
-        target[5:7] = jnp.where(last, jnp.zeros_like(below), below)
+        target[1:3] = jnp.where(last, jnp.zeros_like(below), below)
 
 
 def time_rolled(values, distance):
@@ -201,32 +203,63 @@
     return even.astype(jnp.bfloat16), odd.astype(jnp.bfloat16)
 
 
-def correlated(near, far, words, first_row, count):
+def correlated(patches, block, words):
     lhs = [
-        source[first_row + shift : first_row + shift + count].reshape(count * 64, 128)
-        for shift in (0, 1)
-        for source in (near, far)
+        jnp.concatenate(
+            [block(row + down, col + right) for down in (0, 1) for right in (0, 1)], axis=1
+        )
+        for row, col in patches
     ]
-    return jnp.dot(jnp.concatenate(lhs, axis=1), words[...], preferred_element_type=jnp.float32)
-
-
-def given_back(found, words_back, sides):
-    given = {}
-    for side in sides:
-        for shift in (0, 1):
-            at = 256 * shift + 128 * side
-            given[shift, side] = at
-    columns = {}
-    if len(sides) == 2:
-        full = jnp.dot(found, words_back[...], preferred_element_type=jnp.float32)
-        for key, at in given.items():
-            columns[key] = full[:, at : at + 128].reshape(6, 64, 128)
-    else:
-        picked = jnp.concatenate([words_back[:, at : at + 128] for at in given.values()], axis=1)
-        full = jnp.dot(found, picked, preferred_element_type=jnp.float32)
-        for number, key in enumerate(given):
-            columns[key] = full[:, 128 * number : 128 * number + 128].reshape(6, 64, 128)
-    return [columns[0, side][1:6] + columns[1, side][0:5] for side in sides]
+    return jnp.dot(jnp.concatenate(lhs, axis=0), words[...], preferred_element_type=jnp.float32)
+
+
+def first_codes(patches, block, words, words_back, sums, not_top=1.0, not_left=1.0):
+    found = shrink_codes(correlated(patches, block, words))
+    pieces = [found[64 * number : 64 * number + 64] for number in range(len(patches))]
+    masked = []
+    for (row, col), piece in zip(patches, pieces):
+        piece = piece * not_top if row < 0 else piece
+        masked.append((piece * not_left if col < 0 else piece).astype(jnp.bfloat16))
+    given = jnp.dot(
+        jnp.concatenate(masked, axis=0), words_back[...], preferred_element_type=jnp.float32
+    )
+    for number, (row, col) in enumerate(patches):
+        for down in (0, 1):
+            for right in (0, 1):
+                spot = (row + down, col + right)
+                if 0 <= spot[0] <= 4 and 0 <= spot[1] <= 4:
+                    at = 128 * (2 * down + right)
+                    part = given[64 * number : 64 * number + 64, at : at + 128]
+                    sums[spot] = sums[spot] + part if spot in sums else part
+    return dict(zip(patches, pieces))
+
+
+def last_codes(before, column, block, words):
+    patches = [(row, column) for row in range(4)]
+    found = jnp.concatenate(before, axis=0) + correlated(patches, block, words)
+    return shrink_codes(found).reshape(4, 64, 512)
+
+
+outer_spot = {-1: 0, 4: 1, 5: 2}
+late_first = ((3, 0), (3, 1), (3, 2), (0, 3), (1, 3), (2, 3))
+
+
+def chosen(pair, odd_pairs, even_pairs):
+    odd_device = lax.rem(lax.axis_index("xline"), 2) == 1
+    if pair in (-1, 0):
+        return lambda row: jnp.where(odd_device, even_pairs[row], odd_pairs[row]).astype(jnp.float32)
+    return lambda row: jnp.where(odd_device, odd_pairs[row], even_pairs[row]).astype(jnp.float32)
+
+
+def edge_masks():
+    inline_at, xline_at = lax.axis_index("inline"), lax.axis_index("xline")
+    at_edge = (
+        inline_at == 0,
+        inline_at == lax.axis_size("inline") - 1,
+        xline_at == 0,
+        xline_at == lax.axis_size("xline") - 1,
+    )
+    return [jnp.where(edge, 0.0, 1.0) for edge in at_edge]
 
 
 def rebuilt_half(given, odd):
@@ -242,119 +275,147 @@
     return jnp.where(left, block, pltpu.roll(later, 64, 1)).astype(jnp.bfloat16)
 
 
-def first_codes(near, far, words, not_top):
-    found = shrink_codes(correlated(near, far, words, 0, 6))
-    return found[64:320], jnp.concatenate([found[:64] * not_top, found[64:]], axis=0)
-
-
-def last_codes(before, near, far, words):
-    return shrink_codes(before + correlated(near, far, words, 0, 4)).reshape(4, 64, 512)
-
-
-def inner_kernel(whole, own_even, own_odd, words, words_back, field, first, recon, rests, later, made_codes):
-    inline_at = lax.axis_index("inline")
-    not_top = jnp.where(inline_at == 0, 0.0, 1.0)
-    not_bottom = jnp.where(inline_at == lax.axis_size("inline") - 1, 0.0, 1.0)
-    odd_device = lax.rem(lax.axis_index("xline"), 2) == 1
-
-    def loaded(pair, block_row):
-        if_even, if_odd = ((own_odd, own_even), (own_even, own_odd))[pair]
-        return jnp.where(odd_device, if_odd[block_row], if_even[block_row]).astype(jnp.float32)
-
+def inner_kernel(half, words, words_back, field, first, recon):
     for pair in range(2):
-        for block_row in range(7):
-            even, odd = widened(loaded(pair, block_row))
-            field[2 * pair, block_row] = even
-            field[2 * pair + 1, block_row] = odd
-    kept, found = zip(
-        *(first_codes(field.at[at], field.at[at + 1], words, not_top) for at in range(3))
-    )
-    given = [given_back(part.astype(jnp.bfloat16), words_back, (0, 1)) for part in found]
-    recon[0] = given[0][0]
-    recon[1] = given[2][1]
-    for column in (1, 2):
-        pair, odd = column // 2, column % 2
-        for block_row in range(5):
-            rebuilt = rebuilt_half(given[column][0][block_row] + given[column - 1][1][block_row], odd)
-            if block_row < 4:
-                rest = whole[block_row, pair] - rebuilt
-                rests[column - 1, block_row] = rest
+        for row in range(4):
+            even, odd = widened(half[pair, row].astype(jnp.float32))
+            field[2 * pair, row] = even
+            field[2 * pair + 1, row] = odd
+    sums = {}
+    patches = [(row, col) for col in range(3) for row in range(3)]
+    found = first_codes(patches, lambda row, col: field[col, row], words, words_back, sums)
+    for (row, col), piece in found.items():
+        first[col, row] = piece
+    for (row, col), part in sums.items():
+        recon[col, row] = part
+
+
+def side_kernel(
+    side_odd, side_even, edge_odd, edge_even, whole, inner, first_inner, recon_inner, words, words_back,
+    field_edge, field_side, first, recon, rests, later, made_codes
+):
+    not_top, not_bottom, not_left, not_right = edge_masks()
+    for pair in range(2):
+        load = chosen(pair, edge_odd, edge_even)
+        for number in range(3):
+            even, odd = widened(load(number))
+            field_edge[2 * pair, number] = even
+            field_edge[2 * pair + 1, number] = odd
+    left, right = chosen(-1, side_odd, side_even), chosen(2, side_odd, side_even)
+    for row in range(4):
+        field_side[0, row] = widened(left(row) * not_left)[1]
+        even, odd = widened(right(row) * not_right)
+        field_side[1, row] = even
+        field_side[2, row] = odd
+
+    def block(row, col):
+        if 0 <= col <= 3:
+            return inner[col, row] if 0 <= row <= 3 else field_edge[col, outer_spot[row]]
+        return field_side[outer_spot[col], row]
+
+    sums = {(row, col): recon_inner[col, row] for row in range(4) for col in range(4)}
+    patches = [(row, col) for col in range(3) for row in (-1, 3, 4)]
+    patches += [(row, col) for col in (-1, 3, 4) for row in range(3)]
+    found = first_codes(patches, block, words, words_back, sums, not_top, not_left)
+    for number, spot in enumerate(late_first):
+        first[number] = found[spot]
+    for number, col in enumerate((0, 3, 4)):
+        for row in range(5):
+            if (row, col) != (4, 4):
+                recon[number, row] = sums[row, col]
+    for col in (1, 2):
+        pair, odd = col // 2, col % 2
+        load = chosen(pair, edge_odd, edge_even)
+        for row in range(5):
+            rebuilt = rebuilt_half(sums[row, col], odd)
+            if row < 4:
+                rest = whole[row, pair] - rebuilt
+                rests[col - 1, row] = rest
             else:
-                rest = (loaded(pair, 5) - rebuilt) * not_bottom
-            later[column - 1, block_row] = widened_half(rest, odd)
-    first[0] = kept[0]
-    first[1] = kept[2]
-    made_codes[...] = last_codes(kept[1], later.at[0], later.at[1], words)
+                rest = (load(1) - rebuilt) * not_bottom
+            later[col - 1, row] = widened_half(rest, odd)
+    before = [first_inner[1, row] for row in range(3)] + [found[3, 1]]
+    made_codes[...] = last_codes(before, 1, lambda row, col: later[col - 1, row], words)
 
 
 def sparse_kernel(
-    from_odd, from_even, whole, own_even, own_odd, inner, first_inner, recon_inner, rests, later_inner,
-    codes_inner, words, words_back, codes, residual, outer, later, turned, binned, made_codes, flat_rest, leave
+    corner_odd, corner_even, side_odd, side_even, edge_odd, edge_even, whole, inner, field_edge, field_side,
+    first_inner, first_side, recon_side, rests, later_inner, codes_inner, words, words_back,
+    codes, residual, field_corner, later, turned, binned, made_codes, flat_rest, leave
 ):
     stores = [pltpu.make_async_copy(codes_inner, codes.at[:, 1], leave.at[0])]
     stores[0].start()
-    inline_at, xline_at = lax.axis_index("inline"), lax.axis_index("xline")
-    inline_last = inline_at == lax.axis_size("inline") - 1
-    xline_last = xline_at == lax.axis_size("xline") - 1
-    not_top = jnp.where(inline_at == 0, 0.0, 1.0)
-    not_left = jnp.where(xline_at == 0, 0.0, 1.0)
-    not_bottom = jnp.where(inline_last, 0.0, 1.0)
-    not_right = jnp.where(xline_last, 0.0, 1.0)
-
-    odd_device = lax.rem(xline_at, 2) == 1
-    sources = ((from_odd, from_even), (own_odd, own_even), (own_even, own_odd), (from_even, from_odd))
-    edges = (not_left, None, None, not_right)
-
-    def loaded(pair, block_row):
-        if_even, if_odd = sources[pair]
-        both = jnp.where(odd_device, if_odd[block_row], if_even[block_row]).astype(jnp.float32)
-        return both if edges[pair] is None else both * edges[pair]
+    not_top, not_bottom, not_left, not_right = edge_masks()
 
     def leaving(column, made):
-        made_codes[len(stores) - 1] = made
+        number = len(stores)
+        made_codes[number - 1] = made
         for part in range(2 if column == 3 else 1):
             rows = pl.ds(2 * part, 2) if column == 3 else pl.ds(0, 4)
             stores.append(
                 pltpu.make_async_copy(
-                    made_codes.at[len(stores) - 1 - part, rows],
-                    codes.at[rows, column],
-                    leave.at[len(stores)],
+                    made_codes.at[number - 1, rows], codes.at[rows, column], leave.at[len(stores)]
                 )
             )
             stores[-1].start()
 
-    def rest_of(column, given, spot):
-        pair, odd = column // 2, column % 2
-        for block_row in range(5):
-            rebuilt = rebuilt_half(given[block_row], odd)
-            if column == 4:
-                rest = (loaded(3, block_row + 1) - rebuilt) * not_right
-            elif block_row < 4:
-                rest = whole[block_row, pair] - rebuilt
-                binned[pair, block_row] = rest
+    left, right = chosen(-1, corner_odd, corner_even), chosen(2, corner_odd, corner_even)
+    for number in range(3):
+        field_corner[0, number] = widened(left(number) * not_left)[1]
+        even, odd = widened(right(number) * not_right)
+        field_corner[1, number] = even
+        field_corner[2, number] = odd
+
+    def block(row, col):
+        if 0 <= col <= 3:
+            return inner[col, row] if 0 <= row <= 3 else field_edge[col, outer_spot[row]]
+        if 0 <= row <= 3:
+            return field_side[outer_spot[col], row]
+        return field_corner[outer_spot[col], outer_spot[row]]
+
+    sums = {
+        (row, col): recon_side[number, row]
+        for number, col in enumerate((0, 3, 4))
+        for row in range(5)
+        if (row, col) != (4, 4)
+    }
+    patches = [(row, col) for col in (-1, 3, 4) for row in (-1, 3, 4)]
+    found = first_codes(patches, block, words, words_back, sums, not_top, not_left)
+
+    late_spot = {0: 0, 3: 1, 4: 2}
+
+    def rest_of(col):
+        pair, odd = col // 2, col % 2
+        for row in range(5):
+            rebuilt = rebuilt_half(sums[row, col], odd)
+            if col == 4:
+                source = chosen(2, side_odd, side_even)(row) if row < 4 else right(1)
+                rest = (source - rebuilt) * not_right
+            elif row < 4:
+                rest = whole[row, pair] - rebuilt
+                binned[pair, row] = rest
             else:
-                rest = loaded(pair + 1, 5) - rebuilt
-            if block_row == 4:
+                rest = chosen(pair, edge_odd, edge_even)(1) - rebuilt
+            if row == 4:
                 rest = rest * not_bottom
-            later[spot, block_row] = widened_half(rest, odd)
-
-    for block_row in range(7):
-        outer[0, block_row] = widened(loaded(0, block_row))[1]
-        even, odd = widened(loaded(3, block_row))
-        outer[1, block_row] = even
-        outer[2, block_row] = odd
-    unused, left_found = first_codes(outer.at[0], inner.at[0], words, not_top)
-    kept, middle = first_codes(inner.at[3], outer.at[1], words, not_top)
-    unused, right_found = first_codes(outer.at[1], outer.at[2], words, not_top)
-    (left_far,) = given_back((left_found * not_left).astype(jnp.bfloat16), words_back, (1,))
-    near, far = given_back(middle.astype(jnp.bfloat16), words_back, (0, 1))
-    (right_near,) = given_back(right_found.astype(jnp.bfloat16), words_back, (0,))
-    rest_of(0, recon_inner[0] + left_far, 0)
-    rest_of(3, recon_inner[1] + near, 1)
-    rest_of(4, far + right_near, 2)
-    leaving(0, last_codes(first_inner[0], later.at[0], later_inner.at[0], words))
-    leaving(2, last_codes(first_inner[1], later_inner.at[1], later.at[1], words))
-    leaving(3, last_codes(kept, later.at[1], later.at[2], words))
+            later[late_spot[col], row] = widened_half(rest, odd)
+
+    def rest_block(row, col):
+        if col in (1, 2):
+            return later_inner[col - 1, row]
+        return later[late_spot[col], row]
+
+    def before(col):
+        if col == 3:
+            return [first_side[3 + row] for row in range(3)] + [found[3, 3]]
+        return [first_inner[col, row] for row in range(3)] + [first_side[col]]
+
+    rest_of(0)
+    rest_of(3)
+    rest_of(4)
+    for column in (0, 2, 3):
+        leaving(column, last_codes(before(column), column, rest_block, words))
+
     left = lax.broadcasted_iota(jnp.int32, (64, 128), 1) < 64
     for block_row in range(4):
         binned[0, block_row] = jnp.where(left, binned[0, block_row], rests[0, block_row])
@@ -422,19 +483,20 @@
         .reshape(256, time_len)
     )
     got, base, words, words_back = lax.optimization_barrier((got, base, words, words_back))
+    full_shape = lambda *shape: jax.ShapeDtypeStruct(shape, jnp.float32)
     pair_shape = lambda *lead: jax.ShapeDtypeStruct(lead + (64, 128), jnp.bfloat16)
-    to_odd, to_even, half, whole = call_kernel(
+    to_odd, to_even, side_odd, side_even, half, whole = call_kernel(
         merge_kernel,
         (
             pair_shape(2, 2),
             pair_shape(2, 2),
+            pair_shape(4),
+            pair_shape(4),
             pair_shape(2, 4),
-            jax.ShapeDtypeStruct((4, 2, 64, 128), jnp.float32),
+            full_shape(4, 2, 64, 128),
         ),
-        (pltpu.VMEM,) * 4,
-        [
-            pltpu.VMEM((2, 256, 128), jnp.float32),
-        ],
+        (pltpu.VMEM,) * 6,
+        [pltpu.VMEM((2, 256, 128), jnp.float32)],
         pltpu.VMEM,
         [got, base],
     )
@@ -456,31 +518,45 @@
 
     from_odd = swapped(to_odd, True, 1)
     from_even = swapped(to_even, True, 0)
-    own_odd, own_even = call_kernel(
+    side_odd = swapped(side_odd, False, 1)
+    side_even = swapped(side_even, False, 0)
+    inner, first_inner, recon_inner = call_kernel(
+        inner_kernel,
+        (pair_shape(4, 4), full_shape(3, 3, 64, 512), full_shape(4, 4, 64, 128)),
+        (pltpu.VMEM,) * 3,
+        [],
+        pltpu.VMEM,
+        [half, words, words_back],
+        cost=pl.CostEstimate(flops=600_000_000, bytes_accessed=2_000_000, transcendentals=0),
+    )
+    edge_odd, edge_even = call_kernel(
         assemble_kernel,
-        (pair_shape(7), pair_shape(7)),
+        (pair_shape(3), pair_shape(3)),
         (pltpu.VMEM,) * 2,
         [],
         pltpu.VMEM,
-        [from_odd, from_even, half],
-    )
-    from_odd = swapped(own_odd, False, 1)
-    from_even = swapped(own_even, False, 0)
-    full_shape = lambda *shape: jax.ShapeDtypeStruct(shape, jnp.float32)
-    inner, first, recon, rests, later, codes_inner = call_kernel(
-        inner_kernel,
+        [from_odd, from_even],
+    )
+    corner_odd = swapped(edge_odd, False, 1)
+    corner_even = swapped(edge_even, False, 0)
+    field_edge, field_side, first_side, recon_side, rests, later, codes_inner = call_kernel(
+        side_kernel,
         (
-            pair_shape(4, 7),
-            full_shape(2, 256, 512),
-            full_shape(2, 5, 64, 128),
+            pair_shape(4, 3),
+            pair_shape(3, 4),
+            full_shape(6, 64, 512),
+            full_shape(3, 5, 64, 128),
             full_shape(2, 4, 64, 128),
             pair_shape(2, 5),
             full_shape(4, 64, 512),
         ),
-        (pltpu.VMEM,) * 6,
+        (pltpu.VMEM,) * 7,
         [],
         pltpu.VMEM,
-        [whole, own_even, own_odd, words, words_back],
+        [
+            side_odd, side_even, edge_odd, edge_even, whole, inner, first_inner, recon_inner, words,
+            words_back,
+        ],
         cost=pl.CostEstimate(flops=1_400_000_000, bytes_accessed=4_000_000, transcendentals=0),
     )
     codes, residual = call_kernel(
@@ -488,7 +564,7 @@
         (full_shape(4, 4, 64, 512), full_shape(256, time_len)),
         (pltpu.HBM, pltpu.HBM),
         [
-            pltpu.VMEM((3, 7, 64, 128), jnp.bfloat16),
+            pltpu.VMEM((3, 3, 64, 128), jnp.bfloat16),
             pltpu.VMEM((3, 5, 64, 128), jnp.bfloat16),
             pltpu.VMEM((2, 256, 128), jnp.float32),
             pltpu.VMEM((2, 4, 64, 128), jnp.float32),
@@ -498,8 +574,8 @@
         ],
         pltpu.VMEM,
         [
-            from_odd, from_even, whole, own_even, own_odd, inner, first, recon, rests, later,
-            codes_inner, words, words_back,
+            corner_odd, corner_even, side_odd, side_even, edge_odd, edge_even, whole, inner, field_edge,
+            field_side, first_inner, first_side, recon_side, rests, later, codes_inner, words, words_back,
         ],
     )
     return codes, residual.reshape(16, 16, time_len)

time: 50.7 us -> 50.3 us (level)
  waiting for transfers between devices: 23.4 us -> 20.2 us
  Pallas kernels: 10.7 us -> 12.2 us
  starting transfers between devices: 13.7 us -> 14.6 us
    ppermute x4 -> x6, waiting for transfers between devices: 7.67 us -> 4.46 us  [swapped(): return lax.ppermute(block, ('inline', 'xline'), route)]
    pallas_call x5 -> x6, Pallas kernels: 10.7 us -> 12.2 us  [call_kernel(): pl.pallas_call(kernel, out_shape=out_shape, in_specs=[pl.BlockSpec(memory...]
    ppermute x4 -> x6, starting transfers between devices: 3.37 us -> 4.23 us  [swapped(): return lax.ppermute(block, ('inline', 'xline'), route)]
  transfers between devices with their start and end apart: 5 -> 7, of which waited for: 3 -> 3; matrix products, arithmetic and copies ran while one was open for 2% -> 2% of each run, Pallas kernels for 4% -> 8%
where the time goes in v8:
time: 50.3 us; the launch traced here: 49.5 us
  waiting for transfers between devices  20.2 us (40%)
  starting transfers between devices  14.6 us (29%)
  Pallas kernels  12.2 us (24%)
  local copies, waits for them, and re-layouts  1.75 us (3%)
  between operations  0.76 us (2%)
    all_to_all x1, waiting for transfers between devices, body(): lax.all_to_all(sent.reshape(send_rows, 1, 128), ('inline', 'xline'), spli...  15.7 us
    pallas_call x6, Pallas kernels, call_kernel(): pl.pallas_call(kernel, out_shape=out_shape, in_specs=[pl.BlockSpec(memory...  12.2 us
    all_to_all x1, starting transfers between devices, body(): lax.all_to_all(sent.reshape(send_rows, 1, 128), ('inline', 'xline'), spli...  10.4 us
    ppermute x6, waiting for transfers between devices, swapped(): return lax.ppermute(block, ('inline', 'xline'), route)  4.46 us
    ppermute x6, starting transfers between devices, swapped(): return lax.ppermute(block, ('inline', 'xline'), route)  4.23 us
  transfers between devices with their start and end apart: 7, of which 3 were waited for; matrix products, arithmetic and copies ran while one was open for 2% of the time, Pallas kernels for 8%

profile of v8, /device:TPU:14, one launch (start us, length us, event | category | flops | bytes accessed | tf_op | source)
XLA Modules:
  0.0 49.5 jit_solution(6556536119410437940)
XLA Ops:
  0.6 3.4 %shard_map.86 = s32[2176,128]{1,0:T(8,128)} custom-call(f32[4]{0:T(128)} %gains_in.1, f32[1024,256]{1,0:T(8,128)} %traces_in.1, s32[1,1024]{1,0:T(1,128)} %bitcast.22, s32[1,1024]{1,0:T(1,128)} %bitcast.23, s32[1,1024]{1,0:T(1,128)} %bitcast.24), custom_call_target="tpu_custom_call" | custom-call | tf_op jit(solution)/shard_map/pallas_call | solution.py:24
  4.1 0.0 copy-start.1
  4.1 10.4 %all-to-all-start = ((s32[2176,1,128]{2,1,0:T(1,128)}), s32[2176,1,128]{2,1,0:T(1,128)S(1)}, u32[]{:S(2)}, u32[]{:S(2)}) async-start(s32[2176,1,128]{2,1,0:T(1,128)} %bitcast.19), calls=%async_computation | async-start | bytes 2228224 | tf_op jit(solution)/shard_map/all_to_all | solution.py:474
  14.5 0.0 copy-done.1
  14.5 0.0 copy-start
  14.5 0.1 reshape.39
  14.6 0.1 reshape.40.base
  14.7 0.8 %copy-done = bf16[512,512]{1,0:T(8,128)(2,1)S(1)} copy-done((bf16[512,512]{1,0:T(8,128)(2,1)S(1)}, bf16[512,512]{1,0:T(8,128)(2,1)}, u32[]{:S(2)}) %copy-start) | copy-done | bytes 524312
  15.5 0.1 reshape.41
  15.7 0.3 copy.23
  15.9 0.1 reshape.42
  16.1 0.2 copy.20
  16.3 15.7 %all-to-all-done = s32[2176,1,128]{2,1,0:T(1,128)S(1)} async-done(((s32[2176,1,128]{2,1,0:T(1,128)}), s32[2176,1,128]{2,1,0:T(1,128)S(1)}, u32[]{:S(2)}, u32[]{:S(2)}) %all-to-all-start) | async-done | bytes 1114144 | tf_op jit(solution)/shard_map/all_to_all | solution.py:474
  32.1 2.0 %shard_map.87 = (bf16[2,2,64,128]{3,2,1,0:T(8,128)(2,1)S(1)}, bf16[2,2,64,128]{3,2,1,0:T(8,128)(2,1)S(1)}, bf16[4,64,128]{2,1,0:T(8,128)(2,1)S(1)}, bf16[4,64,12...) custom-call(s32[2176,128]{1,0:T(8,128)S(1)} %bitcast.15, ...), custom_call_target="tpu_custom_call" | custom-call | tf_op jit(solution)/shard_map/pallas_call | solution.py:24
  34.1 2.3 %collective-permute-start = (bf16[2,2,64,128]{3,2,1,0:T(8,128)(2,1)S(1)}, bf16[2,2,64,128]{3,2,1,0:T(8,128)(2,1)S(1)}, u32[]{:S(2)}, u32[]{:S(2)}) collective-permute-start(bf16[2,2,64,128]{3,2,1,0:T(8,128)(2,1)S(1)} %get-tuple-element.28), channel_id=1, source_target_pairs={{0,1},{1,0},{2,3},{3,2},{4,5},{5,4},{6,7},{7,6},{8,9},{9,8},{10,11... | collective-permute-start | bytes 196616 | tf_op jit(solution)/shard_map/ppermute | solution.py:517
  36.4 0.0 collective-permute-start.1
  36.4 0.9 %collective-permute-start.4 = (bf16[4,64,128]{2,1,0:T(8,128)(2,1)S(1)}, bf16[4,64,128]{2,1,0:T(8,128)(2,1)S(1)}, u32[]{:S(2)}, u32[]{:S(2)}) collective-permute-start(bf16[4,64,128]{2,1,0:T(8,128)(2,1)S(1)} %get-tuple-element.32), channel_id=1, source_target_pairs={{0,16},{1,2},{2,1},{3,4},{4,3},{5,6},{6,5},{7,8},{8,7},{9,10},{10,... | collective-permute-start | bytes 196616 | tf_op jit(solution)/shard_map/ppermute | solution.py:517
  37.3 0.0 collective-permute-start.5
  37.3 1.2 %shard_map.89 = (bf16[4,4,64,128]{3,2,1,0:T(8,128)(2,1)S(1)}, f32[3,3,64,512]{3,2,1,0:T(8,128)S(1)}, f32[4,4,64,128]{3,2,1,0:T(8,128)S(1)}) custom-call(bf16[2,4,64,128]{3,2,1,0:T(8,128)(2,1)S(1)} %get-tuple-element.35.half, bf16[512,512]{1,0:T(8,128)(2,1)S(1)} %broadcast_multiply_fusion.words, bf16[512,512]{1,0:T(8,128)(2,1)S(1)} %bitcast.16), custom_call_target="tpu_custom_call" | custom-call | flops 600000000 | bytes 2000000 | tf_op jit(solution)/shard_map/pallas_call | solution.py:24
  38.5 3.5 %collective-permute-done.from_odd = bf16[2,2,64,128]{3,2,1,0:T(8,128)(2,1)S(1)} collective-permute-done((bf16[2,2,64,128]{3,2,1,0:T(8,128)(2,1)S(1)}, bf16[2,2,64,128]{3,2,1,0:T(8,128)(2,1)S(1)}, u32[]{:S(2)}, u32[]{:S(2)}) %collective-permute-start) | collective-permute-done | bytes 65568 | tf_op jit(solution)/shard_map/ppermute | solution.py:517
  42.0 0.0 collective-permute-done.1.from_even
  42.1 0.1 collective-permute-start.2
  42.2 0.9 %collective-permute-start.3 = (bf16[3,64,128]{2,1,0:T(8,128)(2,1)S(1)}, bf16[3,64,128]{2,1,0:T(8,128)(2,1)S(1)}, u32[]{:S(2)}, u32[]{:S(2)}) collective-permute-start(bf16[3,64,128]{2,1,0:T(8,128)(2,1)S(1)} %get-tuple-element.31.edge_even), channel_id=1, source_target_pairs={{0,1},{1,0},{2,3},{3,2},{4,5},{5,4},{6,7},{7,6},{8,9},{9,8},{10,11... | collective-permute-start | bytes 147464 | tf_op jit(solution)/shard_map/ppermute | solution.py:517
  43.1 0.0 collective-permute-done.4.side_odd
  43.1 0.0 collective-permute-done.5.side_even
  43.1 2.5 %shard_map.90 = (bf16[4,3,64,128]{3,2,1,0:T(8,128)(2,1)S(1)}, bf16[3,4,64,128]{3,2,1,0:T(8,128)(2,1)S(1)}, f32[6,64,512]{2,1,0:T(8,128)S(1)}, f32[3,5,64,128]{3,...) custom-call(bf16[4,64,128]{2,1,0:T(8,128)(2,1)S(1)} %collective-perm, ...), custom_call_target="tpu_custom_call" | custom-call | flops 1400000000 | bytes 4000000 | tf_op jit(solution)/shard_map/pallas_call | solution.py:24
  45.6 0.9 %collective-permute-done.2.corner_odd = bf16[3,64,128]{2,1,0:T(8,128)(2,1)S(1)} collective-permute-done((bf16[3,64,128]{2,1,0:T(8,128)(2,1)S(1)}, bf16[3,64,128]{2,1,0:T(8,128)(2,1)S(1)}, u32[]{:S(2)}, u32[]{:S(2)}) %collective-permute-start.2) | collective-permute-done | bytes 49184 | tf_op jit(solution)/shard_map/ppermute | solution.py:517
  46.6 0.0 collective-permute-done.3.corner_even
  46.6 3.0 %shard_map.91 = (f32[4,4,64,512]{3,2,1,0:T(8,128)}, f32[256,256]{1,0:T(8,128)}) custom-call(bf16[3,64,128]{2,1,0:T(8,128)(2,1)S(1)} %collective-permute-done.2.corner_odd, bf16[3,64,128]{2,1,0:T(8,128)(2,1)S(1)} %collective-permute-done.3.corner_even, bf16[4,64,128]{2,1,0:T(8,128)(2,1)S(1)} %collective-permute-done.4.side_odd, ...), custom_call_target="tpu_custom_call" | custom-call | tf_op jit(solution)/shard_map/pallas_call | solution.py:24
  (3 shorter events, 0.1 us)
Async XLA Ops:
  4.1 10.4 %copy-start.1 = (f32[16,16,256]{2,1,0:T(8,128)S(1)}, f32[16,16,256]{2,1,0:T(8,128)}, u32[]{:S(2)}) copy-start(f32[16,16,256]{2,1,0:T(8,128)} %param.7) | copy-start | bytes 786436
  4.1 28.0 %all-to-all-start = ((s32[2176,1,128]{2,1,0:T(1,128)}), s32[2176,1,128]{2,1,0:T(1,128)S(1)}, u32[]{:S(2)}, u32[]{:S(2)}) async-start(s32[2176,1,128]{2,1,0:T(1,128)} %bitcast.19), calls=%async_computation | async-start | bytes 2228224 | tf_op jit(solution)/shard_map/all_to_all | solution.py:474
  14.5 1.0 %copy-start = (bf16[512,512]{1,0:T(8,128)(2,1)S(1)}, bf16[512,512]{1,0:T(8,128)(2,1)}, u32[]{:S(2)}) copy-start(bf16[512,512]{1,0:T(8,128)(2,1)} %param.13) | copy-start | bytes 1572868
  34.1 8.0 %collective-permute-start = (bf16[2,2,64,128]{3,2,1,0:T(8,128)(2,1)S(1)}, bf16[2,2,64,128]{3,2,1,0:T(8,128)(2,1)S(1)}, u32[]{:S(2)}, u32[]{:S(2)}) collective-permute-start(bf16[2,2,64,128]{3,2,1,0:T(8,128)(2,1)S(1)} %get-tuple-element.28), channel_id=1, source_target_pairs={{0,1},{1,0},{2,3},{3,2},{4,5},{5,4},{6,7},{7,6},{8,9},{9,8},{10,11... | collective-permute-start | bytes 196616 | tf_op jit(solution)/shard_map/ppermute | solution.py:517
  36.4 5.7 %collective-permute-start.1 = (bf16[2,2,64,128]{3,2,1,0:T(8,128)(2,1)S(1)}, bf16[2,2,64,128]{3,2,1,0:T(8,128)(2,1)S(1)}, u32[]{:S(2)}, u32[]{:S(2)}) collective-permute-start(bf16[2,2,64,128]{3,2,1,0:T(8,128)(2,1)S(1)} %get-tuple-element.29), channel_id=1, source_target_pairs={{0,16},{1,17},{2,18},{3,19},{4,20},{5,21},{6,22},{7,23},{8,24},{9,... | collective-permute-start | bytes 196616 | tf_op jit(solution)/shard_map/ppermute | solution.py:517
  36.4 6.7 %collective-permute-start.4 = (bf16[4,64,128]{2,1,0:T(8,128)(2,1)S(1)}, bf16[4,64,128]{2,1,0:T(8,128)(2,1)S(1)}, u32[]{:S(2)}, u32[]{:S(2)}) collective-permute-start(bf16[4,64,128]{2,1,0:T(8,128)(2,1)S(1)} %get-tuple-element.32), channel_id=1, source_target_pairs={{0,16},{1,2},{2,1},{3,4},{4,3},{5,6},{6,5},{7,8},{8,7},{9,10},{10,... | collective-permute-start | bytes 196616 | tf_op jit(solution)/shard_map/ppermute | solution.py:517
  37.3 5.8 %collective-permute-start.5 = (bf16[4,64,128]{2,1,0:T(8,128)(2,1)S(1)}, bf16[4,64,128]{2,1,0:T(8,128)(2,1)S(1)}, u32[]{:S(2)}, u32[]{:S(2)}) collective-permute-start(bf16[4,64,128]{2,1,0:T(8,128)(2,1)S(1)} %get-tuple-element.33), channel_id=1, source_target_pairs={{0,1},{1,0},{2,3},{3,2},{4,5},{5,4},{6,7},{7,6},{8,9},{9,8},{10,11... | collective-permute-start | bytes 196616 | tf_op jit(solution)/shard_map/ppermute | solution.py:517
  42.1 4.5 %collective-permute-start.2 = (bf16[3,64,128]{2,1,0:T(8,128)(2,1)S(1)}, bf16[3,64,128]{2,1,0:T(8,128)(2,1)S(1)}, u32[]{:S(2)}, u32[]{:S(2)}) collective-permute-start(bf16[3,64,128]{2,1,0:T(8,128)(2,1)S(1)} %get-tuple-element.30.edge_odd), channel_id=1, source_target_pairs={{0,16},{1,2},{2,1},{3,4},{4,3},{5,6},{6,5},{7,8},{8,7},{9,10},{10,... | collective-permute-start | bytes 147464 | tf_op jit(solution)/shard_map/ppermute | solution.py:517
  42.2 4.4 %collective-permute-start.3 = (bf16[3,64,128]{2,1,0:T(8,128)(2,1)S(1)}, bf16[3,64,128]{2,1,0:T(8,128)(2,1)S(1)}, u32[]{:S(2)}, u32[]{:S(2)}) collective-permute-start(bf16[3,64,128]{2,1,0:T(8,128)(2,1)S(1)} %get-tuple-element.31.edge_even), channel_id=1, source_target_pairs={{0,1},{1,0},{2,3},{3,2},{4,5},{5,4},{6,7},{7,6},{8,9},{9,8},{10,11... | collective-permute-start | bytes 147464 | tf_op jit(solution)/shard_map/ppermute | solution.py:517

commit v9 on v8

--- a/solution.py
+++ b/solution.py
@@ -213,7 +213,7 @@
     return jnp.dot(jnp.concatenate(lhs, axis=0), words[...], preferred_element_type=jnp.float32)
 
 
-def first_codes(patches, block, words, words_back, sums, not_top=1.0, not_left=1.0):
+def group_codes(patches, block, words, words_back, sums, not_top, not_left):
     found = shrink_codes(correlated(patches, block, words))
     pieces = [found[64 * number : 64 * number + 64] for number in range(len(patches))]
     masked = []
@@ -234,6 +234,14 @@
     return dict(zip(patches, pieces))
 
 
+def first_codes(each, patches, block, words, words_back, sums, not_top=1.0, not_left=1.0):
+    found = {}
+    for at in range(0, len(patches), each):
+        group = patches[at : at + each]
+        found.update(group_codes(group, block, words, words_back, sums, not_top, not_left))
+    return found
+
+
 def last_codes(before, column, block, words):
     patches = [(row, column) for row in range(4)]
     found = jnp.concatenate(before, axis=0) + correlated(patches, block, words)
@@ -283,7 +291,7 @@
             field[2 * pair + 1, row] = odd
     sums = {}
     patches = [(row, col) for col in range(3) for row in range(3)]
-    found = first_codes(patches, lambda row, col: field[col, row], words, words_back, sums)
+    found = first_codes(6, patches, lambda row, col: field[col, row], words, words_back, sums)
     for (row, col), piece in found.items():
         first[col, row] = piece
     for (row, col), part in sums.items():
@@ -316,7 +324,7 @@
     sums = {(row, col): recon_inner[col, row] for row in range(4) for col in range(4)}
     patches = [(row, col) for col in range(3) for row in (-1, 3, 4)]
     patches += [(row, col) for col in (-1, 3, 4) for row in range(3)]
-    found = first_codes(patches, block, words, words_back, sums, not_top, not_left)
+    found = first_codes(6, patches, block, words, words_back, sums, not_top, not_left)
     for number, spot in enumerate(late_first):
         first[number] = found[spot]
     for number, col in enumerate((0, 3, 4)):
@@ -380,7 +388,7 @@
         if (row, col) != (4, 4)
     }
     patches = [(row, col) for col in (-1, 3, 4) for row in (-1, 3, 4)]
-    found = first_codes(patches, block, words, words_back, sums, not_top, not_left)
+    found = first_codes(3, patches, block, words, words_back, sums, not_top, not_left)
 
     late_spot = {0: 0, 3: 1, 4: 2}
 

time: 50.3 us -> 49.7 us (0.988)
  Pallas kernels: 12.2 us -> 10.7 us
  waiting for transfers between devices: 20.2 us -> 21.3 us
    pallas_call x6, Pallas kernels: 12.2 us -> 10.7 us  [call_kernel(): pl.pallas_call(kernel, out_shape=out_shape, in_specs=[pl.BlockSpec(memory...]
    ppermute x6, waiting for transfers between devices: 4.46 us -> 5.63 us  [swapped(): return lax.ppermute(block, ('inline', 'xline'), route)]
  transfers between devices with their start and end apart: 7 -> 7, of which waited for: 3 -> 3; matrix products, arithmetic and copies ran while one was open for 2% -> 2% of each run, Pallas kernels for 8% -> 5%
where the time goes in v9:
time: 49.7 us; the launch traced here: 49.3 us
  waiting for transfers between devices  21.3 us (43%)
  starting transfers between devices  14.7 us (30%)
  Pallas kernels  10.7 us (22%)
  local copies, waits for them, and re-layouts  1.75 us (4%)
  between operations  0.76 us (2%)
    all_to_all x1, waiting for transfers between devices, body(): lax.all_to_all(sent.reshape(send_rows, 1, 128), ('inline', 'xline'), spli...  15.7 us
    pallas_call x6, Pallas kernels, call_kernel(): pl.pallas_call(kernel, out_shape=out_shape, in_specs=[pl.BlockSpec(memory...  10.7 us
    all_to_all x1, starting transfers between devices, body(): lax.all_to_all(sent.reshape(send_rows, 1, 128), ('inline', 'xline'), spli...  10.4 us
    ppermute x6, waiting for transfers between devices, swapped(): return lax.ppermute(block, ('inline', 'xline'), route)  5.63 us
    ppermute x6, starting transfers between devices, swapped(): return lax.ppermute(block, ('inline', 'xline'), route)  4.28 us
  transfers between devices with their start and end apart: 7, of which 3 were waited for; matrix products, arithmetic and copies ran while one was open for 2% of the time, Pallas kernels for 5%

profile of v9, /device:TPU:14, one launch (start us, length us, event | category | flops | bytes accessed | tf_op | source)
XLA Modules:
  0.0 49.3 jit_solution(382862750915665917)
XLA Ops:
  0.6 3.4 %shard_map.86 = s32[2176,128]{1,0:T(8,128)} custom-call(f32[4]{0:T(128)} %gains_in.1, f32[1024,256]{1,0:T(8,128)} %traces_in.1, s32[1,1024]{1,0:T(1,128)} %bitcast.22, s32[1,1024]{1,0:T(1,128)} %bitcast.23, s32[1,1024]{1,0:T(1,128)} %bitcast.24), custom_call_target="tpu_custom_call" | custom-call | tf_op jit(solution)/shard_map/pallas_call | solution.py:24
  4.1 0.0 copy-start.1
  4.1 10.4 %all-to-all-start = ((s32[2176,1,128]{2,1,0:T(1,128)}), s32[2176,1,128]{2,1,0:T(1,128)S(1)}, u32[]{:S(2)}, u32[]{:S(2)}) async-start(s32[2176,1,128]{2,1,0:T(1,128)} %bitcast.19), calls=%async_computation | async-start | bytes 2228224 | tf_op jit(solution)/shard_map/all_to_all | solution.py:482
  14.5 0.0 copy-done.1
  14.5 0.0 copy-start
  14.5 0.1 reshape.39
  14.6 0.1 reshape.40.base
  14.7 0.8 %copy-done = bf16[512,512]{1,0:T(8,128)(2,1)S(1)} copy-done((bf16[512,512]{1,0:T(8,128)(2,1)S(1)}, bf16[512,512]{1,0:T(8,128)(2,1)}, u32[]{:S(2)}) %copy-start) | copy-done | bytes 524312
  15.5 0.1 reshape.41
  15.7 0.3 copy.23
  15.9 0.1 reshape.42
  16.1 0.2 copy.20
  16.3 15.7 %all-to-all-done = s32[2176,1,128]{2,1,0:T(1,128)S(1)} async-done(((s32[2176,1,128]{2,1,0:T(1,128)}), s32[2176,1,128]{2,1,0:T(1,128)S(1)}, u32[]{:S(2)}, u32[]{:S(2)}) %all-to-all-start) | async-done | bytes 1114144 | tf_op jit(solution)/shard_map/all_to_all | solution.py:482
  32.1 2.0 %shard_map.87 = (bf16[2,2,64,128]{3,2,1,0:T(8,128)(2,1)S(1)}, bf16[2,2,64,128]{3,2,1,0:T(8,128)(2,1)S(1)}, bf16[4,64,128]{2,1,0:T(8,128)(2,1)S(1)}, bf16[4,64,12...) custom-call(s32[2176,128]{1,0:T(8,128)S(1)} %bitcast.15, ...), custom_call_target="tpu_custom_call" | custom-call | tf_op jit(solution)/shard_map/pallas_call | solution.py:24
  34.1 2.3 %collective-permute-start = (bf16[2,2,64,128]{3,2,1,0:T(8,128)(2,1)S(1)}, bf16[2,2,64,128]{3,2,1,0:T(8,128)(2,1)S(1)}, u32[]{:S(2)}, u32[]{:S(2)}) collective-permute-start(bf16[2,2,64,128]{3,2,1,0:T(8,128)(2,1)S(1)} %get-tuple-element.28), channel_id=1, source_target_pairs={{0,1},{1,0},{2,3},{3,2},{4,5},{5,4},{6,7},{7,6},{8,9},{9,8},{10,11... | collective-permute-start | bytes 196616 | tf_op jit(solution)/shard_map/ppermute | solution.py:525
  36.4 0.0 collective-permute-start.1
  36.4 0.9 %collective-permute-start.4 = (bf16[4,64,128]{2,1,0:T(8,128)(2,1)S(1)}, bf16[4,64,128]{2,1,0:T(8,128)(2,1)S(1)}, u32[]{:S(2)}, u32[]{:S(2)}) collective-permute-start(bf16[4,64,128]{2,1,0:T(8,128)(2,1)S(1)} %get-tuple-element.32), channel_id=1, source_target_pairs={{0,16},{1,2},{2,1},{3,4},{4,3},{5,6},{6,5},{7,8},{8,7},{9,10},{10,... | collective-permute-start | bytes 196616 | tf_op jit(solution)/shard_map/ppermute | solution.py:525
  37.3 0.0 collective-permute-start.5
  37.3 0.8 %shard_map.89 = (bf16[4,4,64,128]{3,2,1,0:T(8,128)(2,1)S(1)}, f32[3,3,64,512]{3,2,1,0:T(8,128)S(1)}, f32[4,4,64,128]{3,2,1,0:T(8,128)S(1)}) custom-call(bf16[2,4,64,128]{3,2,1,0:T(8,128)(2,1)S(1)} %get-tuple-element.35.half, bf16[512,512]{1,0:T(8,128)(2,1)S(1)} %broadcast_multiply_fusion.words, bf16[512,512]{1,0:T(8,128)(2,1)S(1)} %bitcast.16), custom_call_target="tpu_custom_call" | custom-call | flops 600000000 | bytes 2000000 | tf_op jit(solution)/shard_map/pallas_call | solution.py:24
  38.1 3.9 %collective-permute-done.from_odd = bf16[2,2,64,128]{3,2,1,0:T(8,128)(2,1)S(1)} collective-permute-done((bf16[2,2,64,128]{3,2,1,0:T(8,128)(2,1)S(1)}, bf16[2,2,64,128]{3,2,1,0:T(8,128)(2,1)S(1)}, u32[]{:S(2)}, u32[]{:S(2)}) %collective-permute-start) | collective-permute-done | bytes 65568 | tf_op jit(solution)/shard_map/ppermute | solution.py:525
  42.0 0.0 collective-permute-done.1.from_even
  42.1 0.1 collective-permute-start.2
  42.2 1.0 %collective-permute-start.3 = (bf16[3,64,128]{2,1,0:T(8,128)(2,1)S(1)}, bf16[3,64,128]{2,1,0:T(8,128)(2,1)S(1)}, u32[]{:S(2)}, u32[]{:S(2)}) collective-permute-start(bf16[3,64,128]{2,1,0:T(8,128)(2,1)S(1)} %get-tuple-element.31.edge_even), channel_id=1, source_target_pairs={{0,1},{1,0},{2,3},{3,2},{4,5},{5,4},{6,7},{7,6},{8,9},{9,8},{10,11... | collective-permute-start | bytes 147464 | tf_op jit(solution)/shard_map/ppermute | solution.py:525
  43.2 0.0 collective-permute-done.4.side_odd
  43.2 0.0 collective-permute-done.5.side_even
  43.2 1.7 %shard_map.90 = (bf16[4,3,64,128]{3,2,1,0:T(8,128)(2,1)S(1)}, bf16[3,4,64,128]{3,2,1,0:T(8,128)(2,1)S(1)}, f32[6,64,512]{2,1,0:T(8,128)S(1)}, f32[3,5,64,128]{3,...) custom-call(bf16[4,64,128]{2,1,0:T(8,128)(2,1)S(1)} %collective-perm, ...), custom_call_target="tpu_custom_call" | custom-call | flops 1400000000 | bytes 4000000 | tf_op jit(solution)/shard_map/pallas_call | solution.py:24
  44.9 1.7 %collective-permute-done.2.corner_odd = bf16[3,64,128]{2,1,0:T(8,128)(2,1)S(1)} collective-permute-done((bf16[3,64,128]{2,1,0:T(8,128)(2,1)S(1)}, bf16[3,64,128]{2,1,0:T(8,128)(2,1)S(1)}, u32[]{:S(2)}, u32[]{:S(2)}) %collective-permute-start.2) | collective-permute-done | bytes 49184 | tf_op jit(solution)/shard_map/ppermute | solution.py:525
  46.6 0.0 collective-permute-done.3.corner_even
  46.6 2.7 %shard_map.91 = (f32[4,4,64,512]{3,2,1,0:T(8,128)}, f32[256,256]{1,0:T(8,128)}) custom-call(bf16[3,64,128]{2,1,0:T(8,128)(2,1)S(1)} %collective-permute-done.2.corner_odd, bf16[3,64,128]{2,1,0:T(8,128)(2,1)S(1)} %collective-permute-done.3.corner_even, bf16[4,64,128]{2,1,0:T(8,128)(2,1)S(1)} %collective-permute-done.4.side_odd, ...), custom_call_target="tpu_custom_call" | custom-call | tf_op jit(solution)/shard_map/pallas_call | solution.py:24
  (3 shorter events, 0.1 us)
Async XLA Ops:
  4.1 10.4 %copy-start.1 = (f32[16,16,256]{2,1,0:T(8,128)S(1)}, f32[16,16,256]{2,1,0:T(8,128)}, u32[]{:S(2)}) copy-start(f32[16,16,256]{2,1,0:T(8,128)} %param.7) | copy-start | bytes 786436
  4.1 28.0 %all-to-all-start = ((s32[2176,1,128]{2,1,0:T(1,128)}), s32[2176,1,128]{2,1,0:T(1,128)S(1)}, u32[]{:S(2)}, u32[]{:S(2)}) async-start(s32[2176,1,128]{2,1,0:T(1,128)} %bitcast.19), calls=%async_computation | async-start | bytes 2228224 | tf_op jit(solution)/shard_map/all_to_all | solution.py:482
  14.5 1.0 %copy-start = (bf16[512,512]{1,0:T(8,128)(2,1)S(1)}, bf16[512,512]{1,0:T(8,128)(2,1)}, u32[]{:S(2)}) copy-start(bf16[512,512]{1,0:T(8,128)(2,1)} %param.13) | copy-start | bytes 1572868
  34.1 8.0 %collective-permute-start = (bf16[2,2,64,128]{3,2,1,0:T(8,128)(2,1)S(1)}, bf16[2,2,64,128]{3,2,1,0:T(8,128)(2,1)S(1)}, u32[]{:S(2)}, u32[]{:S(2)}) collective-permute-start(bf16[2,2,64,128]{3,2,1,0:T(8,128)(2,1)S(1)} %get-tuple-element.28), channel_id=1, source_target_pairs={{0,1},{1,0},{2,3},{3,2},{4,5},{5,4},{6,7},{7,6},{8,9},{9,8},{10,11... | collective-permute-start | bytes 196616 | tf_op jit(solution)/shard_map/ppermute | solution.py:525
  36.4 5.7 %collective-permute-start.1 = (bf16[2,2,64,128]{3,2,1,0:T(8,128)(2,1)S(1)}, bf16[2,2,64,128]{3,2,1,0:T(8,128)(2,1)S(1)}, u32[]{:S(2)}, u32[]{:S(2)}) collective-permute-start(bf16[2,2,64,128]{3,2,1,0:T(8,128)(2,1)S(1)} %get-tuple-element.29), channel_id=1, source_target_pairs={{0,16},{1,17},{2,18},{3,19},{4,20},{5,21},{6,22},{7,23},{8,24},{9,... | collective-permute-start | bytes 196616 | tf_op jit(solution)/shard_map/ppermute | solution.py:525
  36.4 6.8 %collective-permute-start.4 = (bf16[4,64,128]{2,1,0:T(8,128)(2,1)S(1)}, bf16[4,64,128]{2,1,0:T(8,128)(2,1)S(1)}, u32[]{:S(2)}, u32[]{:S(2)}) collective-permute-start(bf16[4,64,128]{2,1,0:T(8,128)(2,1)S(1)} %get-tuple-element.32), channel_id=1, source_target_pairs={{0,16},{1,2},{2,1},{3,4},{4,3},{5,6},{6,5},{7,8},{8,7},{9,10},{10,... | collective-permute-start | bytes 196616 | tf_op jit(solution)/shard_map/ppermute | solution.py:525
  37.3 5.9 %collective-permute-start.5 = (bf16[4,64,128]{2,1,0:T(8,128)(2,1)S(1)}, bf16[4,64,128]{2,1,0:T(8,128)(2,1)S(1)}, u32[]{:S(2)}, u32[]{:S(2)}) collective-permute-start(bf16[4,64,128]{2,1,0:T(8,128)(2,1)S(1)} %get-tuple-element.33), channel_id=1, source_target_pairs={{0,1},{1,0},{2,3},{3,2},{4,5},{5,4},{6,7},{7,6},{8,9},{9,8},{10,11... | collective-permute-start | bytes 196616 | tf_op jit(solution)/shard_map/ppermute | solution.py:525
  42.1 4.5 %collective-permute-start.2 = (bf16[3,64,128]{2,1,0:T(8,128)(2,1)S(1)}, bf16[3,64,128]{2,1,0:T(8,128)(2,1)S(1)}, u32[]{:S(2)}, u32[]{:S(2)}) collective-permute-start(bf16[3,64,128]{2,1,0:T(8,128)(2,1)S(1)} %get-tuple-element.30.edge_odd), channel_id=1, source_target_pairs={{0,16},{1,2},{2,1},{3,4},{4,3},{5,6},{6,5},{7,8},{8,7},{9,10},{10,... | collective-permute-start | bytes 147464 | tf_op jit(solution)/shard_map/ppermute | solution.py:525
  42.2 4.4 %collective-permute-start.3 = (bf16[3,64,128]{2,1,0:T(8,128)(2,1)S(1)}, bf16[3,64,128]{2,1,0:T(8,128)(2,1)S(1)}, u32[]{:S(2)}, u32[]{:S(2)}) collective-permute-start(bf16[3,64,128]{2,1,0:T(8,128)(2,1)S(1)} %get-tuple-element.31.edge_even), channel_id=1, source_target_pairs={{0,1},{1,0},{2,3},{3,2},{4,5},{5,4},{6,7},{7,6},{8,9},{9,8},{10,11... | collective-permute-start | bytes 147464 | tf_op jit(solution)/shard_map/ppermute | solution.py:525

commit v10 on v9

--- a/solution.py
+++ b/solution.py
@@ -13,7 +13,6 @@
 code_top = 32767.0
 log_top = math.log2(12.0)
 vmem_bytes = 48 * 1024 * 1024
-all_vmem_bytes = 64 * 1024 * 1024
 
 
 def shrink_codes(values):
@@ -122,8 +121,12 @@
     return zero, one, two, three
 
 
-def merge_kernel(got, base, to_odd, to_even, side_odd, side_even, half, whole, turned):
+def merge_kernel(got, base, to_odd, to_even, side_odd, side_even, half, whole, turned, ordered):
     tiles = got.shape[0] // 128
+    for number in range(64):
+        tile, odd, part, pair = number // 32, number // 16 % 2, number // 8 % 2, number // 4 % 2
+        at = (4 * (2 * tile + part) + number % 4) * 16 + 4 * (2 * pair + odd)
+        ordered[4 * number : 4 * number + 4, :] = base[at : at + 4, :]
     bin_row = lax.broadcasted_iota(jnp.int32, (256, 128), 0)
     tile, part, pair, odd = bin_row // 128, (bin_row // 32) % 2, (bin_row // 16) % 2, (bin_row // 64) % 2
     block_row, block_col = 2 * tile + part, 2 * pair + odd
@@ -133,11 +136,11 @@
     begin = 17 * lax.broadcasted_iota(jnp.int32, (128, 128), 0)
     lane = lax.broadcasted_iota(jnp.int32, (128, 128), 1)
     tile_of = begin // 128 + jnp.where(lane < begin % 128, 1, 0)
-    tiles_each = 4
+    tiles_each = 2
     fold = jnp.zeros((256, 128), jnp.float32)
-    stack = jnp.zeros((256, 512), jnp.float32)
+    stack = jnp.zeros((256, 256), jnp.float32)
     for at in range(0, tiles, tiles_each):
-        hits, rows = [], []
+        hits, rows, rests = [], [], []
         for tile in range(at, min(at + tiles_each, tiles)):
             low_group, high_group = (128 * tile) // 136, min((128 * tile + 127) // 136, 15)
             spot = slice(8 * low_group, 8 * high_group + 8)
@@ -152,14 +155,15 @@
                 (value - part.astype(jnp.float32)).astype(jnp.bfloat16)
                 for value, part in zip(values, high)
             ]
-            rows.append(jnp.concatenate(high + low, axis=1))
+            rows.append(jnp.concatenate(high, axis=1))
+            rests.append(jnp.concatenate(low, axis=1))
         stack = stack + jnp.dot(
-            jnp.concatenate(hits, axis=1),
-            jnp.concatenate(rows, axis=0),
+            jnp.concatenate(hits + hits, axis=1),
+            jnp.concatenate(rows + rests, axis=0),
             preferred_element_type=jnp.float32,
         )
     fold = jnp.sum(fold, axis=1, keepdims=True)
-    merged = (base[...] + (stack[:, :256] + stack[:, 256:])) / (1.0 + fold)
+    merged = (ordered[...] + stack) / (1.0 + fold)
     turned[0] = jnp.transpose(merged[:128])
     turned[1] = jnp.transpose(merged[128:])
     for tile in range(2):
@@ -471,26 +475,19 @@
         ],
         pltpu.HBM,
         [
-            vintage_gains,
-            vintage_traces,
-            dest_device.reshape(1, trace_count),
-            dest_slot.reshape(1, trace_count),
-            vintage_id.reshape(1, trace_count),
+            pltpu.with_memory_space_constraint(array, pltpu.HBM)
+            for array in (
+                vintage_gains,
+                vintage_traces,
+                dest_device.reshape(1, trace_count),
+                dest_slot.reshape(1, trace_count),
+                vintage_id.reshape(1, trace_count),
+            )
         ],
-        all_vmem_bytes,
     )
     got = lax.all_to_all(
         sent.reshape(send_rows, 1, 128), ("inline", "xline"), split_axis=0, concat_axis=0, tiled=True
     ).reshape(send_rows, 128)
-    words = dictionary.reshape(2, 4, 2, 4, 2, 4, 512).transpose(0, 2, 4, 5, 1, 3, 6).reshape(512, 512)
-    words_back = words.T
-    words = words * jnp.bfloat16(step_size)
-    base = (
-        base_volume.reshape(2, 2, 4, 2, 2, 4, time_len)
-        .transpose(0, 4, 1, 3, 2, 5, 6)
-        .reshape(256, time_len)
-    )
-    got, base, words, words_back = lax.optimization_barrier((got, base, words, words_back))
     full_shape = lambda *shape: jax.ShapeDtypeStruct(shape, jnp.float32)
     pair_shape = lambda *lead: jax.ShapeDtypeStruct(lead + (64, 128), jnp.bfloat16)
     to_odd, to_even, side_odd, side_even, half, whole = call_kernel(
@@ -504,10 +501,14 @@
             full_shape(4, 2, 64, 128),
         ),
         (pltpu.VMEM,) * 6,
-        [pltpu.VMEM((2, 256, 128), jnp.float32)],
+        [pltpu.VMEM((2, 256, 128), jnp.float32), pltpu.VMEM((256, time_len), jnp.float32)],
         pltpu.VMEM,
-        [got, base],
-    )
+        [got, base_volume.reshape(256, time_len)],
+    )
+    half, dictionary = lax.optimization_barrier((half, dictionary))
+    words = dictionary.reshape(2, 4, 2, 4, 2, 4, 512).transpose(0, 2, 4, 5, 1, 3, 6).reshape(512, 512)
+    words_back = words.T
+    words = words * jnp.bfloat16(step_size)
 
     rows, columns = lax.axis_size("inline"), lax.axis_size("xline")
 

time: 49.7 us -> 48.6 us (0.978)
  blocking collectives: 0 us -> 27.7 us
  waiting for transfers between devices: 21.3 us -> 4.91 us
  starting transfers between devices: 14.7 us -> 4.19 us
  local copies, waits for them, and re-layouts: 1.75 us -> 0.74 us
  Pallas kernels: 10.7 us -> 9.89 us
    all_to_all x0 -> x1, blocking collectives: none -> 27.7 us  [body(): lax.all_to_all(sent.reshape(send_rows, 1, 128), ('inline', 'xline'), spli...]
    all_to_all x1 -> x0, waiting for transfers between devices: 15.7 us -> none  [body(): lax.all_to_all(sent.reshape(send_rows, 1, 128), ('inline', 'xline'), spli...]
    all_to_all x1 -> x0, starting transfers between devices: 10.4 us -> none  [body(): lax.all_to_all(sent.reshape(send_rows, 1, 128), ('inline', 'xline'), spli...]
    pallas_call x6, Pallas kernels: 10.7 us -> 9.89 us  [call_kernel(): pl.pallas_call(kernel, out_shape=out_shape, in_specs=[pl.BlockSpec(memory...]
    unnamed x4, local copies, waits for them, and re-layouts: 0.83 us -> 0.01 us
    ppermute x6, waiting for transfers between devices: 5.63 us -> 4.91 us  [swapped(): return lax.ppermute(block, ('inline', 'xline'), route)]
  transfers between devices with their start and end apart: 7 -> 6, of which waited for: 3 -> 2; matrix products, arithmetic and copies ran while one was open for 2% -> 2% of each run, Pallas kernels for 5% -> 5%
where the time goes in v10:
time: 48.6 us; the launch traced here: 48.2 us
  blocking collectives  27.7 us (57%)
  Pallas kernels  9.89 us (20%)
  waiting for transfers between devices  4.91 us (10%)
  starting transfers between devices  4.19 us (9%)
  local copies, waits for them, and re-layouts  0.74 us (2%)
  between operations  0.71 us (1%)
    all_to_all x1, blocking collectives, body(): lax.all_to_all(sent.reshape(send_rows, 1, 128), ('inline', 'xline'), spli...  27.7 us
    pallas_call x6, Pallas kernels, call_kernel(): pl.pallas_call(kernel, out_shape=out_shape, in_specs=[pl.BlockSpec(memory...  9.89 us
    ppermute x6, waiting for transfers between devices, swapped(): return lax.ppermute(block, ('inline', 'xline'), route)  4.91 us
    ppermute x6, starting transfers between devices, swapped(): return lax.ppermute(block, ('inline', 'xline'), route)  4.19 us
  transfers between devices with their start and end apart: 6, of which 2 were waited for; matrix products, arithmetic and copies ran while one was open for 2% of the time, Pallas kernels for 5%

profile of v10, /device:TPU:14, one launch (start us, length us, event | category | flops | bytes accessed | tf_op | source)
XLA Modules:
  0.0 48.2 jit_solution(6181182480235045503)
XLA Ops:
  0.6 2.6 %shard_map.86 = s32[2176,128]{1,0:T(8,128)S(1)} custom-call(f32[4]{0:T(128)} %gains_in.1, f32[1024,256]{1,0:T(8,128)} %traces_in.1, s32[1,1024]{1,0:T(1,128)} %bitcast.20, s32[1,1024]{1,0:T(1,128)} %bitcast.21, s32[1,1024]{1,0:T(1,128)} %bitcast.22), custom_call_target="tpu_custom_call" | custom-call | tf_op jit(solution)/shard_map/pallas_call | solution.py:23
  3.3 0.0 copy-start
  3.3 27.7 %all_to_all.5 = s32[2176,1,128]{2,1,0:T(1,128)S(1)} all-to-all(s32[2176,1,128]{2,1,0:T(1,128)S(1)} %bitcast.13), channel_id=1, replica_groups=mesh['inline'=8,'xline'=16] {'inline','xline'}, dimensions={0} | all-to-all | bytes 2228224 | tf_op jit(solution)/shard_map/all_to_all | solution.py:488
  31.0 0.0 copy-start.1
  31.0 0.0 copy-done
  31.0 2.0 %shard_map.87 = (bf16[2,2,64,128]{3,2,1,0:T(8,128)(2,1)S(1)}, bf16[2,2,64,128]{3,2,1,0:T(8,128)(2,1)S(1)}, bf16[4,64,128]{2,1,0:T(8,128)(2,1)S(1)}, bf16[4,64,12...) custom-call(s32[2176,128]{1,0:T(8,128)S(1)} %bitcast.14, ...), custom_call_target="tpu_custom_call" | custom-call | tf_op jit(solution)/shard_map/pallas_call | solution.py:23
  33.0 2.3 %collective-permute-start = (bf16[2,2,64,128]{3,2,1,0:T(8,128)(2,1)S(1)}, bf16[2,2,64,128]{3,2,1,0:T(8,128)(2,1)S(1)}, u32[]{:S(2)}, u32[]{:S(2)}) collective-permute-start(bf16[2,2,64,128]{3,2,1,0:T(8,128)(2,1)S(1)} %get-tuple-element.24), channel_id=1, source_target_pairs={{0,1},{1,0},{2,3},{3,2},{4,5},{5,4},{6,7},{7,6},{8,9},{9,8},{10,11... | collective-permute-start | bytes 196616 | tf_op jit(solution)/shard_map/ppermute | solution.py:526
  35.3 0.0 collective-permute-start.1
  35.3 0.9 %collective-permute-start.4 = (bf16[4,64,128]{2,1,0:T(8,128)(2,1)S(1)}, bf16[4,64,128]{2,1,0:T(8,128)(2,1)S(1)}, u32[]{:S(2)}, u32[]{:S(2)}) collective-permute-start(bf16[4,64,128]{2,1,0:T(8,128)(2,1)S(1)} %get-tuple-element.28), channel_id=1, source_target_pairs={{0,16},{1,2},{2,1},{3,4},{4,3},{5,6},{6,5},{7,8},{8,7},{9,10},{10,... | collective-permute-start | bytes 196616 | tf_op jit(solution)/shard_map/ppermute | solution.py:526
  36.2 0.0 collective-permute-start.5
  36.2 0.0 copy-done.1
  36.2 0.1 reshape.37
  36.4 0.3 copy.19
  36.6 0.1 reshape.38
  36.8 0.2 copy.17
  37.0 0.8 %shard_map.89 = (bf16[4,4,64,128]{3,2,1,0:T(8,128)(2,1)S(1)}, f32[3,3,64,512]{3,2,1,0:T(8,128)S(1)}, f32[4,4,64,128]{3,2,1,0:T(8,128)S(1)}) custom-call(bf16[2,4,64,128]{3,2,1,0:T(8,128)(2,1)S(1)} %get-tuple-element.32.half, bf16[512,512]{1,0:T(8,128)(2,1)S(1)} %broadcast_multiply_fusion.words, bf16[512,512]{1,0:T(8,128)(2,1)S(1)} %bitcast.15), custom_call_target="tpu_custom_call" | custom-call | flops 600000000 | bytes 2000000 | tf_op jit(solution)/shard_map/pallas_call | solution.py:23
  37.9 3.1 %collective-permute-done.from_odd = bf16[2,2,64,128]{3,2,1,0:T(8,128)(2,1)S(1)} collective-permute-done((bf16[2,2,64,128]{3,2,1,0:T(8,128)(2,1)S(1)}, bf16[2,2,64,128]{3,2,1,0:T(8,128)(2,1)S(1)}, u32[]{:S(2)}, u32[]{:S(2)}) %collective-permute-start) | collective-permute-done | bytes 65568 | tf_op jit(solution)/shard_map/ppermute | solution.py:526
  41.0 0.0 collective-permute-done.1.from_even
  41.0 0.1 collective-permute-start.2
  41.1 0.9 %collective-permute-start.3 = (bf16[3,64,128]{2,1,0:T(8,128)(2,1)S(1)}, bf16[3,64,128]{2,1,0:T(8,128)(2,1)S(1)}, u32[]{:S(2)}, u32[]{:S(2)}) collective-permute-start(bf16[3,64,128]{2,1,0:T(8,128)(2,1)S(1)} %get-tuple-element.27.edge_even), channel_id=1, source_target_pairs={{0,1},{1,0},{2,3},{3,2},{4,5},{5,4},{6,7},{7,6},{8,9},{9,8},{10,11... | collective-permute-start | bytes 147464 | tf_op jit(solution)/shard_map/ppermute | solution.py:526
  42.0 0.0 collective-permute-done.4.side_odd
  42.0 0.0 collective-permute-done.5.side_even
  42.0 1.7 %shard_map.90 = (bf16[4,3,64,128]{3,2,1,0:T(8,128)(2,1)S(1)}, bf16[3,4,64,128]{3,2,1,0:T(8,128)(2,1)S(1)}, f32[6,64,512]{2,1,0:T(8,128)S(1)}, f32[3,5,64,128]{3,...) custom-call(bf16[4,64,128]{2,1,0:T(8,128)(2,1)S(1)} %collective-perm, ...), custom_call_target="tpu_custom_call" | custom-call | flops 1400000000 | bytes 4000000 | tf_op jit(solution)/shard_map/pallas_call | solution.py:23
  43.7 1.8 %collective-permute-done.2.corner_odd = bf16[3,64,128]{2,1,0:T(8,128)(2,1)S(1)} collective-permute-done((bf16[3,64,128]{2,1,0:T(8,128)(2,1)S(1)}, bf16[3,64,128]{2,1,0:T(8,128)(2,1)S(1)}, u32[]{:S(2)}, u32[]{:S(2)}) %collective-permute-start.2) | collective-permute-done | bytes 49184 | tf_op jit(solution)/shard_map/ppermute | solution.py:526
  45.5 0.0 collective-permute-done.3.corner_even
  45.5 2.7 %shard_map.91 = (f32[4,4,64,512]{3,2,1,0:T(8,128)}, f32[256,256]{1,0:T(8,128)}) custom-call(bf16[3,64,128]{2,1,0:T(8,128)(2,1)S(1)} %collective-permute-done.2.corner_odd, bf16[3,64,128]{2,1,0:T(8,128)(2,1)S(1)} %collective-permute-done.3.corner_even, bf16[4,64,128]{2,1,0:T(8,128)(2,1)S(1)} %collective-permute-done.4.side_odd, ...), custom_call_target="tpu_custom_call" | custom-call | tf_op jit(solution)/shard_map/pallas_call | solution.py:23
  (2 shorter events, 0.1 us)
Async XLA Ops:
  3.3 27.8 %copy-start = (f32[16,16,256]{2,1,0:T(8,128)S(1)}, f32[16,16,256]{2,1,0:T(8,128)}, u32[]{:S(2)}) copy-start(f32[16,16,256]{2,1,0:T(8,128)} %param.7) | copy-start | bytes 786436
  31.0 5.2 %copy-start.1 = (bf16[512,512]{1,0:T(8,128)(2,1)S(1)}, bf16[512,512]{1,0:T(8,128)(2,1)}, u32[]{:S(2)}) copy-start(bf16[512,512]{1,0:T(8,128)(2,1)} %param.13) | copy-start | bytes 1572868
  33.0 8.0 %collective-permute-start = (bf16[2,2,64,128]{3,2,1,0:T(8,128)(2,1)S(1)}, bf16[2,2,64,128]{3,2,1,0:T(8,128)(2,1)S(1)}, u32[]{:S(2)}, u32[]{:S(2)}) collective-permute-start(bf16[2,2,64,128]{3,2,1,0:T(8,128)(2,1)S(1)} %get-tuple-element.24), channel_id=1, source_target_pairs={{0,1},{1,0},{2,3},{3,2},{4,5},{5,4},{6,7},{7,6},{8,9},{9,8},{10,11... | collective-permute-start | bytes 196616 | tf_op jit(solution)/shard_map/ppermute | solution.py:526
  35.3 5.7 %collective-permute-start.1 = (bf16[2,2,64,128]{3,2,1,0:T(8,128)(2,1)S(1)}, bf16[2,2,64,128]{3,2,1,0:T(8,128)(2,1)S(1)}, u32[]{:S(2)}, u32[]{:S(2)}) collective-permute-start(bf16[2,2,64,128]{3,2,1,0:T(8,128)(2,1)S(1)} %get-tuple-element.25), channel_id=1, source_target_pairs={{0,16},{1,17},{2,18},{3,19},{4,20},{5,21},{6,22},{7,23},{8,24},{9,... | collective-permute-start | bytes 196616 | tf_op jit(solution)/shard_map/ppermute | solution.py:526
  35.3 6.7 %collective-permute-start.4 = (bf16[4,64,128]{2,1,0:T(8,128)(2,1)S(1)}, bf16[4,64,128]{2,1,0:T(8,128)(2,1)S(1)}, u32[]{:S(2)}, u32[]{:S(2)}) collective-permute-start(bf16[4,64,128]{2,1,0:T(8,128)(2,1)S(1)} %get-tuple-element.28), channel_id=1, source_target_pairs={{0,16},{1,2},{2,1},{3,4},{4,3},{5,6},{6,5},{7,8},{8,7},{9,10},{10,... | collective-permute-start | bytes 196616 | tf_op jit(solution)/shard_map/ppermute | solution.py:526
  36.2 5.8 %collective-permute-start.5 = (bf16[4,64,128]{2,1,0:T(8,128)(2,1)S(1)}, bf16[4,64,128]{2,1,0:T(8,128)(2,1)S(1)}, u32[]{:S(2)}, u32[]{:S(2)}) collective-permute-start(bf16[4,64,128]{2,1,0:T(8,128)(2,1)S(1)} %get-tuple-element.29), channel_id=1, source_target_pairs={{0,1},{1,0},{2,3},{3,2},{4,5},{5,4},{6,7},{7,6},{8,9},{9,8},{10,11... | collective-permute-start | bytes 196616 | tf_op jit(solution)/shard_map/ppermute | solution.py:526
  41.0 4.5 %collective-permute-start.2 = (bf16[3,64,128]{2,1,0:T(8,128)(2,1)S(1)}, bf16[3,64,128]{2,1,0:T(8,128)(2,1)S(1)}, u32[]{:S(2)}, u32[]{:S(2)}) collective-permute-start(bf16[3,64,128]{2,1,0:T(8,128)(2,1)S(1)} %get-tuple-element.26.edge_odd), channel_id=1, source_target_pairs={{0,16},{1,2},{2,1},{3,4},{4,3},{5,6},{6,5},{7,8},{8,7},{9,10},{10,... | collective-permute-start | bytes 147464 | tf_op jit(solution)/shard_map/ppermute | solution.py:526
  41.1 4.4 %collective-permute-start.3 = (bf16[3,64,128]{2,1,0:T(8,128)(2,1)S(1)}, bf16[3,64,128]{2,1,0:T(8,128)(2,1)S(1)}, u32[]{:S(2)}, u32[]{:S(2)}) collective-permute-start(bf16[3,64,128]{2,1,0:T(8,128)(2,1)S(1)} %get-tuple-element.27.edge_even), channel_id=1, source_target_pairs={{0,1},{1,0},{2,3},{3,2},{4,5},{5,4},{6,7},{7,6},{8,9},{9,8},{10,11... | collective-permute-start | bytes 147464 | tf_op jit(solution)/shard_map/ppermute | solution.py:526

commit v11 on v10

--- a/solution.py
+++ b/solution.py
@@ -44,7 +44,7 @@
     return size * jnp.clip(code, -1.0, 1.0)
 
 
-def pack_kernel(gains_in, traces_in, dest_in, slot_in, vid_in, out, gains, traces, dest, slot, vid, built, words, place, place_at, arrive, leave):
+def pack_kernel(gains_in, traces_in, dest_in, slot_in, vid_in, built, gains, traces, dest, slot, vid, words, place, place_at, arrive):
     loads = [
         pltpu.make_async_copy(source, target, arrive.at[number])
         for number, (source, target) in enumerate(
@@ -54,7 +54,7 @@
     for load in loads:
         load.start()
     trace_count = traces.shape[0]
-    device_count = out.shape[0] // 17
+    device_count = built.shape[0] // 17
     built[...] = jnp.zeros_like(built)
     chunks = trace_count // 128
     me = lax.axis_index("inline") * lax.axis_size("xline") + lax.axis_index("xline")
@@ -101,9 +101,6 @@
     put.wait()
     for trace in range(trace_count):
         built[pl.ds(place_at[0, trace], 1), :] = words[trace : trace + 1, :]
-    send = pltpu.make_async_copy(built, out, leave)
-    send.start()
-    send.wait()
 
 
 def exchanged(four):
@@ -459,19 +456,17 @@
     sent = call_kernel(
         pack_kernel,
         jax.ShapeDtypeStruct((send_rows, 128), jnp.int32),
-        pltpu.HBM,
+        pltpu.VMEM,
         [
             pltpu.SMEM(vintage_gains.shape, jnp.float32),
             pltpu.VMEM(vintage_traces.shape, jnp.float32),
             pltpu.VMEM((1, trace_count), jnp.int32),
             pltpu.VMEM((1, trace_count), jnp.int32),
             pltpu.VMEM((1, trace_count), jnp.int32),
-            pltpu.VMEM((send_rows, 128), jnp.int32),
             pltpu.VMEM((trace_count, 128), jnp.int32),
             pltpu.VMEM((1, trace_count), jnp.int32),
             pltpu.SMEM((1, trace_count), jnp.int32),
             pltpu.SemaphoreType.DMA((6,)),
-            pltpu.SemaphoreType.DMA,
         ],
         pltpu.HBM,
         [

time: 48.6 us -> 48.4 us (level)
  no operation moved by 1% of the time
where the time goes in v11:
time: 48.4 us; the launch traced here: 48.1 us
  blocking collectives  27.7 us (57%)
  Pallas kernels  9.71 us (20%)
  waiting for transfers between devices  4.91 us (10%)
  starting transfers between devices  4.19 us (9%)
  local copies, waits for them, and re-layouts  0.74 us (2%)
  between operations  0.71 us (1%)
    all_to_all x1, blocking collectives, body(): lax.all_to_all(sent.reshape(send_rows, 1, 128), ('inline', 'xline'), spli...  27.7 us
    pallas_call x6, Pallas kernels, call_kernel(): pl.pallas_call(kernel, out_shape=out_shape, in_specs=[pl.BlockSpec(memory...  9.71 us
    ppermute x6, waiting for transfers between devices, swapped(): return lax.ppermute(block, ('inline', 'xline'), route)  4.91 us
    ppermute x6, starting transfers between devices, swapped(): return lax.ppermute(block, ('inline', 'xline'), route)  4.19 us
  transfers between devices with their start and end apart: 6, of which 2 were waited for; matrix products, arithmetic and copies ran while one was open for 2% of the time, Pallas kernels for 5%

profile of v11, /device:TPU:14, one launch (start us, length us, event | category | flops | bytes accessed | tf_op | source)
XLA Modules:
  0.0 48.1 jit_solution(447848793756387903)
XLA Ops:
  0.6 2.4 %shard_map.86 = s32[2176,128]{1,0:T(8,128)S(1)} custom-call(f32[4]{0:T(128)} %gains_in.1, f32[1024,256]{1,0:T(8,128)} %traces_in.1, s32[1,1024]{1,0:T(1,128)} %bitcast.20, s32[1,1024]{1,0:T(1,128)} %bitcast.21, s32[1,1024]{1,0:T(1,128)} %bitcast.22), custom_call_target="tpu_custom_call" | custom-call | tf_op jit(solution)/shard_map/pallas_call | solution.py:23
  3.1 0.0 copy-start
  3.1 27.7 %all_to_all.5 = s32[2176,1,128]{2,1,0:T(1,128)S(1)} all-to-all(s32[2176,1,128]{2,1,0:T(1,128)S(1)} %bitcast.13), channel_id=1, replica_groups=mesh['inline'=8,'xline'=16] {'inline','xline'}, dimensions={0} | all-to-all | bytes 2228224 | tf_op jit(solution)/shard_map/all_to_all | solution.py:483
  30.8 0.0 copy-start.1
  30.8 0.0 copy-done
  30.9 2.0 %shard_map.87 = (bf16[2,2,64,128]{3,2,1,0:T(8,128)(2,1)S(1)}, bf16[2,2,64,128]{3,2,1,0:T(8,128)(2,1)S(1)}, bf16[4,64,128]{2,1,0:T(8,128)(2,1)S(1)}, bf16[4,64,12...) custom-call(s32[2176,128]{1,0:T(8,128)S(1)} %bitcast.14, ...), custom_call_target="tpu_custom_call" | custom-call | tf_op jit(solution)/shard_map/pallas_call | solution.py:23
  32.8 2.3 %collective-permute-start = (bf16[2,2,64,128]{3,2,1,0:T(8,128)(2,1)S(1)}, bf16[2,2,64,128]{3,2,1,0:T(8,128)(2,1)S(1)}, u32[]{:S(2)}, u32[]{:S(2)}) collective-permute-start(bf16[2,2,64,128]{3,2,1,0:T(8,128)(2,1)S(1)} %get-tuple-element.24), channel_id=1, source_target_pairs={{0,1},{1,0},{2,3},{3,2},{4,5},{5,4},{6,7},{7,6},{8,9},{9,8},{10,11... | collective-permute-start | bytes 196616 | tf_op jit(solution)/shard_map/ppermute | solution.py:521
  35.1 0.0 collective-permute-start.1
  35.1 0.9 %collective-permute-start.4 = (bf16[4,64,128]{2,1,0:T(8,128)(2,1)S(1)}, bf16[4,64,128]{2,1,0:T(8,128)(2,1)S(1)}, u32[]{:S(2)}, u32[]{:S(2)}) collective-permute-start(bf16[4,64,128]{2,1,0:T(8,128)(2,1)S(1)} %get-tuple-element.28), channel_id=1, source_target_pairs={{0,16},{1,2},{2,1},{3,4},{4,3},{5,6},{6,5},{7,8},{8,7},{9,10},{10,... | collective-permute-start | bytes 196616 | tf_op jit(solution)/shard_map/ppermute | solution.py:521
  36.0 0.0 collective-permute-start.5
  36.1 0.0 copy-done.1
  36.1 0.1 reshape.37
  36.2 0.3 copy.19
  36.5 0.1 reshape.38
  36.7 0.2 copy.17
  36.9 0.8 %shard_map.89 = (bf16[4,4,64,128]{3,2,1,0:T(8,128)(2,1)S(1)}, f32[3,3,64,512]{3,2,1,0:T(8,128)S(1)}, f32[4,4,64,128]{3,2,1,0:T(8,128)S(1)}) custom-call(bf16[2,4,64,128]{3,2,1,0:T(8,128)(2,1)S(1)} %get-tuple-element.32.half, bf16[512,512]{1,0:T(8,128)(2,1)S(1)} %broadcast_multiply_fusion.words, bf16[512,512]{1,0:T(8,128)(2,1)S(1)} %bitcast.15), custom_call_target="tpu_custom_call" | custom-call | flops 600000000 | bytes 2000000 | tf_op jit(solution)/shard_map/pallas_call | solution.py:23
  37.7 3.1 %collective-permute-done.from_odd = bf16[2,2,64,128]{3,2,1,0:T(8,128)(2,1)S(1)} collective-permute-done((bf16[2,2,64,128]{3,2,1,0:T(8,128)(2,1)S(1)}, bf16[2,2,64,128]{3,2,1,0:T(8,128)(2,1)S(1)}, u32[]{:S(2)}, u32[]{:S(2)}) %collective-permute-start) | collective-permute-done | bytes 65568 | tf_op jit(solution)/shard_map/ppermute | solution.py:521
  40.8 0.0 collective-permute-done.1.from_even
  40.8 0.1 collective-permute-start.2
  40.9 0.9 %collective-permute-start.3 = (bf16[3,64,128]{2,1,0:T(8,128)(2,1)S(1)}, bf16[3,64,128]{2,1,0:T(8,128)(2,1)S(1)}, u32[]{:S(2)}, u32[]{:S(2)}) collective-permute-start(bf16[3,64,128]{2,1,0:T(8,128)(2,1)S(1)} %get-tuple-element.27.edge_even), channel_id=1, source_target_pairs={{0,1},{1,0},{2,3},{3,2},{4,5},{5,4},{6,7},{7,6},{8,9},{9,8},{10,11... | collective-permute-start | bytes 147464 | tf_op jit(solution)/shard_map/ppermute | solution.py:521
  41.8 0.0 collective-permute-done.4.side_odd
  41.8 0.0 collective-permute-done.5.side_even
  41.8 1.7 %shard_map.90 = (bf16[4,3,64,128]{3,2,1,0:T(8,128)(2,1)S(1)}, bf16[3,4,64,128]{3,2,1,0:T(8,128)(2,1)S(1)}, f32[6,64,512]{2,1,0:T(8,128)S(1)}, f32[3,5,64,128]{3,...) custom-call(bf16[4,64,128]{2,1,0:T(8,128)(2,1)S(1)} %collective-perm, ...), custom_call_target="tpu_custom_call" | custom-call | flops 1400000000 | bytes 4000000 | tf_op jit(solution)/shard_map/pallas_call | solution.py:23
  43.5 1.8 %collective-permute-done.2.corner_odd = bf16[3,64,128]{2,1,0:T(8,128)(2,1)S(1)} collective-permute-done((bf16[3,64,128]{2,1,0:T(8,128)(2,1)S(1)}, bf16[3,64,128]{2,1,0:T(8,128)(2,1)S(1)}, u32[]{:S(2)}, u32[]{:S(2)}) %collective-permute-start.2) | collective-permute-done | bytes 49184 | tf_op jit(solution)/shard_map/ppermute | solution.py:521
  45.3 0.0 collective-permute-done.3.corner_even
  45.3 2.7 %shard_map.91 = (f32[4,4,64,512]{3,2,1,0:T(8,128)}, f32[256,256]{1,0:T(8,128)}) custom-call(bf16[3,64,128]{2,1,0:T(8,128)(2,1)S(1)} %collective-permute-done.2.corner_odd, bf16[3,64,128]{2,1,0:T(8,128)(2,1)S(1)} %collective-permute-done.3.corner_even, bf16[4,64,128]{2,1,0:T(8,128)(2,1)S(1)} %collective-permute-done.4.side_odd, ...), custom_call_target="tpu_custom_call" | custom-call | tf_op jit(solution)/shard_map/pallas_call | solution.py:23
  (2 shorter events, 0.1 us)
Async XLA Ops:
  3.1 27.8 %copy-start = (f32[16,16,256]{2,1,0:T(8,128)S(1)}, f32[16,16,256]{2,1,0:T(8,128)}, u32[]{:S(2)}) copy-start(f32[16,16,256]{2,1,0:T(8,128)} %param.7) | copy-start | bytes 786436
  30.8 5.2 %copy-start.1 = (bf16[512,512]{1,0:T(8,128)(2,1)S(1)}, bf16[512,512]{1,0:T(8,128)(2,1)}, u32[]{:S(2)}) copy-start(bf16[512,512]{1,0:T(8,128)(2,1)} %param.13) | copy-start | bytes 1572868
  32.8 8.0 %collective-permute-start = (bf16[2,2,64,128]{3,2,1,0:T(8,128)(2,1)S(1)}, bf16[2,2,64,128]{3,2,1,0:T(8,128)(2,1)S(1)}, u32[]{:S(2)}, u32[]{:S(2)}) collective-permute-start(bf16[2,2,64,128]{3,2,1,0:T(8,128)(2,1)S(1)} %get-tuple-element.24), channel_id=1, source_target_pairs={{0,1},{1,0},{2,3},{3,2},{4,5},{5,4},{6,7},{7,6},{8,9},{9,8},{10,11... | collective-permute-start | bytes 196616 | tf_op jit(solution)/shard_map/ppermute | solution.py:521
  35.1 5.7 %collective-permute-start.1 = (bf16[2,2,64,128]{3,2,1,0:T(8,128)(2,1)S(1)}, bf16[2,2,64,128]{3,2,1,0:T(8,128)(2,1)S(1)}, u32[]{:S(2)}, u32[]{:S(2)}) collective-permute-start(bf16[2,2,64,128]{3,2,1,0:T(8,128)(2,1)S(1)} %get-tuple-element.25), channel_id=1, source_target_pairs={{0,16},{1,17},{2,18},{3,19},{4,20},{5,21},{6,22},{7,23},{8,24},{9,... | collective-permute-start | bytes 196616 | tf_op jit(solution)/shard_map/ppermute | solution.py:521
  35.1 6.7 %collective-permute-start.4 = (bf16[4,64,128]{2,1,0:T(8,128)(2,1)S(1)}, bf16[4,64,128]{2,1,0:T(8,128)(2,1)S(1)}, u32[]{:S(2)}, u32[]{:S(2)}) collective-permute-start(bf16[4,64,128]{2,1,0:T(8,128)(2,1)S(1)} %get-tuple-element.28), channel_id=1, source_target_pairs={{0,16},{1,2},{2,1},{3,4},{4,3},{5,6},{6,5},{7,8},{8,7},{9,10},{10,... | collective-permute-start | bytes 196616 | tf_op jit(solution)/shard_map/ppermute | solution.py:521
  36.0 5.8 %collective-permute-start.5 = (bf16[4,64,128]{2,1,0:T(8,128)(2,1)S(1)}, bf16[4,64,128]{2,1,0:T(8,128)(2,1)S(1)}, u32[]{:S(2)}, u32[]{:S(2)}) collective-permute-start(bf16[4,64,128]{2,1,0:T(8,128)(2,1)S(1)} %get-tuple-element.29), channel_id=1, source_target_pairs={{0,1},{1,0},{2,3},{3,2},{4,5},{5,4},{6,7},{7,6},{8,9},{9,8},{10,11... | collective-permute-start | bytes 196616 | tf_op jit(solution)/shard_map/ppermute | solution.py:521
  40.8 4.5 %collective-permute-start.2 = (bf16[3,64,128]{2,1,0:T(8,128)(2,1)S(1)}, bf16[3,64,128]{2,1,0:T(8,128)(2,1)S(1)}, u32[]{:S(2)}, u32[]{:S(2)}) collective-permute-start(bf16[3,64,128]{2,1,0:T(8,128)(2,1)S(1)} %get-tuple-element.26.edge_odd), channel_id=1, source_target_pairs={{0,16},{1,2},{2,1},{3,4},{4,3},{5,6},{6,5},{7,8},{8,7},{9,10},{10,... | collective-permute-start | bytes 147464 | tf_op jit(solution)/shard_map/ppermute | solution.py:521
  40.9 4.4 %collective-permute-start.3 = (bf16[3,64,128]{2,1,0:T(8,128)(2,1)S(1)}, bf16[3,64,128]{2,1,0:T(8,128)(2,1)S(1)}, u32[]{:S(2)}, u32[]{:S(2)}) collective-permute-start(bf16[3,64,128]{2,1,0:T(8,128)(2,1)S(1)} %get-tuple-element.27.edge_even), channel_id=1, source_target_pairs={{0,1},{1,0},{2,3},{3,2},{4,5},{5,4},{6,7},{7,6},{8,9},{9,8},{10,11... | collective-permute-start | bytes 147464 | tf_op jit(solution)/shard_map/ppermute | solution.py:521
